TPU v7x, 512 devices: a whole 4x8x8 slice. The times are simulated.
512 devices in a mesh: gy: 32 (over x_lo, z, core), gx: 16 (over x_hi, y).
Axes of the slice: x: 4 (x_hi: 2, x_lo: 2; x = x_hi * 2 + x_lo), y: 8, z: 8, core: 2. Of those that a mesh axis runs over, the one named last changes fastest.
Arguments:
- features: bfloat16 [2048, 256, 128], P('gy', 'gx'), may hold values from -40 to 40
- attention_gain: float32 [2, 128], replicated, may hold values from 0.25 to 1.75
- triple_weight: bfloat16 [2, 128, 384], replicated, may hold values from -0.5 to 0.5
- output_weight: bfloat16 [2, 128, 128], replicated, may hold values from -0.5 to 0.5
- position_bias: float32 [2, 4, 225], replicated, may hold values from -2 to 262
- hidden_gain: float32 [2, 128], replicated, may hold values from 0.25 to 1.75
- expand_weight: bfloat16 [2, 128, 512], replicated, may hold values from -0.5 to 0.5
- shrink_weight: bfloat16 [2, 512, 128], replicated, may hold values from -0.25 to 0.25
Outputs:
- result: float32 [2048, 256, 128], P('gy', 'gx')
All inputs are finite; a program needn't handle non-finite values.
Results may differ from a plain program's by a relative error of at most 0.0033.
Values may be sent and summed in bfloat16 or wider, within the bound.
No kernel may reach another device: no remote copies, remote signals or barrier semaphores. Data moves between devices by JAX's collectives and lax.ppermute only.
A program may use at most 64 MiB of HBM per device.

v0:
```python
import jax
import jax.numpy as jnp
from jax import lax
from jax.sharding import PartitionSpec as P

C = 128
HEADS = 4
WIN = 8
HD = 32
SHIFT = 4


EPSILON = 1e-05


def from_behind(x, axis, by):
    length = lax.axis_size(axis)
    return lax.ppermute(x, axis, [(i, (i + by) % length) for i in range(length)])


def layer_norm(values, gain_vector):
    center = values - jnp.mean(values, axis=-1, keepdims=True)
    spread = jnp.mean(center * center, axis=-1, keepdims=True)
    return (center * lax.rsqrt(spread + EPSILON) * gain_vector).astype(jnp.bfloat16)


def bias_tables(position_bias):
    extent = 2 * WIN - 1
    places = jnp.arange(WIN * WIN, dtype=jnp.int32)
    along_y = places // WIN
    along_x = places % WIN
    offset = (
        (along_y[:, None] - along_y[None, :] + WIN - 1) * extent
        + along_x[:, None]
        - along_x[None, :]
        + WIN
        - 1
    )
    selector = (
        offset[:, :, None] == jnp.arange(extent * extent, dtype=jnp.int32)[None, None, :]
    ).astype(jnp.float32)
    return jnp.einsum("bhe,qke->bhqk", position_bias, selector, precision=lax.Precision.HIGHEST)


def region_labels(first_row, first_col, height, breadth, total_rows, total_cols):
    frame_rows = jnp.mod(first_row + jnp.arange(height, dtype=jnp.int32), total_rows)
    frame_cols = jnp.mod(first_col + jnp.arange(breadth, dtype=jnp.int32), total_cols)
    row_label = (frame_rows >= total_rows - WIN).astype(jnp.int32) + (
        frame_rows >= total_rows - SHIFT
    ).astype(jnp.int32)
    col_label = (frame_cols >= total_cols - WIN).astype(jnp.int32) + (
        frame_cols >= total_cols - SHIFT
    ).astype(jnp.int32)
    return row_label[:, None] * 3 + col_label[None, :]


def project(normed, weight):
    output = jnp.dot(normed.reshape(-1, C), weight, preferred_element_type=jnp.float32).astype(
        jnp.bfloat16
    )
    return output.reshape(normed.shape[0], normed.shape[1], -1)


def attend(triple, labels, bias_block, out_weight):
    height, breadth = (triple.shape[0], triple.shape[1])
    bands = height // WIN
    windows = breadth // WIN
    count = bands * windows
    pieces = triple.reshape(bands, WIN, windows, WIN, 3, HEADS, HD).transpose(4, 0, 2, 5, 1, 3, 6)
    pieces = pieces.reshape(3, count, HEADS, WIN * WIN, HD)
    scores = (
        jnp.einsum("whqd,whkd->whqk", pieces[0], pieces[1], preferred_element_type=jnp.float32)
        * HD ** (-0.5)
        + bias_block[None]
    )
    labels_win = (
        labels.reshape(bands, WIN, windows, WIN).transpose(0, 2, 1, 3).reshape(count, WIN * WIN)
    )
    scores = scores + jnp.where(
        labels_win[:, None, :, None] != labels_win[:, None, None, :], -100.0, 0.0
    ).astype(jnp.float32)
    row_max = jnp.max(scores, axis=-1, keepdims=True)
    powers = jnp.exp(scores - row_max)
    probabilities = (powers / jnp.sum(powers, axis=-1, keepdims=True)).astype(jnp.bfloat16)
    context = jnp.einsum(
        "whqk,whkd->whqd", probabilities, pieces[2], preferred_element_type=jnp.float32
    ).astype(jnp.bfloat16)
    context = (
        context.reshape(bands, windows, HEADS, WIN, WIN, HD)
        .transpose(0, 3, 1, 4, 2, 5)
        .reshape(height * breadth, C)
    )
    branch = jnp.dot(context, out_weight, preferred_element_type=jnp.float32).astype(jnp.bfloat16)
    return branch.reshape(height, breadth, C)


def feed_forward(middle, gain_vector, expand, shrink):
    height, breadth = (middle.shape[0], middle.shape[1])
    normed_mid = layer_norm(middle, gain_vector)
    hidden = jax.nn.gelu(
        jnp.dot(normed_mid.reshape(-1, C), expand, preferred_element_type=jnp.float32),
        approximate=False,
    ).astype(jnp.bfloat16)
    return middle + jnp.dot(hidden, shrink, preferred_element_type=jnp.float32).reshape(
        height, breadth, C
    )


def on_device(
    features,
    attention_gain,
    triple_weight,
    output_weight,
    position_bias,
    hidden_gain,
    expand_weight,
    shrink_weight,
):
    height, breadth = (features.shape[0], features.shape[1])
    tables = bias_tables(position_bias)
    start_values = features.astype(jnp.float32)
    no_labels = jnp.zeros((height, breadth), jnp.int32)
    normed = layer_norm(start_values, attention_gain[0])
    branch = attend(project(normed, triple_weight[0]), no_labels, tables[0], output_weight[0])
    first_out = feed_forward(
        start_values + branch.astype(jnp.float32),
        hidden_gain[0],
        expand_weight[0],
        shrink_weight[0],
    )
    normed = layer_norm(first_out, attention_gain[1])
    payload = project(normed, triple_weight[1])
    total_rows = height * lax.axis_size("gy")
    total_cols = breadth * lax.axis_size("gx")
    row_anchor = lax.axis_index("gy") * height
    col_anchor = lax.axis_index("gx") * breadth
    arrived = from_behind(payload[:SHIFT], "gy", -1)
    source = jnp.concatenate([payload[SHIFT:], arrived], axis=0)
    roll_arrived = from_behind(source[:, :SHIFT], "gx", -1)
    shifted = jnp.concatenate([source[:, SHIFT:], roll_arrived], axis=1)
    labels = region_labels(row_anchor, col_anchor, height, breadth, total_rows, total_cols)
    framed = attend(shifted, labels, tables[1], output_weight[1])
    arrived = from_behind(framed[:, -SHIFT:], "gx", 1)
    source = jnp.concatenate([arrived, framed[:, :-SHIFT]], axis=1)
    arrived = from_behind(source[-SHIFT:], "gy", 1)
    branch = jnp.concatenate([arrived, source[:-SHIFT]], axis=0)
    return feed_forward(
        first_out + branch.astype(jnp.float32), hidden_gain[1], expand_weight[1], shrink_weight[1]
    )


def solution(mesh):
    return jax.shard_map(
        on_device,
        mesh=mesh,
        in_specs=(P("gy", "gx", None), P(), P(), P(), P(), P(), P(), P()),
        out_specs=P("gy", "gx", None),
        check_vma=False,
    )
```

profile of v0, /device:TPU:2, one launch (start us, length us, event | category | flops | bytes accessed | tf_op | source)
XLA Modules:
  0.0 98.7 jit_solution(10856749982275089914)
XLA Ops:
  0.0 0.8 slice_bitcast_fusion.4
  0.8 0.8 slice_bitcast_fusion.3
  1.5 1.2 %convert_reduce_fusion = f32[64,16]{1,0:T(8,128)S(1)} fusion(bf16[64,16,128]{2,1,0:T(8,128)(2,1)} %param.8), kind=kLoop, calls=%fused_computation.71 | loop fusion | flops 261120 | bytes 266240 | tf_op jit(solution)/shard_map/reduce_sum | solution.py:22
  2.7 1.3 %fusion.38 = f32[64,16]{1,0:T(8,128)S(1)} fusion(bf16[64,16,128]{2,1,0:T(8,128)(2,1)} %param.8, f32[64,16]{1,0:T(8,128)S(1)} %broadcast_multiply_fusion.3), kind=kLoop, calls=%fused_computation.74 | loop fusion | flops 523264 | bytes 270336 | tf_op jit(solution)/shard_map/reduce_sum | solution.py:23
  4.0 1.3 %fusion.40 = bf16[64,16,128]{2,1,0:T(8,128)(2,1)S(1)} fusion(bf16[64,16,128]{2,1,0:T(8,128)(2,1)} %param.8, f32[128]{0:T(128)S(1)} %get-tuple-element.14, f32[64,16]{1,0:T(8,128)S(1)} %add_rsqrt_fusion.3, f32[64,16]{1,0:T(8,128)S(1)} %broadcast_multiply_fusion.3), kind=kLoop, calls=%fused_computation.76 | loop fusion | flops 655360 | bytes 532992 | tf_op jit(solution)/shard_map/convert_element_type | solution.py:24
  5.3 1.2 %convolution_convert_fusion.1 = bf16[1024,384]{1,0:T(8,128)(2,1)S(1)} fusion(bf16[1024,128]{1,0:T(8,128)(2,1)S(1)} %bitcast.118, bf16[2,128,384]{2,1,0:T(8,128)(2,1)} %param.10), kind=kOutput, calls=%fused_computation.54 | convolution fusion | flops 101056512 | bytes 1146880 | tf_op jit(solution)/shard_map/dot_general | solution.py:58
  6.6 3.0 %reshape_reshape.3 = bf16[8,8,2,8,3,4,32]{6,5,4,3,2,1,0:T(4,128)(2,1)} reshape(bf16[1024,384]{1,0:T(8,128)(2,1)S(1)} %convolution_convert_fusion.1) | data formatting | bytes 1572864 | tf_op jit(solution)/shard_map/reshape;reshape | solution.py:69
  9.6 2.8 %copy.60 = bf16[8,8,2,8,3,4,32]{6,3,1,5,2,0,4:T(8,128)(2,1)S(1)} copy(bf16[8,8,2,8,3,4,32]{6,5,4,3,2,1,0:T(4,128)(2,1)} %reshape_reshape.3) | data formatting | bytes 1572864 | tf_op jit(solution)/shard_map/reshape;reshape | solution.py:69
  12.4 1.9 %fusion.71 = (bf16[1,8,2,4,8,8,32]{6,5,4,3,2,1,0:T(8,128)(2,1)S(1)}, bf16[1,8,2,4,8,8,32]{6,5,4,3,2,1,0:T(8,128)(2,1)S(1)}, bf16[1,8,2,4,8,8,32]{6,5,4,3,2,1,0:T(8,128)(2,1)}) fusion(bf16[3,8,2,4,8,8,32]{6,5,4,3,2,1,0:T(8,128)(2,1)S(1)} %bitcast.97), kind=kLoop, calls=%fused_computation.146 | loop fusion | bytes 1572864 | tf_op jit(solution)/shard_map/slice | solution.py:72
  14.3 0.1 subtract_add_fusion
  14.4 2.8 %fusion.28 = f32[2,4,64,64]{3,1,0,2:T(4,128)S(1)} fusion(s32[64,64]{1,0:T(8,128)S(1)} %subtract_add_fusion, f32[2,4,225]{2,1,0:T(4,128)S(1)} %copy-done), kind=kOutput, calls=%fused_computation.61 | convolution fusion | flops 89395200 | bytes 154656 | tf_op jit(solution)/shard_map/bhe,qke->bhqk/dot_general | solution.py:42
  17.2 0.1 slice_bitcast_fusion
  17.3 0.1 copy.35
  17.4 3.5 %fusion.72 = (f32[16,4,64]{2,1,0:T(4,128)S(1)}, f32[16,4,64,64]{2,3,1,0:T(8,128)}) fusion(f32[4,64,64]{1,2,0:T(8,128)S(1)} %copy.35, bf16[16,4,64,32]{3,2,1,0:T(8,128)(2,1)} %bitcast.121, bf16[16,4,64,32]{3,2,1,0:T(8,128)(2,1)S(1)} %bitcast.120), kind=kOutput, calls=%fused_computation.147 | convolution fusion | flops 17825856 | bytes 1654784 | tf_op jit(solution)/shard_map/sub | solution.py:83
  20.9 2.1 %convolution_convert_fusion.3 = bf16[16,4,64,32]{2,3,1,0:T(8,128)(2,1)S(1)} fusion(bf16[16,4,64,32]{3,2,1,0:T(8,128)(2,1)S(1)} %bitcast.119, f32[16,4,64,64]{2,3,1,0:T(8,128)} %get-tuple-element.18, f32[16,4,64]{2,1,0:T(4,128)S(1)} %get-tuple-element.17), kind=kOutput, calls=%fused_computation.56 | convolution fusion | flops 17432576 | bytes 1589248 | tf_op jit(solution)/shard_map/whqk,whkd->whqd/dot_general | solution.py:85
  22.9 0.5 copy.38
  23.4 0.0 copy-start.1
  23.4 1.4 %copy.39 = bf16[8,8,2,8,4,32]{5,4,3,2,1,0:T(4,128)(2,1)S(1)} copy(bf16[8,8,2,8,4,32]{5,3,1,4,2,0:T(8,128)(2,1)S(1)} %bitcast.110) | data formatting | bytes 524288 | tf_op jit(solution)/shard_map/transpose | solution.py:90
  24.8 0.0 copy-start.7
  24.8 0.5 reshape.280
  25.3 0.2 convolution_convert_fusion.5
  25.6 0.2 fusion.41
  25.8 0.4 multiply_reduce_fusion.2
  26.2 0.3 multiply_convert_fusion.2
  26.6 0.0 copy-start.2
  26.6 5.0 %fusion.7 = bf16[1024,512]{1,0:T(8,128)(2,1)S(1)} fusion(bf16[1024,128]{1,0:T(8,128)(2,1)S(1)} %bitcast.122, bf16[2,128,512]{2,1,0:T(8,128)(2,1)S(1)} %copy-done.7), kind=kOutput, calls=%fused_computation.10 | convolution fusion | flops 168296448 | bytes 1441792 | tf_op jit(solution)/shard_map/dot_general | solution.py:101
  31.5 0.0 copy-start.3
  31.5 0.5 fusion.73
  32.1 0.4 multiply_reduce_fusion.1
  32.5 0.3 multiply_convert_fusion.1
  32.8 0.3 convolution_convert_fusion
  33.2 10.4 %collective-permute-start = (bf16[4,16,384]{2,1,0:T(8,128)(2,1)S(1)}, bf16[4,16,384]{2,1,0:T(8,128)(2,1)S(1)}, u32[]{:S(2)}, u32[]{:S(2)}) collective-permute-start(bf16[4,16,384]{2,1,0:T(8,128)(2,1)S(1)} %bitcast.124), channel_id=1, source_target_pairs={{0,496},{16,0},{32,16},{48,32},{64,48},{80,64},{96,80},{112,96},{1... | collective-permute-start | bytes 147464 | tf_op jit(solution)/shard_map/ppermute | solution.py:18
  43.6 0.1 broadcast_add_fusion
  43.7 0.1 slice.130
  43.7 0.1 add.227
  43.8 1.4 %collective-permute-done = bf16[4,16,384]{2,1,0:T(8,128)(2,1)S(1)} collective-permute-done((bf16[4,16,384]{2,1,0:T(8,128)(2,1)S(1)}, bf16[4,16,384]{2,1,0:T(8,128)(2,1)S(1)}, u32[]{:S(2)}, u32[]{:S(2)}) %collective-permute-start) | collective-permute-done | bytes 49184 | tf_op jit(solution)/shard_map/ppermute | solution.py:18
  45.3 0.1 pad_maximum_fusion.2
  45.3 7.4 %collective-permute-start.1 = (bf16[64,4,384]{2,1,0:T(4,128)(2,1)S(1)}, bf16[64,4,384]{2,1,0:T(4,128)(2,1)S(1)}, u32[]{:S(2)}, u32[]{:S(2)}) collective-permute-start(bf16[64,4,384]{2,1,0:T(4,128)(2,1)S(1)} %pad_maximum_fusion.2), channel_id=1, source_target_pairs={{0,15},{1,0},{2,1},{3,2},{4,3},{5,4},{6,5},{7,6},{8,7},{9,8},{10,9... | collective-permute-start | bytes 589832 | tf_op jit(solution)/shard_map/ppermute | solution.py:18
  52.7 0.2 compare_select_fusion
  53.0 0.8 copy.44
  53.7 0.2 slice_maximum_fusion
  54.0 1.8 %collective-permute-done.1 = bf16[64,4,384]{2,1,0:T(4,128)(2,1)S(1)} collective-permute-done((bf16[64,4,384]{2,1,0:T(4,128)(2,1)S(1)}, bf16[64,4,384]{2,1,0:T(4,128)(2,1)S(1)}, u32[]{:S(2)}, u32[]{:S(2)}) %collective-permute-start.1) | collective-permute-done | bytes 196640 | tf_op jit(solution)/shard_map/ppermute | solution.py:18
  55.7 0.2 pad_maximum_fusion
  56.0 3.0 %reshape.283 = bf16[8,8,2,8,3,4,32]{6,5,4,3,2,1,0:T(4,128)(2,1)} reshape(bf16[64,16,384]{2,1,0:T(8,128)(2,1)S(1)} %pad_maximum_fusion) | data formatting | bytes 1572864 | tf_op jit(solution)/shard_map/reshape | solution.py:69
  59.0 4.2 %fusion.70 = (bf16[1,8,2,4,8,8,32]{6,3,0,5,2,4,1:T(4,128)(2,1)S(1)}, bf16[1,8,2,4,8,8,32]{6,3,0,5,2,4,1:T(4,128)(2,1)S(1)}, bf16[1,8,2,4,8,8,32]{6,3,0,5,2,4,1:T(4,128)(2,1)S(1)}) fusion(bf16[3,8,2,4,8,8,32]{6,3,0,5,2,4,1:T(4,128)(2,1)} %bitcast.98), kind=kLoop, calls=%fused_computation.145 | loop fusion | bytes 1572864 | tf_op jit(solution)/shard_map/slice | solution.py:72
  63.2 0.3 copy.45
  63.5 0.0 copy-start.4
  63.5 0.3 copy.40
  63.8 1.3 %copy.41 = bf16[1,8,2,4,8,8,32]{6,5,4,3,2,1,0:T(8,128)(2,1)} copy(bf16[1,8,2,4,8,8,32]{6,3,0,5,2,4,1:T(4,128)(2,1)S(1)} %get-tuple-element.5) | data formatting | bytes 524288 | tf_op jit(solution)/shard_map/slice | solution.py:72
  65.0 4.2 %fusion.74 = (f32[16,4,64]{2,1,0:T(4,128)}, f32[16,4,64,64]{2,3,1,0:T(8,128)}) fusion(f32[16,64,64]{1,2,0:T(8,128)S(1)} %compare_select_fusion, f32[4,64,64]{1,2,0:T(8,128)S(1)} %copy-done.4, bf16[16,4,64,32]{3,2,1,0:T(8,128)(2,1)S(1)} %bitcast.113, bf16[16,4,64,32]{3,2,1,0:T(8,128)(2,1)} %bitcast.114), kind=kOutput, calls=%fused_computation.149 | convolution fusion | flops 18088000 | bytes 1916928 | tf_op jit(solution)/shard_map/sub | solution.py:83
  69.3 2.1 %convolution_convert_fusion.2 = bf16[16,4,64,32]{2,3,1,0:T(8,128)(2,1)S(1)} fusion(bf16[16,4,64,32]{3,2,1,0:T(8,128)(2,1)S(1)} %bitcast.112, f32[16,4,64,64]{2,3,1,0:T(8,128)} %get-tuple-element.22, f32[16,4,64]{2,1,0:T(4,128)} %get-tuple-element.21), kind=kOutput, calls=%fused_computation.55 | convolution fusion | flops 17432576 | bytes 1589248 | tf_op jit(solution)/shard_map/whqk,whkd->whqd/dot_general | solution.py:85
  71.4 0.5 copy.48
  71.8 1.4 %copy.49 = bf16[8,8,2,8,4,32]{5,4,3,2,1,0:T(4,128)(2,1)S(1)} copy(bf16[8,8,2,8,4,32]{5,3,1,4,2,0:T(8,128)(2,1)S(1)} %bitcast.111) | data formatting | bytes 524288 | tf_op jit(solution)/shard_map/transpose | solution.py:90
  73.2 0.5 reshape.285
  73.7 0.2 convolution_convert_fusion.4
  74.0 1.9 %collective-permute-start.2 = (bf16[64,4,128]{2,1,0:T(4,128)(2,1)S(1)}, bf16[64,4,128]{2,1,0:T(4,128)(2,1)S(1)}, u32[]{:S(2)}, u32[]{:S(2)}) collective-permute-start(bf16[64,4,128]{2,1,0:T(4,128)(2,1)S(1)} %slice.138), channel_id=1, source_target_pairs={{0,1},{1,2},{2,3},{3,4},{4,5},{5,6},{6,7},{7,8},{8,9},{9,10},{10,1... | collective-permute-start | bytes 196616 | tf_op jit(solution)/shard_map/ppermute | solution.py:18
  75.9 8.3 %collective-permute-done.2 = bf16[64,4,128]{2,1,0:T(4,128)(2,1)S(1)} collective-permute-done((bf16[64,4,128]{2,1,0:T(4,128)(2,1)S(1)}, bf16[64,4,128]{2,1,0:T(4,128)(2,1)S(1)}, u32[]{:S(2)}, u32[]{:S(2)}) %collective-permute-start.2) | collective-permute-done | bytes 65568 | tf_op jit(solution)/shard_map/ppermute | solution.py:18
  84.3 1.9 %collective-permute-start.3 = (bf16[4,16,128]{2,1,0:T(8,128)(2,1)S(1)}, bf16[4,16,128]{2,1,0:T(8,128)(2,1)S(1)}, u32[]{:S(2)}, u32[]{:S(2)}) collective-permute-start(bf16[4,16,128]{2,1,0:T(8,128)(2,1)S(1)} %pad_maximum_fusion.3), channel_id=1, source_target_pairs={{0,16},{16,32},{32,48},{48,64},{64,80},{80,96},{96,112},{112,128},... | collective-permute-start | bytes 49160 | tf_op jit(solution)/shard_map/ppermute | solution.py:18
  86.2 5.2 %collective-permute-done.3 = bf16[4,16,128]{2,1,0:T(8,128)(2,1)S(1)} collective-permute-done((bf16[4,16,128]{2,1,0:T(8,128)(2,1)S(1)}, bf16[4,16,128]{2,1,0:T(8,128)(2,1)S(1)}, u32[]{:S(2)}, u32[]{:S(2)}) %collective-permute-start.3) | collective-permute-done | bytes 16416 | tf_op jit(solution)/shard_map/ppermute | solution.py:18
  91.4 0.2 fusion.69
  91.7 0.4 multiply_reduce_fusion
  92.1 0.4 multiply_convert_fusion
  92.5 5.0 %fusion.10 = bf16[1024,512]{1,0:T(8,128)(2,1)S(1)} fusion(bf16[1024,128]{1,0:T(8,128)(2,1)S(1)} %bitcast.123, bf16[2,128,512]{2,1,0:T(8,128)(2,1)S(1)} %copy-done.8), kind=kOutput, calls=%fused_computation.13 | convolution fusion | flops 168296448 | bytes 1441792 | tf_op jit(solution)/shard_map/dot_general | solution.py:101
  97.4 1.2 %convolution_add_fusion = f32[64,16,128]{2,1,0:T(8,128)} fusion(bf16[64,16,512]{2,1,0:T(8,128)(2,1)S(1)} %bitcast.115, bf16[2,512,128]{2,1,0:T(8,128)(2,1)S(1)} %copy-done.2, f32[64,16,128]{2,1,0:T(8,128)S(1)} %get-tuple-element.20, bf16[64,12,128]{2,1,0:T(8,128)(2,1)S(1)} %bitcast.104, bf16[64,4,128]{2,1,0:T(4,128)(2,1)S(1)} %collective-permute-done.2, ...), kind=kOutput, calls=%fused_computation.57 | convolution fusion | flops 135266304 | bytes 2572288 | tf_op jit(solution)/shard_map/dot_general | solution.py:104
  (27 shorter events, 0.2 us)
Async XLA Ops:
  0.0 14.4 %copy-start = (f32[2,4,225]{2,1,0:T(4,128)S(1)}, f32[2,4,225]{2,1,0:T(4,128)}, u32[]{:S(2)}) copy-start(f32[2,4,225]{2,1,0:T(4,128)} %param.12) | copy-start | bytes 21604
  23.4 1.9 %copy-start.5 = (bf16[2,128,128]{2,1,0:T(8,128)(2,1)S(1)}, bf16[2,128,128]{2,1,0:T(8,128)(2,1)}, u32[]{:S(2)}) copy-start(bf16[2,128,128]{2,1,0:T(8,128)(2,1)} %param.11) | copy-start | bytes 196612
  23.4 2.1 %copy-start.1 = (bf16[64,16,128]{2,1,0:T(8,128)(2,1)S(1)}, bf16[64,16,128]{2,1,0:T(8,128)(2,1)}, u32[]{:S(2)}) copy-start(bf16[64,16,128]{2,1,0:T(8,128)(2,1)} %param.8) | copy-start | bytes 786436
  24.8 1.7 %copy-start.7 = (bf16[2,128,512]{2,1,0:T(8,128)(2,1)S(1)}, bf16[2,128,512]{2,1,0:T(8,128)(2,1)}, u32[]{:S(2)}) copy-start(bf16[2,128,512]{2,1,0:T(8,128)(2,1)} %param.14) | copy-start | bytes 786436
  26.6 5.0 %copy-start.2 = (bf16[2,512,128]{2,1,0:T(8,128)(2,1)S(1)}, bf16[2,512,128]{2,1,0:T(8,128)(2,1)}, u32[]{:S(2)}) copy-start(bf16[2,512,128]{2,1,0:T(8,128)(2,1)} %param.15) | copy-start | bytes 786436
  31.5 1.3 %copy-start.3 = (bf16[2,128,384]{2,1,0:T(8,128)(2,1)S(1)}, bf16[2,128,384]{2,1,0:T(8,128)(2,1)}, u32[]{:S(2)}) copy-start(bf16[2,128,384]{2,1,0:T(8,128)(2,1)} %param.10) | copy-start | bytes 589828
  33.2 12.1 %collective-permute-start = (bf16[4,16,384]{2,1,0:T(8,128)(2,1)S(1)}, bf16[4,16,384]{2,1,0:T(8,128)(2,1)S(1)}, u32[]{:S(2)}, u32[]{:S(2)}) collective-permute-start(bf16[4,16,384]{2,1,0:T(8,128)(2,1)S(1)} %bitcast.124), channel_id=1, source_target_pairs={{0,496},{16,0},{32,16},{48,32},{64,48},{80,64},{96,80},{112,96},{1... | collective-permute-start | bytes 147464 | tf_op jit(solution)/shard_map/ppermute | solution.py:18
  45.3 10.4 %collective-permute-start.1 = (bf16[64,4,384]{2,1,0:T(4,128)(2,1)S(1)}, bf16[64,4,384]{2,1,0:T(4,128)(2,1)S(1)}, u32[]{:S(2)}, u32[]{:S(2)}) collective-permute-start(bf16[64,4,384]{2,1,0:T(4,128)(2,1)S(1)} %pad_maximum_fusion.2), channel_id=1, source_target_pairs={{0,15},{1,0},{2,1},{3,2},{4,3},{5,4},{6,5},{7,6},{8,7},{9,8},{10,9... | collective-permute-start | bytes 589832 | tf_op jit(solution)/shard_map/ppermute | solution.py:18
  63.5 1.6 %copy-start.4 = (f32[4,64,64]{1,2,0:T(8,128)S(1)}, f32[4,64,64]{1,2,0:T(8,128)}, u32[]{:S(2)}) copy-start(f32[4,64,64]{1,2,0:T(8,128)} %copy.44) | copy-start | bytes 196612
  71.8 1.9 %copy-start.6 = (bf16[2,128,128]{2,1,0:T(8,128)(2,1)S(1)}, bf16[2,128,128]{2,1,0:T(8,128)(2,1)}, u32[]{:S(2)}) copy-start(bf16[2,128,128]{2,1,0:T(8,128)(2,1)} %param.11) | copy-start | bytes 196612
  73.7 18.7 %copy-start.8 = (bf16[2,128,512]{2,1,0:T(8,128)(2,1)S(1)}, bf16[2,128,512]{2,1,0:T(8,128)(2,1)}, u32[]{:S(2)}) copy-start(bf16[2,128,512]{2,1,0:T(8,128)(2,1)} %param.14) | copy-start | bytes 786436
  74.0 10.2 %collective-permute-start.2 = (bf16[64,4,128]{2,1,0:T(4,128)(2,1)S(1)}, bf16[64,4,128]{2,1,0:T(4,128)(2,1)S(1)}, u32[]{:S(2)}, u32[]{:S(2)}) collective-permute-start(bf16[64,4,128]{2,1,0:T(4,128)(2,1)S(1)} %slice.138), channel_id=1, source_target_pairs={{0,1},{1,2},{2,3},{3,4},{4,5},{5,6},{6,7},{7,8},{8,9},{9,10},{10,1... | collective-permute-start | bytes 196616 | tf_op jit(solution)/shard_map/ppermute | solution.py:18
  84.3 7.2 %collective-permute-start.3 = (bf16[4,16,128]{2,1,0:T(8,128)(2,1)S(1)}, bf16[4,16,128]{2,1,0:T(8,128)(2,1)S(1)}, u32[]{:S(2)}, u32[]{:S(2)}) collective-permute-start(bf16[4,16,128]{2,1,0:T(8,128)(2,1)S(1)} %pad_maximum_fusion.3), channel_id=1, source_target_pairs={{0,16},{16,32},{32,48},{48,64},{64,80},{80,96},{96,112},{112,128},... | collective-permute-start | bytes 49160 | tf_op jit(solution)/shard_map/ppermute | solution.py:18
where the time goes:
time: 99.2 us; the launch traced here: 98.7 us
  matrix products  28.3 us (29%)
  local copies, waits for them, and re-layouts  24.1 us (24%)
  starting transfers between devices  21.6 us (22%)
  waiting for transfers between devices  16.8 us (17%)
  other arithmetic  7.38 us (7%)
    ppermute x4, starting transfers between devices, from_behind(): lax.ppermute(x, axis, [(i, (i + by) % length) for i in range(length)])  21.6 us
    ppermute x4, waiting for transfers between devices, from_behind(): lax.ppermute(x, axis, [(i, (i + by) % length) for i in range(length)])  16.8 us
    dot_general x2, matrix products, feed_forward(): jnp.dot(normed_mid.reshape(-1, C), expand, preferred_element_type=jnp.flo...  9.91 us
    sub x2, matrix products, attend(): powers = jnp.exp(scores - row_max)  7.7 us
    slice x3, local copies, waits for them, and re-layouts, attend(): pieces[1]  7.45 us
    another operation x2, local copies, waits for them, and re-layouts, attend(): triple.reshape(bands, WIN, windows, WIN, 3, HEADS, HD)  5.77 us
    dot_general x2, matrix products, attend(): jnp.einsum('whqk,whkd->whqd', probabilities, pieces[2], preferred_element...  4.11 us
    reshape x1, local copies, waits for them, and re-layouts, attend(): triple.reshape(bands, WIN, windows, WIN, 3, HEADS, HD)  3.02 us
  transfers between devices with their start and end apart: 4, of which 4 were waited for; matrix products, arithmetic and copies ran while one was open for 1% of the time, Pallas kernels for 0%

commit v1 on v0

v1 whole, which is shorter than its diff:
```python
import math

import jax
import jax.numpy as jnp
from jax import lax
from jax.experimental import pallas as pl
from jax.experimental.pallas import tpu as pltpu
from jax.sharding import PartitionSpec as P

C = 128
HEADS = 4
HID = 512
WIN = 8
HD = 32
SHIFT = 4
EPSILON = 1e-05
LOG2E = math.log2(math.e)
SCALE = HD ** (-0.5) * LOG2E
F32 = jnp.float32
BF16 = jnp.bfloat16
NT = (((1,), (1,)), ((), ()))
TN = (((0,), (0,)), ((), ()))


def from_behind(x, axis, by):
    length = lax.axis_size(axis)
    return lax.ppermute(x, axis, [(i, (i + by) % length) for i in range(length)])


def iota(shape, dim):
    return lax.broadcasted_iota(jnp.int32, shape, dim)


def layer_norm(x, gain):
    center = x - jnp.mean(x, axis=-1, keepdims=True)
    spread = jnp.mean(center * center, axis=-1, keepdims=True)
    return center * lax.rsqrt(spread + EPSILON) * gain


def gelu(x):
    half = 0.5 * x
    return half + half * lax.erf(x * (0.5**0.5))


def fill_bias(pb_ref, block, store):
    sub = iota((8, 128), 0)
    lane = iota((8, 128), 1)
    place = lax.min((lane >> 3) * 15 + 7 + (lane & 7) - sub, 224)
    for head in range(HEADS):
        low = jnp.broadcast_to(pb_ref[block, head : head + 1, 0:128], (8, 128))
        high = jnp.broadcast_to(pb_ref[block, head : head + 1, 97:225], (8, 128))
        strip = jnp.where(
            place < 128,
            jnp.take_along_axis(low, lax.min(place, 127), axis=1),
            jnp.take_along_axis(high, lax.max(place - 97, 0), axis=1),
        )
        strip = strip * LOG2E
        for yj in range(8):
            turn = (128 - (7 - yj) * 8) % 128
            first = pltpu.roll(strip, turn, 1) if turn else strip
            second = pltpu.roll(strip, (turn + 64) % 128, 1)
            store(head, yj, jnp.where(lane < 64, first, second))


def lane_masks(rows):
    lane = iota((rows, 128), 1)
    left = jnp.where(lane < 64, 1.0, 0.0).astype(BF16)
    right = jnp.where(lane >= 64, 1.0, 0.0).astype(BF16)
    return left, right


def fill_weights(w_ref, block, wqv, wk):
    wqv[0:128, :] = jnp.transpose(w_ref[block, :, 0:128].astype(F32)).astype(BF16)
    wqv[128:256, :] = jnp.transpose(w_ref[block, :, 256:384].astype(F32)).astype(BF16)
    keys = w_ref[block, :, 128:256].astype(F32)
    turned = pltpu.roll(keys, 64, 1)
    lane = iota((128, 128), 1)
    zero = jnp.zeros((128, 128), F32)
    wk[0:128, 0:128] = jnp.where(lane < 64, keys, zero).astype(BF16)
    wk[0:128, 128:256] = jnp.where(lane < 64, turned, zero).astype(BF16)
    wk[128:256, 0:128] = jnp.where(lane >= 64, turned, zero).astype(BF16)
    wk[128:256, 128:256] = jnp.where(lane >= 64, keys, zero).astype(BF16)


def softmax_columns(s):
    p = jnp.exp2(s - jnp.max(s, axis=0, keepdims=True))
    return (p * (1.0 / jnp.sum(p, axis=0, keepdims=True))).astype(BF16)


def dot(a, b, dims=None):
    if dims is None:
        return jnp.dot(a, b, preferred_element_type=F32)
    return lax.dot_general(a, b, dims, preferred_element_type=F32)


def attention(query_tokens, key_tokens, masks, wqv, wk, bias_of):
    windows = len(key_tokens)
    if windows == 2:
        vt = dot(wqv[128:256, :], jnp.concatenate(key_tokens, axis=0), NT).astype(BF16)
        keys = dot(jnp.concatenate(key_tokens, axis=1), wk[...]).astype(BF16)
        keys = [keys[:, 0:128], keys[:, 128:256]]
        values = vt
    else:
        vt = dot(wqv[128:256, :], jnp.concatenate(key_tokens[0:2], axis=0), NT).astype(BF16)
        third = dot(
            wqv[128:256, :], jnp.concatenate([key_tokens[2], key_tokens[2]], axis=0), NT
        ).astype(BF16)
        values = jnp.concatenate([vt, third], axis=1)
        keys = dot(jnp.concatenate(key_tokens[0:2], axis=1), wk[...]).astype(BF16)
        last = dot(key_tokens[2], wk[0:128, :]).astype(BF16)
        keys = [
            jnp.concatenate([keys[:, 0:128], last[:, 0:128]], axis=1),
            jnp.concatenate([keys[:, 128:256], last[:, 128:256]], axis=1),
        ]
    qt = dot(wqv[0:128, :], query_tokens, NT).astype(BF16)
    zero = jnp.zeros((32, 128), BF16)
    out = []
    for pair in range(2):
        r = 64 * pair
        rows = []
        for mask in masks:
            rows.append(jnp.concatenate([qt[r : r + 32] * mask[0:32], zero], axis=1))
            rows.append(jnp.concatenate([zero, qt[r + 32 : r + 64] * mask[0:32]], axis=1))
        if windows == 3:
            rows.append(jnp.zeros((64, 256), BF16))
        s = dot(keys[pair], jnp.concatenate(rows, axis=0))
        p = softmax_columns(s * SCALE + bias_of(pair))
        seen = [
            jnp.concatenate([p[:, 0:128] * mask, p[:, 128:256] * mask], axis=1) for mask in masks
        ]
        if windows == 3:
            seen.append(jnp.zeros((64, 256), BF16))
        ct = dot(values[r : r + 64], jnp.concatenate(seen, axis=0))
        out += [ct[0:32, 0:128], ct[32:64, 128:256]]
    return jnp.concatenate(out, axis=0)


def finish(z, ctx, wo, gain, we, ws):
    branch = dot(ctx, wo, TN).astype(BF16)
    middle = z + branch.astype(F32)
    hidden = gelu(dot(layer_norm(middle, gain).astype(BF16), we)).astype(BF16)
    return middle + dot(hidden, ws)


def swap_halves(first, second):
    rows = first.shape[0]
    a = pltpu.roll(first.reshape(rows // 8, 8, 128), 4, 1)
    b = pltpu.roll(second.reshape(rows // 8, 8, 128), 4, 1)
    return jnp.where(iota(a.shape, 1) < 4, a, b).reshape(rows, 128)


def regular_kernel(
    x_ref, up_ref, down_ref, ag_ref, w_ref, wo_ref, pb_ref, hg_ref, we_ref, ws_ref,
    fa_ref, fb_ref, na_ref, nb_ref, sl_ref, sr_ref,
    bias, wqv, wk, xs,
):
    def store(head, yj, values):
        bias[yj * 8 : yj * 8 + 8, head * 128 : head * 128 + 128] = values

    fill_bias(pb_ref, 0, store)
    fill_weights(w_ref, 0, wqv, wk)
    xs[0:8] = up_ref[...]
    xs[8:72] = x_ref[...]
    xs[72:80] = down_ref[...]
    masks = lane_masks(64)
    wo = wo_ref[0]

    def step(w, carry):
        block = xs[pl.ds(w * 8, 8)].astype(F32).reshape(8, 2, 8, 128)
        z = jnp.concatenate([block[:, 0].reshape(64, 128), block[:, 1].reshape(64, 128)], axis=0)
        n = layer_norm(z, ag_ref[0:1, :]).astype(BF16)
        ctx = attention(
            n, [n[0:64], n[64:128]], masks, wqv, wk,
            lambda pair: bias[:, pair * 256 : pair * 256 + 256],
        )
        out = finish(z, ctx.astype(BF16), wo, hg_ref[0:1, :], we_ref[0], ws_ref[0])
        n1 = layer_norm(out, ag_ref[1:2, :])
        at = pl.multiple_of(w * 64, 64)
        fa_ref[pl.ds(at, 64), :] = swap_halves(out[0:64], out[64:128])
        fb_ref[pl.ds(at, 64), :] = swap_halves(out[64:128], out[0:64])
        na_ref[pl.ds(at, 64), :] = swap_halves(n1[0:64], n1[64:128]).astype(BF16)
        nb = swap_halves(n1[64:128], n1[0:64])
        nb_ref[pl.ds(at, 64), :] = nb.astype(BF16)
        pairs = nb.reshape(4, 2, 8, 128)
        even, odd = pairs[:, 0], pairs[:, 1]
        low = iota((4, 8, 128), 1) < 4
        half = pl.multiple_of(w * 32, 32)
        sr_ref[pl.ds(half, 32), :] = (
            jnp.where(low, even, pltpu.roll(odd, 4, 1)).reshape(32, 128).astype(BF16)
        )
        sl_ref[pl.ds(half, 32), :] = (
            jnp.where(low, pltpu.roll(even, 4, 1), odd).reshape(32, 128).astype(BF16)
        )
        return carry

    lax.fori_loop(0, 10, step, 0)


def shifted_kernel(
    flag_ref, fa_ref, fb_ref, na_ref, nb_ref, hl_ref, hr_ref,
    w_ref, wo_ref, pb_ref, hg_ref, we_ref, ws_ref,
    out_ref,
    bias, wqv, wk,
):
    sub = iota((8, 128), 0)
    lane = iota((8, 128), 1)
    last_col = jnp.where((lane & 7) < 4, flag_ref[3], flag_ref[2])
    cut_col = (lane >= 64) & (last_col > 0) & (((lane & 7) < 4) != (sub < 4))
    query_low = ((lane >> 3) & 7) < 4

    def store(head, yj, values):
        cut = values - 100.0 * LOG2E
        rows = slice(yj * 8, yj * 8 + 8)
        cols = slice(head * 128, head * 128 + 128)
        bias[0, rows, cols] = jnp.where(cut_col, cut, values)
        cut_row = jnp.logical_not(query_low) if yj < 4 else query_low
        bias[1, rows, cols] = jnp.where(cut_col | cut_row, cut, values)

    fill_bias(pb_ref, 1, store)
    fill_weights(w_ref, 1, wqv, wk)
    mask_a, _ = lane_masks(64)
    lanes = iota((64, 128), 1)
    mask_2 = jnp.where((lanes >= 64) & ((lanes & 7) < 4), 1.0, 0.0).astype(BF16)
    mask_0 = jnp.where((lanes >= 64) & ((lanes & 7) >= 4), 1.0, 0.0).astype(BF16)
    masks = [mask_a, mask_2, mask_0]
    wo = wo_ref[1]
    low = iota((8, 8, 128), 1) < 4
    low4 = iota((4, 8, 128), 1) < 4

    def attend(w, which):
        at = pl.multiple_of(w * 64 + 32, 32)
        half = pl.multiple_of(w * 32 + 16, 16)
        na = na_ref[pl.ds(at, 64), :]
        nb = nb_ref[pl.ds(at, 64), :]
        hl = hl_ref[pl.ds(half, 32), :].astype(F32).reshape(4, 8, 128)
        hr = hr_ref[pl.ds(half, 32), :].astype(F32).reshape(4, 8, 128)
        even = jnp.where(low4, hl, pltpu.roll(hr, 4, 1))
        odd = jnp.where(low4, pltpu.roll(hl, 4, 1), hr)
        halo = jnp.stack([even, odd], axis=1).reshape(8, 8, 128)
        own = nb.astype(F32).reshape(8, 8, 128)
        k2 = jnp.where(low, own, halo).reshape(64, 128).astype(BF16)
        k0 = jnp.where(low, halo, own).reshape(64, 128).astype(BF16)
        return attention(
            jnp.concatenate([na, nb], axis=0), [na, k2, k0], masks, wqv, wk,
            lambda pair: bias[which, :, pair * 256 : pair * 256 + 256],
        )

    def end(z, ctx):
        out = finish(z, ctx.astype(BF16), wo, hg_ref[1:2, :], we_ref[1], ws_ref[1])
        left = swap_halves(out[64:128], out[0:64]).reshape(8, 1, 8, 128)
        right = swap_halves(out[0:64], out[64:128]).reshape(8, 1, 8, 128)
        return jnp.concatenate([left, right], axis=1).reshape(8, 16, 128)

    def step(w, carry):
        at = pl.multiple_of(w * 64 + 32, 32)
        z = jnp.concatenate([fa_ref[pl.ds(at, 64), :], fb_ref[pl.ds(at, 64), :]], axis=0)
        out_ref[pl.ds(w * 8 - 4, 8)] = end(z, attend(w, 0))
        return carry

    lax.fori_loop(1, 8, step, 0)
    top = attend(0, flag_ref[0])
    bottom = attend(8, flag_ref[1])
    ctx = jnp.where(((iota((128, 128), 1) >> 3) & 7) < 4, bottom, top)
    z = jnp.concatenate(
        [fa_ref[544:576, :], fa_ref[64:96, :], fb_ref[544:576, :], fb_ref[64:96, :]], axis=0
    )
    ends = end(z, ctx)
    out_ref[60:64] = ends[0:4]
    out_ref[0:4] = ends[4:8]


def vmem():
    return pl.BlockSpec(memory_space=pltpu.VMEM)


def on_device(x, ag, tw, ow, pb, hg, ew, sw):
    height, breadth = x.shape[0], x.shape[1]
    up = from_behind(x[height - WIN :], "gy", 1)
    down = from_behind(x[:WIN], "gy", -1)
    tokens = (height + 2 * WIN) * WIN
    shape = jax.ShapeDtypeStruct
    fa, fb, na, nb, sl, sr = pl.pallas_call(
        regular_kernel,
        out_shape=[
            shape((tokens, C), F32),
            shape((tokens, C), F32),
            shape((tokens, C), BF16),
            shape((tokens, C), BF16),
            shape((tokens // 2, C), BF16),
            shape((tokens // 2, C), BF16),
        ],
        in_specs=[vmem()] * 10,
        out_specs=[vmem()] * 6,
        scratch_shapes=[
            pltpu.VMEM((64, HEADS * 128), F32),
            pltpu.VMEM((256, 128), BF16),
            pltpu.VMEM((256, 256), BF16),
            pltpu.VMEM((height + 2 * WIN, breadth, C), BF16),
        ],
        compiler_params=pltpu.CompilerParams(vmem_limit_bytes=32 * 1024 * 1024),
        name="regular",
    )(x, up, down, ag, tw, ow, pb, hg, ew, sw)
    hr = from_behind(sl, "gx", -1)
    hl = from_behind(sr, "gx", 1)
    row, col = lax.axis_index("gy"), lax.axis_index("gx")
    flags = jnp.stack(
        [row == 0, row == lax.axis_size("gy") - 1, col == 0, col == lax.axis_size("gx") - 1]
    ).astype(jnp.int32)
    return pl.pallas_call(
        shifted_kernel,
        out_shape=shape((height, breadth, C), F32),
        in_specs=[pl.BlockSpec(memory_space=pltpu.SMEM)] + [vmem()] * 12,
        out_specs=vmem(),
        scratch_shapes=[
            pltpu.VMEM((2, 64, HEADS * 128), F32),
            pltpu.VMEM((256, 128), BF16),
            pltpu.VMEM((256, 256), BF16),
        ],
        compiler_params=pltpu.CompilerParams(vmem_limit_bytes=32 * 1024 * 1024),
        name="shifted",
    )(flags, fa, fb, na, nb, hl, hr, tw, ow, pb, hg, ew, sw)


def solution(mesh):
    return jax.shard_map(
        on_device,
        mesh=mesh,
        in_specs=(P("gy", "gx", None), P(), P(), P(), P(), P(), P(), P()),
        out_specs=P("gy", "gx", None),
        check_vma=False,
    )
```

time: 99.2 us -> 65.1 us (0.66)
  the two profiles are of different devices: /device:TPU:2 before, /device:TPU:56 now
where the time goes in v1:
time: 65.1 us; the launch traced here: 64.7 us
  Pallas kernels  27.6 us (42%)
  starting transfers between devices  19.1 us (29%)
  waiting for transfers between devices  13.2 us (20%)
  local copies, waits for them, and re-layouts  4.61 us (7%)
    ppermute x4, starting transfers between devices, from_behind(): lax.ppermute(x, axis, [(i, (i + by) % length) for i in range(length)])  19.1 us
    pallas_call x1, Pallas kernels, on_device(): pl.pallas_call(regular_kernel, out_shape=[shape((tokens, C), F32), shape(...  15.6 us
    ppermute x4, waiting for transfers between devices, from_behind(): lax.ppermute(x, axis, [(i, (i + by) % length) for i in range(length)])  13.2 us
    pallas_call x1, Pallas kernels, on_device(): pl.pallas_call(shifted_kernel, out_shape=shape((height, breadth, C), F32)...  12 us
    unnamed x20, local copies, waits for them, and re-layouts  3.8 us
  transfers between devices with their start and end apart: 4, of which 3 were waited for; matrix products, arithmetic and copies ran while one was open for 0% of the time, Pallas kernels for 0%

profile of v1, /device:TPU:56, one launch (start us, length us, event | category | flops | bytes accessed | tf_op | source)
XLA Modules:
  0.0 64.7 jit_solution(18325977068567879023)
XLA Ops:
  0.0 0.0 copy-start.6
  0.0 0.8 %fusion = (bf16[8,16,128]{2,1,0:T(8,128)(2,1)S(1)}, bf16[8,16,128]{2,1,0:T(8,128)(2,1)S(1)}) fusion(bf16[64,16,128]{2,1,0:T(8,128)(2,1)} %x_ref.1), kind=kLoop, calls=%fused_computation.1 | loop fusion | bytes 131072 | tf_op jit(solution)/shard_map/slice | solution.py:279
  0.8 11.3 %collective-permute-start.1 = (bf16[8,16,128]{2,1,0:T(8,128)(2,1)S(1)}, bf16[8,16,128]{2,1,0:T(8,128)(2,1)S(1)}, u32[]{:S(2)}, u32[]{:S(2)}) collective-permute-start(bf16[8,16,128]{2,1,0:T(8,128)(2,1)S(1)} %get-tuple-element.17), channel_id=1, source_target_pairs={{0,496},{16,0},{32,16},{48,32},{64,48},{80,64},{96,80},{112,96},{1... | collective-permute-start | bytes 98312 | tf_op jit(solution)/shard_map/ppermute | solution.py:27
  12.1 1.9 %collective-permute-start = (bf16[8,16,128]{2,1,0:T(8,128)(2,1)S(1)}, bf16[8,16,128]{2,1,0:T(8,128)(2,1)S(1)}, u32[]{:S(2)}, u32[]{:S(2)}) collective-permute-start(bf16[8,16,128]{2,1,0:T(8,128)(2,1)S(1)} %get-tuple-element.18), channel_id=1, source_target_pairs={{0,16},{16,32},{32,48},{48,64},{64,80},{80,96},{96,112},{112,128},... | collective-permute-start | bytes 98312 | tf_op jit(solution)/shard_map/ppermute | solution.py:27
  14.1 0.0 copy-start.7
  14.1 0.0 copy-start.9
  14.1 0.0 copy-start.8
  14.1 0.0 collective-permute-done.1.down_ref
  14.1 5.4 %collective-permute-done.up_ref = bf16[8,16,128]{2,1,0:T(8,128)(2,1)S(1)} collective-permute-done((bf16[8,16,128]{2,1,0:T(8,128)(2,1)S(1)}, bf16[8,16,128]{2,1,0:T(8,128)(2,1)S(1)}, u32[]{:S(2)}, u32[]{:S(2)}) %collective-permute-start) | collective-permute-done | bytes 32800 | tf_op jit(solution)/shard_map/ppermute | solution.py:27
  19.5 0.0 copy-done.6
  19.5 0.0 copy-done.7
  19.5 0.0 copy-done.9
  19.5 0.0 copy-done.8
  19.5 0.0 copy-start
  19.5 0.9 %copy-done = bf16[2,128,512]{2,1,0:T(8,128)(2,1)S(1)} copy-done((bf16[2,128,512]{2,1,0:T(8,128)(2,1)S(1)}, bf16[2,128,512]{2,1,0:T(8,128)(2,1)}, u32[]{:S(2)}) %copy-start) | copy-done | bytes 262168
  20.4 0.0 copy-start.2
  20.4 0.9 %copy-done.2 = bf16[2,512,128]{2,1,0:T(8,128)(2,1)S(1)} copy-done((bf16[2,512,128]{2,1,0:T(8,128)(2,1)S(1)}, bf16[2,512,128]{2,1,0:T(8,128)(2,1)}, u32[]{:S(2)}) %copy-start.2) | copy-done | bytes 262168
  21.4 0.0 copy-start.4
  21.4 0.9 %copy-done.4 = bf16[2,128,384]{2,1,0:T(8,128)(2,1)S(1)} copy-done((bf16[2,128,384]{2,1,0:T(8,128)(2,1)S(1)}, bf16[2,128,384]{2,1,0:T(8,128)(2,1)}, u32[]{:S(2)}) %copy-start.4) | copy-done | bytes 196632
  22.3 0.0 copy-start.5
  22.3 0.9 %copy-done.5 = bf16[64,16,128]{2,1,0:T(8,128)(2,1)S(1)} copy-done((bf16[64,16,128]{2,1,0:T(8,128)(2,1)S(1)}, bf16[64,16,128]{2,1,0:T(8,128)(2,1)}, u32[]{:S(2)}) %copy-start.5) | copy-done | bytes 262168
  23.3 0.0 copy-start.1
  23.3 0.0 copy-start.3
  23.3 15.6 %regular.1 = (f32[640,128]{1,0:T(8,128)S(1)}, f32[640,128]{1,0:T(8,128)S(1)}, bf16[640,128]{1,0:T(8,128)(2,1)S(1)}, bf16[640,128]{1,0:T(8,128)(2,1)S(1)}, bf16[3...) custom-call(bf16[64,16,128]{2,1,0:T(8,128)(2,1)S(1)} %copy-done.5, ...), custom_call_target="tpu_custom_call" | custom-call | tf_op jit(solution)/shard_map/regular/pallas_call | solution.py:282
  38.9 3.8 %collective-permute-start.2 = (bf16[320,128]{1,0:T(8,128)(2,1)S(1)}, bf16[320,128]{1,0:T(8,128)(2,1)S(1)}, u32[]{:S(2)}, u32[]{:S(2)}) collective-permute-start(bf16[320,128]{1,0:T(8,128)(2,1)S(1)} %get-tuple-element.15), channel_id=1, source_target_pairs={{0,1},{1,2},{2,3},{3,4},{4,5},{5,6},{6,7},{7,8},{8,9},{9,10},{10,1... | collective-permute-start | bytes 245768 | tf_op jit(solution)/shard_map/ppermute | solution.py:27
  42.7 2.0 %collective-permute-start.3 = (bf16[320,128]{1,0:T(8,128)(2,1)S(1)}, bf16[320,128]{1,0:T(8,128)(2,1)S(1)}, u32[]{:S(2)}, u32[]{:S(2)}) collective-permute-start(bf16[320,128]{1,0:T(8,128)(2,1)S(1)} %get-tuple-element.16), channel_id=1, source_target_pairs={{0,15},{1,0},{2,1},{3,2},{4,3},{5,4},{6,5},{7,6},{8,7},{9,8},{10,9... | collective-permute-start | bytes 245768 | tf_op jit(solution)/shard_map/ppermute | solution.py:27
  44.7 0.1 add_convert_fusion.flag_ref
  44.8 0.4 collective-permute-done.2.hl_ref
  45.2 7.5 %collective-permute-done.3.hr_ref = bf16[320,128]{1,0:T(8,128)(2,1)S(1)} collective-permute-done((bf16[320,128]{1,0:T(8,128)(2,1)S(1)}, bf16[320,128]{1,0:T(8,128)(2,1)S(1)}, u32[]{:S(2)}, u32[]{:S(2)}) %collective-permute-start.3) | collective-permute-done | bytes 81952 | tf_op jit(solution)/shard_map/ppermute | solution.py:27
  52.7 0.0 copy-done.1
  52.7 0.0 copy-done.3
  52.7 12.0 %shifted.1 = f32[64,16,128]{2,1,0:T(8,128)} custom-call(s32[4]{0:T(128)S(1)} %add_convert_fusion.flag_ref, f32[640,128]{1,0:T(8,128)S(1)} %get-tuple-element.11.fa_ref, f32[640,128]{1,0:T(8,128)S(1)} %get-tuple-element.12.fb_ref, bf16[640,128]{1,0:T(8,128)(2,1)S(1)} %get-tuple-element.13.na_ref, bf16[640,128]{1,0:T(8,128)(2,1)S(1)} %get-tuple-element.14.nb_ref, ...), custom_call_target="tpu_custom_call" | custom-call | tf_op jit(solution)/shard_map/shifted/pallas_call | solution.py:309
Async XLA Ops:
  0.0 19.5 %copy-start.6 = (bf16[2,128,128]{2,1,0:T(8,128)(2,1)S(1)}, bf16[2,128,128]{2,1,0:T(8,128)(2,1)}, u32[]{:S(2)}) copy-start(bf16[2,128,128]{2,1,0:T(8,128)(2,1)} %wo_ref.3) | copy-start | bytes 196612
  0.8 13.3 %collective-permute-start.1 = (bf16[8,16,128]{2,1,0:T(8,128)(2,1)S(1)}, bf16[8,16,128]{2,1,0:T(8,128)(2,1)S(1)}, u32[]{:S(2)}, u32[]{:S(2)}) collective-permute-start(bf16[8,16,128]{2,1,0:T(8,128)(2,1)S(1)} %get-tuple-element.17), channel_id=1, source_target_pairs={{0,496},{16,0},{32,16},{48,32},{64,48},{80,64},{96,80},{112,96},{1... | collective-permute-start | bytes 98312 | tf_op jit(solution)/shard_map/ppermute | solution.py:27
  12.1 7.3 %collective-permute-start = (bf16[8,16,128]{2,1,0:T(8,128)(2,1)S(1)}, bf16[8,16,128]{2,1,0:T(8,128)(2,1)S(1)}, u32[]{:S(2)}, u32[]{:S(2)}) collective-permute-start(bf16[8,16,128]{2,1,0:T(8,128)(2,1)S(1)} %get-tuple-element.18), channel_id=1, source_target_pairs={{0,16},{16,32},{32,48},{48,64},{64,80},{80,96},{96,112},{112,128},... | collective-permute-start | bytes 98312 | tf_op jit(solution)/shard_map/ppermute | solution.py:27
  14.1 5.4 %copy-start.7 = (f32[2,4,225]{2,1,0:T(4,128)S(1)}, f32[2,4,225]{2,1,0:T(4,128)}, u32[]{:S(2)}) copy-start(f32[2,4,225]{2,1,0:T(4,128)} %pb_ref.3) | copy-start | bytes 21604
  14.1 5.4 %copy-start.9 = (f32[2,128]{1,0:T(2,128)S(1)}, f32[2,128]{1,0:T(2,128)}, u32[]{:S(2)}) copy-start(f32[2,128]{1,0:T(2,128)} %ag_ref.1) | copy-start | bytes 3076
  14.1 5.4 %copy-start.8 = (f32[2,128]{1,0:T(2,128)S(1)}, f32[2,128]{1,0:T(2,128)}, u32[]{:S(2)}) copy-start(f32[2,128]{1,0:T(2,128)} %hg_ref.3) | copy-start | bytes 3076
  19.5 1.0 %copy-start = (bf16[2,128,512]{2,1,0:T(8,128)(2,1)S(1)}, bf16[2,128,512]{2,1,0:T(8,128)(2,1)}, u32[]{:S(2)}) copy-start(bf16[2,128,512]{2,1,0:T(8,128)(2,1)} %we_ref.3) | copy-start | bytes 786436
  20.4 0.9 %copy-start.2 = (bf16[2,512,128]{2,1,0:T(8,128)(2,1)S(1)}, bf16[2,512,128]{2,1,0:T(8,128)(2,1)}, u32[]{:S(2)}) copy-start(bf16[2,512,128]{2,1,0:T(8,128)(2,1)} %ws_ref.3) | copy-start | bytes 786436
  21.4 0.9 %copy-start.4 = (bf16[2,128,384]{2,1,0:T(8,128)(2,1)S(1)}, bf16[2,128,384]{2,1,0:T(8,128)(2,1)}, u32[]{:S(2)}) copy-start(bf16[2,128,384]{2,1,0:T(8,128)(2,1)} %w_ref.3) | copy-start | bytes 589828
  22.3 0.9 %copy-start.5 = (bf16[64,16,128]{2,1,0:T(8,128)(2,1)S(1)}, bf16[64,16,128]{2,1,0:T(8,128)(2,1)}, u32[]{:S(2)}) copy-start(bf16[64,16,128]{2,1,0:T(8,128)(2,1)} %x_ref.1) | copy-start | bytes 786436
  23.3 29.4 %copy-start.1 = (bf16[2,128,512]{2,1,0:T(8,128)(2,1)S(1)}, bf16[2,128,512]{2,1,0:T(8,128)(2,1)}, u32[]{:S(2)}) copy-start(bf16[2,128,512]{2,1,0:T(8,128)(2,1)} %we_ref.3) | copy-start | bytes 786436
  23.3 29.4 %copy-start.3 = (bf16[2,512,128]{2,1,0:T(8,128)(2,1)S(1)}, bf16[2,512,128]{2,1,0:T(8,128)(2,1)}, u32[]{:S(2)}) copy-start(bf16[2,512,128]{2,1,0:T(8,128)(2,1)} %ws_ref.3) | copy-start | bytes 786436
  38.9 6.3 %collective-permute-start.2 = (bf16[320,128]{1,0:T(8,128)(2,1)S(1)}, bf16[320,128]{1,0:T(8,128)(2,1)S(1)}, u32[]{:S(2)}, u32[]{:S(2)}) collective-permute-start(bf16[320,128]{1,0:T(8,128)(2,1)S(1)} %get-tuple-element.15), channel_id=1, source_target_pairs={{0,1},{1,2},{2,3},{3,4},{4,5},{5,6},{6,7},{7,8},{8,9},{9,10},{10,1... | collective-permute-start | bytes 245768 | tf_op jit(solution)/shard_map/ppermute | solution.py:27
  42.7 9.9 %collective-permute-start.3 = (bf16[320,128]{1,0:T(8,128)(2,1)S(1)}, bf16[320,128]{1,0:T(8,128)(2,1)S(1)}, u32[]{:S(2)}, u32[]{:S(2)}) collective-permute-start(bf16[320,128]{1,0:T(8,128)(2,1)S(1)} %get-tuple-element.16), channel_id=1, source_target_pairs={{0,15},{1,0},{2,1},{3,2},{4,3},{5,4},{6,5},{7,6},{8,7},{9,8},{10,9... | collective-permute-start | bytes 245768 | tf_op jit(solution)/shard_map/ppermute | solution.py:27

commit v2 on v1

--- a/solution.py
+++ b/solution.py
@@ -14,6 +14,9 @@
 HD = 32
 SHIFT = 4
 EPSILON = 1e-05
+ROWS_1 = 10
+ROWS_2 = 9
+ROWS_3 = 8
 LOG2E = math.log2(math.e)
 SCALE = HD ** (-0.5) * LOG2E
 F32 = jnp.float32
@@ -82,11 +85,6 @@
     wk[128:256, 128:256] = jnp.where(lane >= 64, keys, zero).astype(BF16)
 
 
-def softmax_columns(s):
-    p = jnp.exp2(s - jnp.max(s, axis=0, keepdims=True))
-    return (p * (1.0 / jnp.sum(p, axis=0, keepdims=True))).astype(BF16)
-
-
 def dot(a, b, dims=None):
     if dims is None:
         return jnp.dot(a, b, preferred_element_type=F32)
@@ -95,6 +93,7 @@
 
 def attention(query_tokens, key_tokens, masks, wqv, wk, bias_of):
     windows = len(key_tokens)
+    qt = dot(wqv[0:128, :], query_tokens, NT).astype(BF16)
     if windows == 2:
         vt = dot(wqv[128:256, :], jnp.concatenate(key_tokens, axis=0), NT).astype(BF16)
         keys = dot(jnp.concatenate(key_tokens, axis=1), wk[...]).astype(BF16)
@@ -112,9 +111,9 @@
             jnp.concatenate([keys[:, 0:128], last[:, 0:128]], axis=1),
             jnp.concatenate([keys[:, 128:256], last[:, 128:256]], axis=1),
         ]
-    qt = dot(wqv[0:128, :], query_tokens, NT).astype(BF16)
+    yield
     zero = jnp.zeros((32, 128), BF16)
-    out = []
+    scores = []
     for pair in range(2):
         r = 64 * pair
         rows = []
@@ -123,8 +122,18 @@
             rows.append(jnp.concatenate([zero, qt[r + 32 : r + 64] * mask[0:32]], axis=1))
         if windows == 3:
             rows.append(jnp.zeros((64, 256), BF16))
-        s = dot(keys[pair], jnp.concatenate(rows, axis=0))
-        p = softmax_columns(s * SCALE + bias_of(pair))
+        scores.append(dot(keys[pair], jnp.concatenate(rows, axis=0)))
+    yield
+    tops = []
+    for pair in range(2):
+        scores[pair] = scores[pair] * SCALE + bias_of(pair)
+        tops.append(jnp.max(scores[pair], axis=0, keepdims=True))
+    yield
+    out = []
+    for pair in range(2):
+        r = 64 * pair
+        p = jnp.exp2(scores[pair] - tops[pair])
+        p = (p * (1.0 / jnp.sum(p, axis=0, keepdims=True))).astype(BF16)
         seen = [
             jnp.concatenate([p[:, 0:128] * mask, p[:, 128:256] * mask], axis=1) for mask in masks
         ]
@@ -132,14 +141,36 @@
             seen.append(jnp.zeros((64, 256), BF16))
         ct = dot(values[r : r + 64], jnp.concatenate(seen, axis=0))
         out += [ct[0:32, 0:128], ct[32:64, 128:256]]
-    return jnp.concatenate(out, axis=0)
+    yield
+    return jnp.concatenate(out, axis=0).astype(BF16)
 
 
 def finish(z, ctx, wo, gain, we, ws):
     branch = dot(ctx, wo, TN).astype(BF16)
+    yield
     middle = z + branch.astype(F32)
-    hidden = gelu(dot(layer_norm(middle, gain).astype(BF16), we)).astype(BF16)
-    return middle + dot(hidden, ws)
+    normed = layer_norm(middle, gain).astype(BF16)
+    yield
+    hidden = dot(normed, we)
+    yield
+    hidden = gelu(hidden).astype(BF16)
+    yield
+    out = middle + dot(hidden, ws)
+    yield
+    return out
+
+
+def together(chains):
+    results = [None] * len(chains)
+    live = list(range(len(chains)))
+    while live:
+        for i in list(live):
+            try:
+                next(chains[i])
+            except StopIteration as stop:
+                results[i] = stop.value
+                live.remove(i)
+    return results
 
 
 def swap_halves(first, second):
@@ -165,16 +196,27 @@
     masks = lane_masks(64)
     wo = wo_ref[0]
 
-    def step(w, carry):
+    def chain(w):
         block = xs[pl.ds(w * 8, 8)].astype(F32).reshape(8, 2, 8, 128)
         z = jnp.concatenate([block[:, 0].reshape(64, 128), block[:, 1].reshape(64, 128)], axis=0)
         n = layer_norm(z, ag_ref[0:1, :]).astype(BF16)
-        ctx = attention(
+        yield
+        ctx = yield from attention(
             n, [n[0:64], n[64:128]], masks, wqv, wk,
             lambda pair: bias[:, pair * 256 : pair * 256 + 256],
         )
-        out = finish(z, ctx.astype(BF16), wo, hg_ref[0:1, :], we_ref[0], ws_ref[0])
+        out = yield from finish(z, ctx, wo, hg_ref[0:1, :], we_ref[0], ws_ref[0])
         n1 = layer_norm(out, ag_ref[1:2, :])
+        yield
+        return out, n1
+
+    def step(i, carry):
+        rows = [i * ROWS_1 + u for u in range(ROWS_1)]
+        for w, (out, n1) in zip(rows, together([chain(w) for w in rows])):
+            save(w, out, n1)
+        return carry
+
+    def save(w, out, n1):
         at = pl.multiple_of(w * 64, 64)
         fa_ref[pl.ds(at, 64), :] = swap_halves(out[0:64], out[64:128])
         fb_ref[pl.ds(at, 64), :] = swap_halves(out[64:128], out[0:64])
@@ -191,16 +233,15 @@
         sl_ref[pl.ds(half, 32), :] = (
             jnp.where(low, pltpu.roll(even, 4, 1), odd).reshape(32, 128).astype(BF16)
         )
-        return carry
-
-    lax.fori_loop(0, 10, step, 0)
+
+    lax.fori_loop(0, 10 // ROWS_1, step, 0)
 
 
 def shifted_kernel(
     flag_ref, fa_ref, fb_ref, na_ref, nb_ref, hl_ref, hr_ref,
     w_ref, wo_ref, pb_ref, hg_ref, we_ref, ws_ref,
     out_ref,
-    bias, wqv, wk,
+    bias, wqv, wk, context,
 ):
     sub = iota((8, 128), 0)
     lane = iota((8, 128), 1)
@@ -240,33 +281,45 @@
         own = nb.astype(F32).reshape(8, 8, 128)
         k2 = jnp.where(low, own, halo).reshape(64, 128).astype(BF16)
         k0 = jnp.where(low, halo, own).reshape(64, 128).astype(BF16)
-        return attention(
+        ctx = yield from attention(
             jnp.concatenate([na, nb], axis=0), [na, k2, k0], masks, wqv, wk,
             lambda pair: bias[which, :, pair * 256 : pair * 256 + 256],
         )
 
-    def end(z, ctx):
-        out = finish(z, ctx.astype(BF16), wo, hg_ref[1:2, :], we_ref[1], ws_ref[1])
+        return ctx
+
+    def attend_step(i, carry):
+        rows = [i * ROWS_2 + u for u in range(ROWS_2)]
+        chains = []
+        for w in rows:
+            which = jnp.where(w == 0, flag_ref[0], jnp.where(w == 8, flag_ref[1], 0))
+            chains.append(attend(w, which))
+        for w, ctx in zip(rows, together(chains)):
+            context[w] = ctx
+        return carry
+
+    lax.fori_loop(0, 9 // ROWS_2, attend_step, 0)
+    swapped = ((iota((128, 128), 1) >> 3) & 7) < 4
+    context[0] = jnp.where(swapped, context[8].astype(F32), context[0].astype(F32)).astype(BF16)
+
+    def end(w):
+        low = pl.multiple_of(jnp.where(w == 0, 544, w * 64 + 32), 32)
+        high = pl.multiple_of(w * 64 + 64, 64)
+        parts = [f[pl.ds(at, 32), :] for f in (fa_ref, fb_ref) for at in (low, high)]
+        z = jnp.concatenate(parts, axis=0)
+        out = yield from finish(z, context[w], wo, hg_ref[1:2, :], we_ref[1], ws_ref[1])
         left = swap_halves(out[64:128], out[0:64]).reshape(8, 1, 8, 128)
         right = swap_halves(out[0:64], out[64:128]).reshape(8, 1, 8, 128)
         return jnp.concatenate([left, right], axis=1).reshape(8, 16, 128)
 
-    def step(w, carry):
-        at = pl.multiple_of(w * 64 + 32, 32)
-        z = jnp.concatenate([fa_ref[pl.ds(at, 64), :], fb_ref[pl.ds(at, 64), :]], axis=0)
-        out_ref[pl.ds(w * 8 - 4, 8)] = end(z, attend(w, 0))
+    def end_step(i, carry):
+        rows = [i * ROWS_3 + u for u in range(ROWS_3)]
+        for w, out in zip(rows, together([end(w) for w in rows])):
+            out_ref[pl.ds(jnp.where(w == 0, 60, w * 8 - 4), 4)] = out[0:4]
+            out_ref[pl.ds(w * 8, 4)] = out[4:8]
         return carry
 
-    lax.fori_loop(1, 8, step, 0)
-    top = attend(0, flag_ref[0])
-    bottom = attend(8, flag_ref[1])
-    ctx = jnp.where(((iota((128, 128), 1) >> 3) & 7) < 4, bottom, top)
-    z = jnp.concatenate(
-        [fa_ref[544:576, :], fa_ref[64:96, :], fb_ref[544:576, :], fb_ref[64:96, :]], axis=0
-    )
-    ends = end(z, ctx)
-    out_ref[60:64] = ends[0:4]
-    out_ref[0:4] = ends[4:8]
+    lax.fori_loop(0, 8 // ROWS_3, end_step, 0)
 
 
 def vmem():
@@ -315,6 +368,7 @@
             pltpu.VMEM((2, 64, HEADS * 128), F32),
             pltpu.VMEM((256, 128), BF16),
             pltpu.VMEM((256, 256), BF16),
+            pltpu.VMEM((9, 128, 128), BF16),
         ],
         compiler_params=pltpu.CompilerParams(vmem_limit_bytes=32 * 1024 * 1024),
         name="shifted",

time: 65.1 us -> 45.6 us (0.70)
  Pallas kernels: 27.6 us -> 8.19 us
    pallas_call x1, Pallas kernels: 15.6 us -> 3.73 us  [on_device(): pl.pallas_call(regular_kernel, out_shape=[shape((tokens, C), F32), shape(...]
    pallas_call x1, Pallas kernels: 12 us -> 4.47 us  [on_device(): pl.pallas_call(shifted_kernel, out_shape=shape((height, breadth, C), F32)...]
where the time goes in v2:
time: 45.6 us; the launch traced here: 45.3 us
  starting transfers between devices  19.1 us (42%)
  waiting for transfers between devices  13.2 us (29%)
  Pallas kernels  8.19 us (18%)
  local copies, waits for them, and re-layouts  4.61 us (10%)
    ppermute x4, starting transfers between devices, from_behind(): lax.ppermute(x, axis, [(i, (i + by) % length) for i in range(length)])  19.1 us
    ppermute x4, waiting for transfers between devices, from_behind(): lax.ppermute(x, axis, [(i, (i + by) % length) for i in range(length)])  13.2 us
    pallas_call x1, Pallas kernels, on_device(): pl.pallas_call(shifted_kernel, out_shape=shape((height, breadth, C), F32)...  4.47 us
    unnamed x20, local copies, waits for them, and re-layouts  3.8 us
    pallas_call x1, Pallas kernels, on_device(): pl.pallas_call(regular_kernel, out_shape=[shape((tokens, C), F32), shape(...  3.73 us
  transfers between devices with their start and end apart: 4, of which 3 were waited for; matrix products, arithmetic and copies ran while one was open for 0% of the time, Pallas kernels for 0%

profile of v2, /device:TPU:56, one launch (start us, length us, event | category | flops | bytes accessed | tf_op | source)
XLA Modules:
  0.0 45.3 jit_solution(6467170747801304174)
XLA Ops:
  0.0 0.0 copy-start.6
  0.0 0.8 %fusion = (bf16[8,16,128]{2,1,0:T(8,128)(2,1)S(1)}, bf16[8,16,128]{2,1,0:T(8,128)(2,1)S(1)}) fusion(bf16[64,16,128]{2,1,0:T(8,128)(2,1)} %x_ref.1), kind=kLoop, calls=%fused_computation.1 | loop fusion | bytes 131072 | tf_op jit(solution)/shard_map/slice | solution.py:332
  0.8 11.3 %collective-permute-start.1 = (bf16[8,16,128]{2,1,0:T(8,128)(2,1)S(1)}, bf16[8,16,128]{2,1,0:T(8,128)(2,1)S(1)}, u32[]{:S(2)}, u32[]{:S(2)}) collective-permute-start(bf16[8,16,128]{2,1,0:T(8,128)(2,1)S(1)} %get-tuple-element.17), channel_id=1, source_target_pairs={{0,496},{16,0},{32,16},{48,32},{64,48},{80,64},{96,80},{112,96},{1... | collective-permute-start | bytes 98312 | tf_op jit(solution)/shard_map/ppermute | solution.py:30
  12.1 1.9 %collective-permute-start = (bf16[8,16,128]{2,1,0:T(8,128)(2,1)S(1)}, bf16[8,16,128]{2,1,0:T(8,128)(2,1)S(1)}, u32[]{:S(2)}, u32[]{:S(2)}) collective-permute-start(bf16[8,16,128]{2,1,0:T(8,128)(2,1)S(1)} %get-tuple-element.18), channel_id=1, source_target_pairs={{0,16},{16,32},{32,48},{48,64},{64,80},{80,96},{96,112},{112,128},... | collective-permute-start | bytes 98312 | tf_op jit(solution)/shard_map/ppermute | solution.py:30
  14.1 0.0 copy-start.7
  14.1 0.0 copy-start.9
  14.1 0.0 copy-start.8
  14.1 0.0 collective-permute-done.1.down_ref
  14.1 5.4 %collective-permute-done.up_ref = bf16[8,16,128]{2,1,0:T(8,128)(2,1)S(1)} collective-permute-done((bf16[8,16,128]{2,1,0:T(8,128)(2,1)S(1)}, bf16[8,16,128]{2,1,0:T(8,128)(2,1)S(1)}, u32[]{:S(2)}, u32[]{:S(2)}) %collective-permute-start) | collective-permute-done | bytes 32800 | tf_op jit(solution)/shard_map/ppermute | solution.py:30
  19.5 0.0 copy-done.6
  19.5 0.0 copy-done.7
  19.5 0.0 copy-done.9
  19.5 0.0 copy-done.8
  19.5 0.0 copy-start
  19.5 0.9 %copy-done = bf16[2,128,512]{2,1,0:T(8,128)(2,1)S(1)} copy-done((bf16[2,128,512]{2,1,0:T(8,128)(2,1)S(1)}, bf16[2,128,512]{2,1,0:T(8,128)(2,1)}, u32[]{:S(2)}) %copy-start) | copy-done | bytes 262168
  20.4 0.0 copy-start.2
  20.4 0.9 %copy-done.2 = bf16[2,512,128]{2,1,0:T(8,128)(2,1)S(1)} copy-done((bf16[2,512,128]{2,1,0:T(8,128)(2,1)S(1)}, bf16[2,512,128]{2,1,0:T(8,128)(2,1)}, u32[]{:S(2)}) %copy-start.2) | copy-done | bytes 262168
  21.4 0.0 copy-start.4
  21.4 0.9 %copy-done.4 = bf16[2,128,384]{2,1,0:T(8,128)(2,1)S(1)} copy-done((bf16[2,128,384]{2,1,0:T(8,128)(2,1)S(1)}, bf16[2,128,384]{2,1,0:T(8,128)(2,1)}, u32[]{:S(2)}) %copy-start.4) | copy-done | bytes 196632
  22.3 0.0 copy-start.5
  22.3 0.9 %copy-done.5 = bf16[64,16,128]{2,1,0:T(8,128)(2,1)S(1)} copy-done((bf16[64,16,128]{2,1,0:T(8,128)(2,1)S(1)}, bf16[64,16,128]{2,1,0:T(8,128)(2,1)}, u32[]{:S(2)}) %copy-start.5) | copy-done | bytes 262168
  23.3 0.0 copy-start.1
  23.3 0.0 copy-start.3
  23.3 3.7 %regular.1 = (f32[640,128]{1,0:T(8,128)S(1)}, f32[640,128]{1,0:T(8,128)S(1)}, bf16[640,128]{1,0:T(8,128)(2,1)S(1)}, bf16[640,128]{1,0:T(8,128)(2,1)S(1)}, bf16[3...) custom-call(bf16[64,16,128]{2,1,0:T(8,128)(2,1)S(1)} %copy-done.5, ...), custom_call_target="tpu_custom_call" | custom-call | tf_op jit(solution)/shard_map/regular/pallas_call | solution.py:335
  27.0 3.8 %collective-permute-start.2 = (bf16[320,128]{1,0:T(8,128)(2,1)S(1)}, bf16[320,128]{1,0:T(8,128)(2,1)S(1)}, u32[]{:S(2)}, u32[]{:S(2)}) collective-permute-start(bf16[320,128]{1,0:T(8,128)(2,1)S(1)} %get-tuple-element.15), channel_id=1, source_target_pairs={{0,1},{1,2},{2,3},{3,4},{4,5},{5,6},{6,7},{7,8},{8,9},{9,10},{10,1... | collective-permute-start | bytes 245768 | tf_op jit(solution)/shard_map/ppermute | solution.py:30
  30.9 2.0 %collective-permute-start.3 = (bf16[320,128]{1,0:T(8,128)(2,1)S(1)}, bf16[320,128]{1,0:T(8,128)(2,1)S(1)}, u32[]{:S(2)}, u32[]{:S(2)}) collective-permute-start(bf16[320,128]{1,0:T(8,128)(2,1)S(1)} %get-tuple-element.16), channel_id=1, source_target_pairs={{0,15},{1,0},{2,1},{3,2},{4,3},{5,4},{6,5},{7,6},{8,7},{9,8},{10,9... | collective-permute-start | bytes 245768 | tf_op jit(solution)/shard_map/ppermute | solution.py:30
  32.9 0.1 add_convert_fusion.flag_ref
  33.0 0.4 collective-permute-done.2.hl_ref
  33.3 7.5 %collective-permute-done.3.hr_ref = bf16[320,128]{1,0:T(8,128)(2,1)S(1)} collective-permute-done((bf16[320,128]{1,0:T(8,128)(2,1)S(1)}, bf16[320,128]{1,0:T(8,128)(2,1)S(1)}, u32[]{:S(2)}, u32[]{:S(2)}) %collective-permute-start.3) | collective-permute-done | bytes 81952 | tf_op jit(solution)/shard_map/ppermute | solution.py:30
  40.8 0.0 copy-done.1
  40.8 0.0 copy-done.3
  40.8 4.5 %shifted.1 = f32[64,16,128]{2,1,0:T(8,128)} custom-call(s32[4]{0:T(128)S(1)} %add_convert_fusion.flag_ref, f32[640,128]{1,0:T(8,128)S(1)} %get-tuple-element.11.fa_ref, f32[640,128]{1,0:T(8,128)S(1)} %get-tuple-element.12.fb_ref, bf16[640,128]{1,0:T(8,128)(2,1)S(1)} %get-tuple-element.13.na_ref, bf16[640,128]{1,0:T(8,128)(2,1)S(1)} %get-tuple-element.14.nb_ref, ...), custom_call_target="tpu_custom_call" | custom-call | tf_op jit(solution)/shard_map/shifted/pallas_call | solution.py:362
Async XLA Ops:
  0.0 19.5 %copy-start.6 = (bf16[2,128,128]{2,1,0:T(8,128)(2,1)S(1)}, bf16[2,128,128]{2,1,0:T(8,128)(2,1)}, u32[]{:S(2)}) copy-start(bf16[2,128,128]{2,1,0:T(8,128)(2,1)} %wo_ref.3) | copy-start | bytes 196612
  0.8 13.3 %collective-permute-start.1 = (bf16[8,16,128]{2,1,0:T(8,128)(2,1)S(1)}, bf16[8,16,128]{2,1,0:T(8,128)(2,1)S(1)}, u32[]{:S(2)}, u32[]{:S(2)}) collective-permute-start(bf16[8,16,128]{2,1,0:T(8,128)(2,1)S(1)} %get-tuple-element.17), channel_id=1, source_target_pairs={{0,496},{16,0},{32,16},{48,32},{64,48},{80,64},{96,80},{112,96},{1... | collective-permute-start | bytes 98312 | tf_op jit(solution)/shard_map/ppermute | solution.py:30
  12.1 7.3 %collective-permute-start = (bf16[8,16,128]{2,1,0:T(8,128)(2,1)S(1)}, bf16[8,16,128]{2,1,0:T(8,128)(2,1)S(1)}, u32[]{:S(2)}, u32[]{:S(2)}) collective-permute-start(bf16[8,16,128]{2,1,0:T(8,128)(2,1)S(1)} %get-tuple-element.18), channel_id=1, source_target_pairs={{0,16},{16,32},{32,48},{48,64},{64,80},{80,96},{96,112},{112,128},... | collective-permute-start | bytes 98312 | tf_op jit(solution)/shard_map/ppermute | solution.py:30
  14.1 5.4 %copy-start.7 = (f32[2,4,225]{2,1,0:T(4,128)S(1)}, f32[2,4,225]{2,1,0:T(4,128)}, u32[]{:S(2)}) copy-start(f32[2,4,225]{2,1,0:T(4,128)} %pb_ref.3) | copy-start | bytes 21604
  14.1 5.4 %copy-start.9 = (f32[2,128]{1,0:T(2,128)S(1)}, f32[2,128]{1,0:T(2,128)}, u32[]{:S(2)}) copy-start(f32[2,128]{1,0:T(2,128)} %ag_ref.1) | copy-start | bytes 3076
  14.1 5.4 %copy-start.8 = (f32[2,128]{1,0:T(2,128)S(1)}, f32[2,128]{1,0:T(2,128)}, u32[]{:S(2)}) copy-start(f32[2,128]{1,0:T(2,128)} %hg_ref.3) | copy-start | bytes 3076
  19.5 1.0 %copy-start = (bf16[2,128,512]{2,1,0:T(8,128)(2,1)S(1)}, bf16[2,128,512]{2,1,0:T(8,128)(2,1)}, u32[]{:S(2)}) copy-start(bf16[2,128,512]{2,1,0:T(8,128)(2,1)} %we_ref.3) | copy-start | bytes 786436
  20.4 0.9 %copy-start.2 = (bf16[2,512,128]{2,1,0:T(8,128)(2,1)S(1)}, bf16[2,512,128]{2,1,0:T(8,128)(2,1)}, u32[]{:S(2)}) copy-start(bf16[2,512,128]{2,1,0:T(8,128)(2,1)} %ws_ref.3) | copy-start | bytes 786436
  21.4 0.9 %copy-start.4 = (bf16[2,128,384]{2,1,0:T(8,128)(2,1)S(1)}, bf16[2,128,384]{2,1,0:T(8,128)(2,1)}, u32[]{:S(2)}) copy-start(bf16[2,128,384]{2,1,0:T(8,128)(2,1)} %w_ref.3) | copy-start | bytes 589828
  22.3 0.9 %copy-start.5 = (bf16[64,16,128]{2,1,0:T(8,128)(2,1)S(1)}, bf16[64,16,128]{2,1,0:T(8,128)(2,1)}, u32[]{:S(2)}) copy-start(bf16[64,16,128]{2,1,0:T(8,128)(2,1)} %x_ref.1) | copy-start | bytes 786436
  23.3 17.5 %copy-start.1 = (bf16[2,128,512]{2,1,0:T(8,128)(2,1)S(1)}, bf16[2,128,512]{2,1,0:T(8,128)(2,1)}, u32[]{:S(2)}) copy-start(bf16[2,128,512]{2,1,0:T(8,128)(2,1)} %we_ref.3) | copy-start | bytes 786436
  23.3 17.5 %copy-start.3 = (bf16[2,512,128]{2,1,0:T(8,128)(2,1)S(1)}, bf16[2,512,128]{2,1,0:T(8,128)(2,1)}, u32[]{:S(2)}) copy-start(bf16[2,512,128]{2,1,0:T(8,128)(2,1)} %ws_ref.3) | copy-start | bytes 786436
  27.0 6.3 %collective-permute-start.2 = (bf16[320,128]{1,0:T(8,128)(2,1)S(1)}, bf16[320,128]{1,0:T(8,128)(2,1)S(1)}, u32[]{:S(2)}, u32[]{:S(2)}) collective-permute-start(bf16[320,128]{1,0:T(8,128)(2,1)S(1)} %get-tuple-element.15), channel_id=1, source_target_pairs={{0,1},{1,2},{2,3},{3,4},{4,5},{5,6},{6,7},{7,8},{8,9},{9,10},{10,1... | collective-permute-start | bytes 245768 | tf_op jit(solution)/shard_map/ppermute | solution.py:30
  30.9 9.9 %collective-permute-start.3 = (bf16[320,128]{1,0:T(8,128)(2,1)S(1)}, bf16[320,128]{1,0:T(8,128)(2,1)S(1)}, u32[]{:S(2)}, u32[]{:S(2)}) collective-permute-start(bf16[320,128]{1,0:T(8,128)(2,1)S(1)} %get-tuple-element.16), channel_id=1, source_target_pairs={{0,15},{1,0},{2,1},{3,2},{4,3},{5,4},{6,5},{7,6},{8,7},{9,8},{10,9... | collective-permute-start | bytes 245768 | tf_op jit(solution)/shard_map/ppermute | solution.py:30

commit v3 on v0

v3 whole, which is shorter than its diff:
```python
import math

import jax
import jax.numpy as jnp
from jax import lax
from jax.experimental import pallas as pl
from jax.experimental.pallas import tpu as pltpu
from jax.sharding import PartitionSpec as P

C = 128
HEADS = 4
HID = 512
WIN = 8
HD = 32
EPSILON = 1e-05
LOG2E = math.log2(math.e)
SCALE = HD ** (-0.5) * LOG2E
F32 = jnp.float32
BF16 = jnp.bfloat16
NT = (((1,), (1,)), ((), ()))
TN = (((0,), (0,)), ((), ()))
CHUNK = 256
EDGE_ROOM = 32 * 1024


def from_behind(x, axis, by):
    length = lax.axis_size(axis)
    return lax.ppermute(x, axis, [(i, (i + by) % length) for i in range(length)])


def iota(shape, dim):
    return lax.broadcasted_iota(jnp.int32, shape, dim)


def dot(a, b, dims=None):
    if dims is None:
        return jnp.dot(a, b, preferred_element_type=F32)
    return lax.dot_general(a, b, dims, preferred_element_type=F32)


def cat(parts, axis=0):
    return jnp.concatenate(parts, axis=axis)


def layer_norm(x, gain):
    center = x - jnp.mean(x, axis=-1, keepdims=True)
    spread = jnp.sum(center * center, axis=-1, keepdims=True)
    return center * lax.rsqrt(spread + C * EPSILON) * (gain * C**0.5)


def twice_gelu(x):
    return x + x * lax.erf(x * (0.5**0.5))


def bias_rows(pb_ref, block):
    sub = iota((8, 128), 0)
    lane = iota((8, 128), 1)
    place = lax.min((lane >> 3) * 15 + 7 + (lane & 7) - sub, 224)
    for head in range(HEADS):
        low = jnp.broadcast_to(pb_ref[block, head : head + 1, 0:128], (8, 128))
        high = jnp.broadcast_to(pb_ref[block, head : head + 1, 97:225], (8, 128))
        strip = jnp.where(
            place < 128,
            jnp.take_along_axis(low, lax.min(place, 127), axis=1),
            jnp.take_along_axis(high, lax.max(place - 97, 0), axis=1),
        )
        strip = strip * LOG2E
        for yj in range(8):
            turn = (128 - (7 - yj) * 8) % 128
            first = pltpu.roll(strip, turn, 1) if turn else strip
            second = pltpu.roll(strip, (turn + 64) % 128, 1)
            yield head, yj, jnp.where(lane < 64, first, second)


def fill_weights(w, wqv, wk):
    wqv[0:128, :] = jnp.transpose(w[:, 0:128].astype(F32)).astype(BF16)
    wqv[128:256, :] = jnp.transpose(w[:, 256:384].astype(F32)).astype(BF16)
    keys = w[:, 128:256].astype(F32)
    turned = pltpu.roll(keys, 64, 1)
    lane = iota((128, 128), 1)
    zero = jnp.zeros((128, 128), F32)
    wk[0:128, 0:128] = jnp.where(lane < 64, keys, zero).astype(BF16)
    wk[0:128, 128:256] = jnp.where(lane < 64, turned, zero).astype(BF16)
    wk[128:256, 0:128] = jnp.where(lane >= 64, turned, zero).astype(BF16)
    wk[128:256, 128:256] = jnp.where(lane >= 64, keys, zero).astype(BF16)


def mask(*conditions):
    lane = iota((64, 128), 1)
    sides = {"1": lane < 64, "2": lane >= 64, "up": (lane & 32) == 0, "down": (lane & 32) > 0}
    sides |= {"left": (lane & 4) == 0, "right": (lane & 4) > 0}
    keep = sides[conditions[0]]
    for name in conditions[1:]:
        keep = keep & sides[name]
    return jnp.where(keep, 1.0, 0.0).astype(BF16)


def side_by_side(tokens, wk):
    pairs = tokens.reshape(-1, 2, 64, 128)
    lanes = cat([cat([pairs[p, 0], pairs[p, 1]], 1) for p in range(pairs.shape[0])])
    return dot(lanes, wk).astype(BF16)


def attention(queries, keys, values, units):
    zero = jnp.zeros((32, 128), BF16)
    scores = []
    for u, (pairs, masks, bias) in enumerate(units):
        q = queries[:, 128 * u : 128 * u + 128]
        for half in range(2):
            r = 64 * half
            rows = []
            for m in masks:
                rows.append(cat([q[r : r + 32] * m[0:32], zero], 1))
                rows.append(cat([zero, q[r + 32 : r + 64] * m[0:32]], 1))
            k = cat([keys[64 * p : 64 * p + 64, 128 * half : 128 * half + 128] for p in pairs], 1)
            scores.append(dot(k, cat(rows)))
    for u, (pairs, masks, bias) in enumerate(units):
        for half in range(2):
            s = scores[2 * u + half] * SCALE + bias[:, 256 * half : 256 * half + 256]
            p = jnp.exp2(s - jnp.max(s, axis=0, keepdims=True))
            part = 1.0 / jnp.sum(p, axis=0, keepdims=True)
            scores[2 * u + half] = (p * part).astype(BF16)
    context = []
    for u, (pairs, masks, bias) in enumerate(units):
        out = []
        for half in range(2):
            r = 64 * half
            p = scores[2 * u + half]
            seen = cat([cat([p[:, 0:128] * m, p[:, 128:256] * m], 1) for m in masks])
            v = cat([values[r : r + 64, 128 * j : 128 * j + 128] for j in pairs], 1)
            ct = dot(v, seen)
            out += [ct[0:32, 0:128], ct[32:64, 128:256]]
        context.append(cat(out).astype(BF16))
    return cat(context, 1)


def finish(z, context, wo, gain, we, ws):
    middle = z + dot(context, wo, TN).astype(BF16).astype(F32)
    normed = layer_norm(middle, gain).astype(BF16)
    size = min(CHUNK, z.shape[0])
    hidden = [dot(normed[i : i + size], we) for i in range(0, z.shape[0], size)]
    hidden = [twice_gelu(h).astype(BF16) for h in hidden]
    return middle + 0.5 * cat([dot(h, ws) for h in hidden])


def half_turn(x):
    return pltpu.roll(x.reshape(-1, 8, 128), 4, 1)


def low_half(shape):
    return iota(shape, 1) < 4


def windows_of(block):
    parts = block.astype(F32).reshape(8, 2, 8, 128)
    return [parts[:, 0].reshape(64, 128), parts[:, 1].reshape(64, 128)]


def shifted_columns(tokens):
    pairs = tokens.reshape(-1, 2, 64, 128)
    a, b = half_turn(pairs[:, 0]), half_turn(pairs[:, 1])
    low = low_half(a.shape)
    return jnp.where(low, a, b).reshape(-1, 128), jnp.where(low, b, a).reshape(-1, 128)


def edges(outer):
    pairs = outer.reshape(-1, 2, 8, 128)
    even, odd = pairs[:, 0], pairs[:, 1]
    low = low_half(even.shape)
    right = jnp.where(low, even, pltpu.roll(odd, 4, 1)).reshape(-1, 128)
    left = jnp.where(low, pltpu.roll(even, 4, 1), odd).reshape(-1, 128)
    return right.astype(BF16), left.astype(BF16)


def edge_rows_kernel(x_ref, first_ref, last_ref, sems):
    height = x_ref.shape[0]
    copies = [
        pltpu.make_async_copy(x_ref.at[pl.ds(0, WIN)], first_ref, sems.at[0]),
        pltpu.make_async_copy(x_ref.at[pl.ds(height - WIN, WIN)], last_ref, sems.at[1]),
    ]
    for copy in copies:
        copy.start()
    for copy in copies:
        copy.wait()


def own_kernel(
    x_hbm, w_hbm, wo_hbm, we_hbm, ws_hbm, ag_ref, pb_ref, hg_ref,
    fa_ref, fb_ref, na_ref, nb_ref, right_ref, left_ref, bias_ref, wqv_ref, wk_ref, w_ref, wo_ref, we_ref, ws_ref,
    x_ref, sems,
):
    copies = [
        pltpu.make_async_copy(a, b, sems.at[i])
        for i, (a, b) in enumerate(
            [(w_hbm, w_ref), (x_hbm, x_ref), (wo_hbm, wo_ref), (we_hbm, we_ref), (ws_hbm, ws_ref)]
        )
    ]
    for copy in copies:
        copy.start()
    for head, yj, values in bias_rows(pb_ref, 0):
        bias_ref[yj * 8 : yj * 8 + 8, head * 128 : head * 128 + 128] = values
    copies[0].wait()
    fill_weights(w_ref[0], wqv_ref, wk_ref)
    copies[1].wait()
    bands = x_ref.shape[0] // WIN
    z = cat([t for b in range(bands) for t in windows_of(x_ref[WIN * b : WIN * b + WIN])])
    normed = layer_norm(z, ag_ref[0:1, :]).astype(BF16)
    qv = dot(wqv_ref[...], normed, NT).astype(BF16)
    keys = side_by_side(normed, wk_ref[...])
    masks = [mask("1"), mask("2")]
    units = [([b], masks, bias_ref[...]) for b in range(bands)]
    context = attention(qv[0:128], keys, qv[128:256], units)
    for copy in copies[2:]:
        copy.wait()
    out = finish(z, context, wo_ref[0], hg_ref[0:1, :], we_ref[0], ws_ref[0])
    fa_ref[...], fb_ref[...] = shifted_columns(out)
    na, nb = shifted_columns(layer_norm(out, ag_ref[1:2, :]))
    na_ref[...] = na.astype(BF16)
    nb_ref[...] = nb.astype(BF16)
    right_ref[...], left_ref[...] = edges(nb)


def halo_kernel(
    up_ref, down_ref, own_right_ref, own_left_ref, bias_ref, wqv_ref, wk_ref, wo_ref, we_ref, ws_ref, ag_ref, hg_ref,
    na_ref, nb_ref, right_ref, left_ref,
):
    z = cat(windows_of(down_ref[...]) + windows_of(up_ref[...]))
    normed = layer_norm(z, ag_ref[0:1, :]).astype(BF16)
    keys = side_by_side(normed, wk_ref[...])
    values = dot(wqv_ref[128:256, :], normed, NT).astype(BF16)

    def wanted(t):
        return cat([t[0:32], t[160:192], t[64:96], t[224:256]])

    queries = dot(wqv_ref[0:128, :], wanted(normed), NT).astype(BF16)
    masks = [mask("1", "up"), mask("2", "up"), mask("1", "down"), mask("2", "down")]
    context = attention(queries, keys, values, [([0, 1], masks, bias_ref[...])])
    out = finish(wanted(z), context, wo_ref[0], hg_ref[0:1, :], we_ref[0], ws_ref[0])
    na, nb = shifted_columns(layer_norm(out, ag_ref[1:2, :]))
    na_ref[...] = na.astype(BF16)
    nb_ref[...] = nb.astype(BF16)
    right, left = edges(nb)
    n = own_right_ref.shape[0]
    right_ref[0:n, :] = own_right_ref[...]
    left_ref[0:n, :] = own_left_ref[...]
    right_ref[n : n + 32, :] = right
    left_ref[n : n + 32, :] = left


def middle_kernel(
    flag_ref, fa_ref, na_ref, va_ref, pb_ref, w_ref, wo_ref, we_ref, ws_ref, hg_ref,
    out_ref, bias_b, bias_bv, wqv_ref, wk_ref,
    bias_a, bias_av,
):
    sub = iota((8, 128), 0)
    lane = iota((8, 128), 1)
    query_left = (lane & 4) == 0
    query_up = (lane & 32) == 0
    last_col = jnp.where(query_left, flag_ref[3], flag_ref[2]) > 0
    last_row = jnp.where(query_up, flag_ref[1], flag_ref[0]) > 0
    cut_col = last_col & (query_left != (sub < 4))
    for head, yj, values in bias_rows(pb_ref, 1):
        at = (slice(yj * 8, yj * 8 + 8), slice(head * 128, head * 128 + 128))
        cut = values - 100.0 * LOG2E
        cut_row = (lane >= 64) & last_row & (jnp.logical_not(query_up) if yj < 4 else query_up)
        bias_a[at] = values
        bias_av[at] = jnp.where(cut_row, cut, values)
        bias_b[at] = jnp.where(cut_col, cut, values)
        bias_bv[at] = jnp.where(cut_row | cut_col, cut, values)
    fill_weights(w_ref[1], wqv_ref, wk_ref)
    n = na_ref.shape[0]
    inner = na_ref[32 : n - 32, :]
    first = cat([va_ref[32:64, :], na_ref[0:32, :]])
    last = cat([na_ref[n - 32 : n, :], va_ref[0:32, :]])
    looked_at = cat([inner, last, first, first])
    keys = side_by_side(looked_at, wk_ref[...])
    values = dot(wqv_ref[128:256, :], looked_at, NT).astype(BF16)
    wanted = cat([na_ref[32:n, :], na_ref[0:32, :]])
    queries = dot(wqv_ref[0:128, :], wanted, NT).astype(BF16)
    last_unit = n // 128 - 1
    masks = [mask("1"), mask("2")]
    units = [([u], masks, bias_a[...]) for u in range(last_unit)]
    masks = [mask("1"), mask("2", "up"), mask("2", "down"), jnp.zeros((64, 128), BF16)]
    units.append(([last_unit, last_unit + 1], masks, bias_av[...]))
    context = attention(queries, keys, values, units)
    z = cat([fa_ref[32:n, :], fa_ref[0:32, :]])
    out = finish(z, context, wo_ref[1], hg_ref[1:2, :], we_ref[1], ws_ref[1])
    out = half_turn(out).reshape(n, 128)
    out_ref[32:n, :] = out[0 : n - 32]
    out_ref[0:32, :] = out[n - 32 : n]


def outer_kernel(
    fb_ref, nb_ref, vb_ref, hl_ref, hr_ref, oa_ref, bias_b, bias_bv, wqv_ref, wk_ref, wo_ref, we_ref, ws_ref, hg_ref,
    out_ref,
):
    n = nb_ref.shape[0]
    h = n // 2

    def in_order(ref, end, size):
        rows = cat([ref[end + size : end + 2 * size, :], ref[0:end, :], ref[end : end + size, :]])
        return rows.astype(F32).reshape(-1, 8, 128)

    own = cat([vb_ref[32:64, :], nb_ref[...], vb_ref[0:32, :]]).astype(F32).reshape(-1, 8, 128)
    hl, hr = in_order(hl_ref, h, 16), in_order(hr_ref, h, 16)
    low = low_half(hl.shape)
    even = jnp.where(low, hl, pltpu.roll(hr, 4, 1))
    odd = jnp.where(low, pltpu.roll(hl, 4, 1), hr)
    halo = jnp.stack([even, odd], axis=1).reshape(own.shape)
    low = low_half(own.shape)
    right = jnp.where(low, own, halo).reshape(-1, 64, 128).astype(BF16)
    left = jnp.where(low, halo, own).reshape(-1, 64, 128).astype(BF16)
    count = right.shape[0]
    looked_at = cat([t for w in range(count) for t in (right[w], left[w])])
    keys = side_by_side(looked_at, wk_ref[...])
    values = dot(wqv_ref[128:256, :], looked_at, NT).astype(BF16)
    wanted = cat([nb_ref[32:n, :], nb_ref[0:32, :]])
    queries = dot(wqv_ref[0:128, :], wanted, NT).astype(BF16)
    masks = [mask(w, s) for w in "12" for s in ("left", "right")]
    units = [([w, w + 1], masks, bias_b[...]) for w in range(1, count - 2, 2)]
    masks = masks[0:2] + [mask("2", v, s) for v in ("up", "down") for s in ("left", "right")]
    units.append(([count - 2, count - 1, 0], masks, bias_bv[...]))
    context = attention(queries, keys, values, units)
    z = cat([fb_ref[32:n, :], fb_ref[0:32, :]])
    out = finish(z, context, wo_ref[1], hg_ref[1:2, :], we_ref[1], ws_ref[1])
    out = half_turn(out)
    rows = n // 8
    out = cat([out[rows - 4 :], out[: rows - 4]])
    inner = oa_ref[...].reshape(rows, 8, 128)
    low = low_half(out.shape)
    out_ref[:, 0:8, :] = jnp.where(low, out, inner)
    out_ref[:, 8:16, :] = jnp.where(low, inner, out)


def vmem(count):
    return [pl.BlockSpec(memory_space=pltpu.VMEM)] * count


def call(kernel, name, operands, specs, outs, scratch=(), flops=0, room=32 * 1024):
    shapes = [jax.ShapeDtypeStruct(shape, dtype) for shape, dtype in outs]
    return pl.pallas_call(
        kernel,
        out_shape=shapes,
        in_specs=specs,
        out_specs=vmem(len(outs)),
        scratch_shapes=list(scratch),
        compiler_params=pltpu.CompilerParams(vmem_limit_bytes=room * 1024),
        cost_estimate=pl.CostEstimate(flops=flops, bytes_accessed=1 << 20, transcendentals=0),
        name=name,
    )(*operands)


def on_device(x, ag, tw, ow, pb, hg, ew, sw):
    height, breadth = x.shape[0], x.shape[1]
    n = height * WIN
    hbm = [pl.BlockSpec(memory_space=pltpu.HBM)]
    first, last = call(
        edge_rows_kernel, "edge_rows", (x,), hbm,
        [((WIN, breadth, C), BF16)] * 2, [pltpu.SemaphoreType.DMA((2,))], 4 * 10**10, EDGE_ROOM,
    )
    up = from_behind(last, "gy", 1)
    down = from_behind(first, "gy", -1)
    table = ((64, HEADS * 128), F32)
    prepared = [((256, 128), BF16), ((256, 256), BF16)]
    fa, fb, na, nb, right, left, bias, wqv, wk, w, wo, we, ws = call(
        own_kernel, "own", (x, tw, ow, ew, sw, ag, pb, hg), hbm * 5 + vmem(3),
        [((n, C), F32)] * 2 + [((n, C), BF16)] * 2 + [((n // 2, C), BF16)] * 2 + [table] + prepared
        + [(tw.shape, BF16), (ow.shape, BF16), (ew.shape, BF16), (sw.shape, BF16)],
        [pltpu.VMEM(x.shape, BF16), pltpu.SemaphoreType.DMA((5,))], 4 * 10**9,
    )
    va, vb, right, left = call(
        halo_kernel, "halo", (up, down, right, left, bias, wqv, wk, wo, we, ws, ag, hg), vmem(12),
        [((64, C), BF16)] * 2 + [((n // 2 + 32, C), BF16)] * 2, (), 10**9,
    )
    hr = from_behind(left, "gx", -1)
    hl = from_behind(right, "gx", 1)
    row, col = lax.axis_index("gy"), lax.axis_index("gx")
    flags = jnp.stack(
        [row == 0, row == lax.axis_size("gy") - 1, col == 0, col == lax.axis_size("gx") - 1]
    ).astype(jnp.int32)
    oa, bias_b, bias_bv, wqv, wk = call(
        middle_kernel, "middle", (flags, fa, na, va, pb, w, wo, we, ws, hg),
        [pl.BlockSpec(memory_space=pltpu.SMEM)] + vmem(9),
        [((n, C), F32), table, table] + prepared,
        [pltpu.VMEM(*table)] * 2, 2 * 10**9,
    )
    return call(
        outer_kernel, "outer", (fb, nb, vb, hl, hr, oa, bias_b, bias_bv, wqv, wk, wo, we, ws, hg), vmem(14),
        [((height, breadth, C), F32)], (), 2 * 10**9,
    )[0]


def solution(mesh):
    return jax.shard_map(
        on_device,
        mesh=mesh,
        in_specs=(P("gy", "gx", None), P(), P(), P(), P(), P(), P(), P()),
        out_specs=P("gy", "gx", None),
        check_vma=False,
    )
```

time: 99.2 us -> 37 us (0.37)
  the two profiles are of different devices: /device:TPU:2 before, /device:TPU:56 now
where the time goes in v3:
time: 37 us; the launch traced here: 36.7 us
  starting transfers between devices  19.2 us (52%)
  Pallas kernels  10.1 us (27%)
  waiting for transfers between devices  5.59 us (15%)
  local copies, waits for them, and re-layouts  1.59 us (4%)
    ppermute x4, starting transfers between devices, from_behind(): lax.ppermute(x, axis, [(i, (i + by) % length) for i in range(length)])  19.2 us
    pallas_call x5, Pallas kernels, call(): pl.pallas_call(kernel, out_shape=shapes, in_specs=specs, out_specs=vmem(l...  10.1 us
    ppermute x4, waiting for transfers between devices, from_behind(): lax.ppermute(x, axis, [(i, (i + by) % length) for i in range(length)])  5.59 us
    unnamed x18, local copies, waits for them, and re-layouts  1.59 us
  transfers between devices with their start and end apart: 4, of which 1 were waited for; matrix products, arithmetic and copies ran while one was open for 0% of the time, Pallas kernels for 16%

profile of v3, /device:TPU:56, one launch (start us, length us, event | category | flops | bytes accessed | tf_op | source)
XLA Modules:
  0.0 36.7 jit_solution(7231323689062858989)
XLA Ops:
  0.0 0.0 copy-start
  0.0 0.9 %copy-done = bf16[64,16,128]{2,1,0:T(8,128)(2,1)S(1)} copy-done((bf16[64,16,128]{2,1,0:T(8,128)(2,1)S(1)}, bf16[64,16,128]{2,1,0:T(8,128)(2,1)}, u32[]{:S(2)}) %copy-start) | copy-done | bytes 262168
  1.0 0.0 copy-start.1
  1.0 0.0 copy-start.2
  1.0 0.0 copy-start.3
  1.0 0.0 copy-start.4
  1.0 0.0 copy-start.5
  1.0 0.0 copy-start.8
  1.0 0.1 edge_rows.1
  1.1 2.1 %collective-permute-start = (bf16[8,16,128]{2,1,0:T(8,128)(2,1)S(1)}, bf16[8,16,128]{2,1,0:T(8,128)(2,1)S(1)}, u32[]{:S(2)}, u32[]{:S(2)}) collective-permute-start(bf16[8,16,128]{2,1,0:T(8,128)(2,1)S(1)} %get-tuple-element.31), channel_id=1, source_target_pairs={{0,16},{16,32},{32,48},{48,64},{64,80},{80,96},{96,112},{112,128},... | collective-permute-start | bytes 98312 | tf_op jit(solution)/shard_map/ppermute | solution.py:28
  3.2 11.3 %collective-permute-start.1 = (bf16[8,16,128]{2,1,0:T(8,128)(2,1)S(1)}, bf16[8,16,128]{2,1,0:T(8,128)(2,1)S(1)}, u32[]{:S(2)}, u32[]{:S(2)}) collective-permute-start(bf16[8,16,128]{2,1,0:T(8,128)(2,1)S(1)} %get-tuple-element.32), channel_id=1, source_target_pairs={{0,496},{16,0},{32,16},{48,32},{64,48},{80,64},{96,80},{112,96},{1... | collective-permute-start | bytes 98312 | tf_op jit(solution)/shard_map/ppermute | solution.py:28
  14.5 0.0 copy-start.6
  14.5 0.0 copy-start.7
  14.5 0.0 copy-done.1
  14.5 0.0 copy-done.2
  14.5 0.0 copy-done.3
  14.5 0.0 copy-done.4
  14.6 0.0 copy-done.5
  14.6 0.0 copy-done.8
  14.6 0.6 %copy-done.6 = f32[2,4,225]{2,1,0:T(4,128)S(1)} copy-done((f32[2,4,225]{2,1,0:T(4,128)S(1)}, f32[2,4,225]{2,1,0:T(4,128)}, u32[]{:S(2)}) %copy-start.6) | copy-done | bytes 7224
  15.2 0.0 copy-done.7
  15.2 3.7 %own.1 = (f32[512,128]{1,0:T(8,128)S(1)}, f32[512,128]{1,0:T(8,128)S(1)}, bf16[512,128]{1,0:T(8,128)(2,1)S(1)}, bf16[512,128]{1,0:T(8,128)(2,1)S(1)}, bf16[256,1...) custom-call(bf16[64,16,128]{2,1,0:T(8,128)(2,1)S(1)} %copy-done.1, ...), custom_call_target="tpu_custom_call" | custom-call | flops 4000000000 | bytes 1048576 | tf_op jit(solution)/shard_map/own/pallas_call | solution.py:341
  18.9 0.1 add_convert_fusion.flag_ref
  19.0 0.0 collective-permute-done.up_ref
  19.0 0.0 collective-permute-done.1.down_ref
  19.0 1.5 %halo.1 = (bf16[64,128]{1,0:T(8,128)(2,1)S(1)}, bf16[64,128]{1,0:T(8,128)(2,1)S(1)}, bf16[288,128]{1,0:T(8,128)(2,1)S(1)}, bf16[288,128]{1,0:T(8,128)(2,1)S(1)}) custom-call(bf16[8,16,128]{2,1,0:T(8,128)(2,1)S(1)} %collective-permute-done.up_ref, bf16[8,16,128]{2,1,0:T(8,128)(2,1)S(1)} %collective-permute-done.1.down_ref, ...), custom_call_target="tpu_custom_call" | custom-call | flops 1000000000 | bytes 1048576 | tf_op jit(solution)/shard_map/halo/pallas_call | solution.py:341
  20.5 3.8 %collective-permute-start.2 = (bf16[288,128]{1,0:T(8,128)(2,1)S(1)}, bf16[288,128]{1,0:T(8,128)(2,1)S(1)}, u32[]{:S(2)}, u32[]{:S(2)}) collective-permute-start(bf16[288,128]{1,0:T(8,128)(2,1)S(1)} %get-tuple-element.42), channel_id=1, source_target_pairs={{0,1},{1,2},{2,3},{3,4},{4,5},{5,6},{6,7},{7,8},{8,9},{9,10},{10,1... | collective-permute-start | bytes 221192 | tf_op jit(solution)/shard_map/ppermute | solution.py:28
  24.4 2.0 %collective-permute-start.3 = (bf16[288,128]{1,0:T(8,128)(2,1)S(1)}, bf16[288,128]{1,0:T(8,128)(2,1)S(1)}, u32[]{:S(2)}, u32[]{:S(2)}) collective-permute-start(bf16[288,128]{1,0:T(8,128)(2,1)S(1)} %get-tuple-element.43), channel_id=1, source_target_pairs={{0,15},{1,0},{2,1},{3,2},{4,3},{5,4},{6,5},{7,6},{8,7},{9,8},{10,9... | collective-permute-start | bytes 221192 | tf_op jit(solution)/shard_map/ppermute | solution.py:28
  26.4 2.3 %middle.1 = (f32[512,128]{1,0:T(8,128)S(1)}, f32[64,512]{1,0:T(8,128)S(1)}, f32[64,512]{1,0:T(8,128)S(1)}, bf16[256,128]{1,0:T(8,128)(2,1)S(1)}, bf16[256,256]{1,0:T(8,128)(2,1)S(1)}) custom-call(s32[4]{0:T(128)S(1)} %add_convert_fusion.flag_ref, f32[512,128]{1,0:T(8,128)S(1)} %get-tuple-element.44.fa_ref, bf16[512,128]{1,0:T(8,128)(2,1)S(1)} %get-tuple-element.45.na_ref, ...), custom_call_target="tpu_custom_call" | custom-call | flops 2000000000 | bytes 1048576 | tf_op jit(solution)/shard_map/middle/pallas_call | solution.py:341
  28.7 0.0 collective-permute-done.2.hl_ref
  28.7 5.6 %collective-permute-done.3.hr_ref = bf16[288,128]{1,0:T(8,128)(2,1)S(1)} collective-permute-done((bf16[288,128]{1,0:T(8,128)(2,1)S(1)}, bf16[288,128]{1,0:T(8,128)(2,1)S(1)}, u32[]{:S(2)}, u32[]{:S(2)}) %collective-permute-start.3) | collective-permute-done | bytes 73760 | tf_op jit(solution)/shard_map/ppermute | solution.py:28
  34.3 2.5 %outer.1 = f32[64,16,128]{2,1,0:T(8,128)} custom-call(f32[512,128]{1,0:T(8,128)S(1)} %get-tuple-element.29.fb_ref, bf16[512,128]{1,0:T(8,128)(2,1)S(1)} %get-tuple-element.30.nb_ref, bf16[64,128]{1,0:T(8,128)(2,1)S(1)} %get-tuple-element.41.vb_ref, bf16[288,128]{1,0:T(8,128)(2,1)S(1)} %collective-permute-done.2.hl_ref, ...), custom_call_target="tpu_custom_call" | custom-call | flops 2000000000 | bytes 1048576 | tf_op jit(solution)/shard_map/outer/pallas_call | solution.py:341
Async XLA Ops:
  0.0 0.9 %copy-start = (bf16[64,16,128]{2,1,0:T(8,128)(2,1)S(1)}, bf16[64,16,128]{2,1,0:T(8,128)(2,1)}, u32[]{:S(2)}) copy-start(bf16[64,16,128]{2,1,0:T(8,128)(2,1)} %x_ref.1) | copy-start | bytes 786436
  1.0 13.6 %copy-start.1 = (bf16[64,16,128]{2,1,0:T(8,128)(2,1)S(1)}, bf16[64,16,128]{2,1,0:T(8,128)(2,1)}, u32[]{:S(2)}) copy-start(bf16[64,16,128]{2,1,0:T(8,128)(2,1)} %x_ref.1) | copy-start | bytes 786436
  1.0 13.6 %copy-start.2 = (bf16[2,128,512]{2,1,0:T(8,128)(2,1)S(1)}, bf16[2,128,512]{2,1,0:T(8,128)(2,1)}, u32[]{:S(2)}) copy-start(bf16[2,128,512]{2,1,0:T(8,128)(2,1)} %we_hbm.1) | copy-start | bytes 786436
  1.0 13.6 %copy-start.3 = (bf16[2,512,128]{2,1,0:T(8,128)(2,1)S(1)}, bf16[2,512,128]{2,1,0:T(8,128)(2,1)}, u32[]{:S(2)}) copy-start(bf16[2,512,128]{2,1,0:T(8,128)(2,1)} %ws_hbm.1) | copy-start | bytes 786436
  1.0 13.6 %copy-start.4 = (bf16[2,128,384]{2,1,0:T(8,128)(2,1)S(1)}, bf16[2,128,384]{2,1,0:T(8,128)(2,1)}, u32[]{:S(2)}) copy-start(bf16[2,128,384]{2,1,0:T(8,128)(2,1)} %w_hbm.1) | copy-start | bytes 589828
  1.0 13.6 %copy-start.5 = (bf16[2,128,128]{2,1,0:T(8,128)(2,1)S(1)}, bf16[2,128,128]{2,1,0:T(8,128)(2,1)}, u32[]{:S(2)}) copy-start(bf16[2,128,128]{2,1,0:T(8,128)(2,1)} %wo_hbm.1) | copy-start | bytes 196612
  1.0 13.6 %copy-start.8 = (f32[2,128]{1,0:T(2,128)S(1)}, f32[2,128]{1,0:T(2,128)}, u32[]{:S(2)}) copy-start(f32[2,128]{1,0:T(2,128)} %hg_ref.7) | copy-start | bytes 3076
  1.1 17.9 %collective-permute-start = (bf16[8,16,128]{2,1,0:T(8,128)(2,1)S(1)}, bf16[8,16,128]{2,1,0:T(8,128)(2,1)S(1)}, u32[]{:S(2)}, u32[]{:S(2)}) collective-permute-start(bf16[8,16,128]{2,1,0:T(8,128)(2,1)S(1)} %get-tuple-element.31), channel_id=1, source_target_pairs={{0,16},{16,32},{32,48},{48,64},{64,80},{80,96},{96,112},{112,128},... | collective-permute-start | bytes 98312 | tf_op jit(solution)/shard_map/ppermute | solution.py:28
  3.2 15.9 %collective-permute-start.1 = (bf16[8,16,128]{2,1,0:T(8,128)(2,1)S(1)}, bf16[8,16,128]{2,1,0:T(8,128)(2,1)S(1)}, u32[]{:S(2)}, u32[]{:S(2)}) collective-permute-start(bf16[8,16,128]{2,1,0:T(8,128)(2,1)S(1)} %get-tuple-element.32), channel_id=1, source_target_pairs={{0,496},{16,0},{32,16},{48,32},{64,48},{80,64},{96,80},{112,96},{1... | collective-permute-start | bytes 98312 | tf_op jit(solution)/shard_map/ppermute | solution.py:28
  14.5 0.7 %copy-start.6 = (f32[2,4,225]{2,1,0:T(4,128)S(1)}, f32[2,4,225]{2,1,0:T(4,128)}, u32[]{:S(2)}) copy-start(f32[2,4,225]{2,1,0:T(4,128)} %pb_ref.3) | copy-start | bytes 21604
  14.5 0.7 %copy-start.7 = (f32[2,128]{1,0:T(2,128)S(1)}, f32[2,128]{1,0:T(2,128)}, u32[]{:S(2)}) copy-start(f32[2,128]{1,0:T(2,128)} %ag_ref.3) | copy-start | bytes 3076
  20.5 8.1 %collective-permute-start.2 = (bf16[288,128]{1,0:T(8,128)(2,1)S(1)}, bf16[288,128]{1,0:T(8,128)(2,1)S(1)}, u32[]{:S(2)}, u32[]{:S(2)}) collective-permute-start(bf16[288,128]{1,0:T(8,128)(2,1)S(1)} %get-tuple-element.42), channel_id=1, source_target_pairs={{0,1},{1,2},{2,3},{3,4},{4,5},{5,6},{6,7},{7,8},{8,9},{9,10},{10,1... | collective-permute-start | bytes 221192 | tf_op jit(solution)/shard_map/ppermute | solution.py:28
  24.4 9.9 %collective-permute-start.3 = (bf16[288,128]{1,0:T(8,128)(2,1)S(1)}, bf16[288,128]{1,0:T(8,128)(2,1)S(1)}, u32[]{:S(2)}, u32[]{:S(2)}) collective-permute-start(bf16[288,128]{1,0:T(8,128)(2,1)S(1)} %get-tuple-element.43), channel_id=1, source_target_pairs={{0,15},{1,0},{2,1},{3,2},{4,3},{5,4},{6,5},{7,6},{8,7},{9,8},{10,9... | collective-permute-start | bytes 221192 | tf_op jit(solution)/shard_map/ppermute | solution.py:28

commit v4 on v3

--- a/solution.py
+++ b/solution.py
@@ -20,12 +20,12 @@
 NT = (((1,), (1,)), ((), ()))
 TN = (((0,), (0,)), ((), ()))
 CHUNK = 256
-EDGE_ROOM = 32 * 1024
-
-
-def from_behind(x, axis, by):
+
+
+def swap(x, axis, first):
     length = lax.axis_size(axis)
-    return lax.ppermute(x, axis, [(i, (i + by) % length) for i in range(length)])
+    there = [(i, (i + 1) % length) for i in range(first, length, 2)]
+    return lax.ppermute(x, axis, there + [(b, a) for a, b in there])
 
 
 def iota(shape, dim):
@@ -172,11 +172,12 @@
     return right.astype(BF16), left.astype(BF16)
 
 
-def edge_rows_kernel(x_ref, first_ref, last_ref, sems):
-    height = x_ref.shape[0]
+def edge_rows_kernel(x_ref, odd_ref, even_ref, sems):
+    bottom = x_ref.shape[0] - WIN
+    is_odd = lax.rem(lax.axis_index("gy"), 2)
     copies = [
-        pltpu.make_async_copy(x_ref.at[pl.ds(0, WIN)], first_ref, sems.at[0]),
-        pltpu.make_async_copy(x_ref.at[pl.ds(height - WIN, WIN)], last_ref, sems.at[1]),
+        pltpu.make_async_copy(x_ref.at[pl.ds(is_odd * bottom, WIN)], odd_ref, sems.at[0]),
+        pltpu.make_async_copy(x_ref.at[pl.ds((1 - is_odd) * bottom, WIN)], even_ref, sems.at[1]),
     ]
     for copy in copies:
         copy.start()
@@ -221,10 +222,14 @@
 
 
 def halo_kernel(
-    up_ref, down_ref, own_right_ref, own_left_ref, bias_ref, wqv_ref, wk_ref, wo_ref, we_ref, ws_ref, ag_ref, hg_ref,
-    na_ref, nb_ref, right_ref, left_ref,
+    rows_odd_ref, rows_even_ref, own_right_ref, own_left_ref, bias_ref, wqv_ref, wk_ref, wo_ref, we_ref, ws_ref, ag_ref, hg_ref,
+    na_ref, nb_ref, cols_odd_ref, cols_even_ref,
 ):
-    z = cat(windows_of(down_ref[...]) + windows_of(up_ref[...]))
+    row_odd = lax.rem(lax.axis_index("gy"), 2) == 1
+    rows_odd, rows_even = rows_odd_ref[...].astype(F32), rows_even_ref[...].astype(F32)
+    down = jnp.where(row_odd, rows_odd, rows_even)
+    up = jnp.where(row_odd, rows_even, rows_odd)
+    z = cat(windows_of(down) + windows_of(up))
     normed = layer_norm(z, ag_ref[0:1, :]).astype(BF16)
     keys = side_by_side(normed, wk_ref[...])
     values = dot(wqv_ref[128:256, :], normed, NT).astype(BF16)
@@ -241,14 +246,15 @@
     nb_ref[...] = nb.astype(BF16)
     right, left = edges(nb)
     n = own_right_ref.shape[0]
-    right_ref[0:n, :] = own_right_ref[...]
-    left_ref[0:n, :] = own_left_ref[...]
-    right_ref[n : n + 32, :] = right
-    left_ref[n : n + 32, :] = left
+    col_odd = lax.rem(lax.axis_index("gx"), 2) == 1
+    for at, size, a, b in [(0, n, own_right_ref[...], own_left_ref[...]), (n, 32, right, left)]:
+        a, b = a.astype(F32), b.astype(F32)
+        cols_odd_ref[at : at + size, :] = jnp.where(col_odd, a, b).astype(BF16)
+        cols_even_ref[at : at + size, :] = jnp.where(col_odd, b, a).astype(BF16)
 
 
 def middle_kernel(
-    flag_ref, fa_ref, na_ref, va_ref, pb_ref, w_ref, wo_ref, we_ref, ws_ref, hg_ref,
+    fa_ref, na_ref, va_ref, pb_ref, w_ref, wo_ref, we_ref, ws_ref, hg_ref,
     out_ref, bias_b, bias_bv, wqv_ref, wk_ref,
     bias_a, bias_av,
 ):
@@ -256,8 +262,9 @@
     lane = iota((8, 128), 1)
     query_left = (lane & 4) == 0
     query_up = (lane & 32) == 0
-    last_col = jnp.where(query_left, flag_ref[3], flag_ref[2]) > 0
-    last_row = jnp.where(query_up, flag_ref[1], flag_ref[0]) > 0
+    row, col = lax.axis_index("gy"), lax.axis_index("gx")
+    last_col = jnp.where(query_left, lax.axis_size("gx") - 1, 0) == col
+    last_row = jnp.where(query_up, lax.axis_size("gy") - 1, 0) == row
     cut_col = last_col & (query_left != (sub < 4))
     for head, yj, values in bias_rows(pb_ref, 1):
         at = (slice(yj * 8, yj * 8 + 8), slice(head * 128, head * 128 + 128))
@@ -291,7 +298,7 @@
 
 
 def outer_kernel(
-    fb_ref, nb_ref, vb_ref, hl_ref, hr_ref, oa_ref, bias_b, bias_bv, wqv_ref, wk_ref, wo_ref, we_ref, ws_ref, hg_ref,
+    fb_ref, nb_ref, vb_ref, cols_odd_ref, cols_even_ref, oa_ref, bias_b, bias_bv, wqv_ref, wk_ref, wo_ref, we_ref, ws_ref, hg_ref,
     out_ref,
 ):
     n = nb_ref.shape[0]
@@ -302,7 +309,9 @@
         return rows.astype(F32).reshape(-1, 8, 128)
 
     own = cat([vb_ref[32:64, :], nb_ref[...], vb_ref[0:32, :]]).astype(F32).reshape(-1, 8, 128)
-    hl, hr = in_order(hl_ref, h, 16), in_order(hr_ref, h, 16)
+    odd, even = in_order(cols_odd_ref, h, 16), in_order(cols_even_ref, h, 16)
+    col_odd = lax.rem(lax.axis_index("gx"), 2) == 1
+    hl, hr = jnp.where(col_odd, even, odd), jnp.where(col_odd, odd, even)
     low = low_half(hl.shape)
     even = jnp.where(low, hl, pltpu.roll(hr, 4, 1))
     odd = jnp.where(low, pltpu.roll(hl, 4, 1), hr)
@@ -336,7 +345,7 @@
     return [pl.BlockSpec(memory_space=pltpu.VMEM)] * count
 
 
-def call(kernel, name, operands, specs, outs, scratch=(), flops=0, room=32 * 1024):
+def call(kernel, name, operands, specs, outs, scratch=(), flops=0):
     shapes = [jax.ShapeDtypeStruct(shape, dtype) for shape, dtype in outs]
     return pl.pallas_call(
         kernel,
@@ -344,7 +353,7 @@
         in_specs=specs,
         out_specs=vmem(len(outs)),
         scratch_shapes=list(scratch),
-        compiler_params=pltpu.CompilerParams(vmem_limit_bytes=room * 1024),
+        compiler_params=pltpu.CompilerParams(vmem_limit_bytes=32 * 1024 * 1024),
         cost_estimate=pl.CostEstimate(flops=flops, bytes_accessed=1 << 20, transcendentals=0),
         name=name,
     )(*operands)
@@ -354,12 +363,11 @@
     height, breadth = x.shape[0], x.shape[1]
     n = height * WIN
     hbm = [pl.BlockSpec(memory_space=pltpu.HBM)]
-    first, last = call(
+    odd, even = call(
         edge_rows_kernel, "edge_rows", (x,), hbm,
-        [((WIN, breadth, C), BF16)] * 2, [pltpu.SemaphoreType.DMA((2,))], 4 * 10**10, EDGE_ROOM,
+        [((WIN, breadth, C), BF16)] * 2, [pltpu.SemaphoreType.DMA((2,))], 4 * 10**10,
     )
-    up = from_behind(last, "gy", 1)
-    down = from_behind(first, "gy", -1)
+    odd, even = swap(odd, "gy", 1), swap(even, "gy", 0)
     table = ((64, HEADS * 128), F32)
     prepared = [((256, 128), BF16), ((256, 256), BF16)]
     fa, fb, na, nb, right, left, bias, wqv, wk, w, wo, we, ws = call(
@@ -368,24 +376,19 @@
         + [(tw.shape, BF16), (ow.shape, BF16), (ew.shape, BF16), (sw.shape, BF16)],
         [pltpu.VMEM(x.shape, BF16), pltpu.SemaphoreType.DMA((5,))], 4 * 10**9,
     )
-    va, vb, right, left = call(
-        halo_kernel, "halo", (up, down, right, left, bias, wqv, wk, wo, we, ws, ag, hg), vmem(12),
+    va, vb, odd, even = call(
+        halo_kernel, "halo", (odd, even, right, left, bias, wqv, wk, wo, we, ws, ag, hg), vmem(12),
         [((64, C), BF16)] * 2 + [((n // 2 + 32, C), BF16)] * 2, (), 10**9,
     )
-    hr = from_behind(left, "gx", -1)
-    hl = from_behind(right, "gx", 1)
-    row, col = lax.axis_index("gy"), lax.axis_index("gx")
-    flags = jnp.stack(
-        [row == 0, row == lax.axis_size("gy") - 1, col == 0, col == lax.axis_size("gx") - 1]
-    ).astype(jnp.int32)
+    odd, even = swap(odd, "gx", 1), swap(even, "gx", 0)
     oa, bias_b, bias_bv, wqv, wk = call(
-        middle_kernel, "middle", (flags, fa, na, va, pb, w, wo, we, ws, hg),
-        [pl.BlockSpec(memory_space=pltpu.SMEM)] + vmem(9),
+        middle_kernel, "middle", (fa, na, va, pb, w, wo, we, ws, hg),
+        vmem(9),
         [((n, C), F32), table, table] + prepared,
         [pltpu.VMEM(*table)] * 2, 2 * 10**9,
     )
     return call(
-        outer_kernel, "outer", (fb, nb, vb, hl, hr, oa, bias_b, bias_bv, wqv, wk, wo, we, ws, hg), vmem(14),
+        outer_kernel, "outer", (fb, nb, vb, odd, even, oa, bias_b, bias_bv, wqv, wk, wo, we, ws, hg), vmem(14),
         [((height, breadth, C), F32)], (), 2 * 10**9,
     )[0]
 

time: 37 us -> 36.8 us (level)
  the two profiles are of different devices: /device:TPU:56 before, /device:TPU:1 now
where the time goes in v4:
time: 36.8 us; the launch traced here: 36.6 us
  starting transfers between devices  24 us (65%)
  Pallas kernels  9.58 us (26%)
  waiting for transfers between devices  1.82 us (5%)
  local copies, waits for them, and re-layouts  0.98 us (3%)
    ppermute x4, starting transfers between devices, swap(): return lax.ppermute(x, axis, there + [(b, a) for a, b in there])  24 us
    pallas_call x5, Pallas kernels, call(): pl.pallas_call(kernel, out_shape=shapes, in_specs=specs, out_specs=vmem(l...  9.58 us
    ppermute x4, waiting for transfers between devices, swap(): return lax.ppermute(x, axis, there + [(b, a) for a, b in there])  1.82 us
    unnamed x16, local copies, waits for them, and re-layouts  0.98 us
  transfers between devices with their start and end apart: 4, of which 1 were waited for; matrix products, arithmetic and copies ran while one was open for 0% of the time, Pallas kernels for 15%

profile of v4, /device:TPU:1, one launch (start us, length us, event | category | flops | bytes accessed | tf_op | source)
XLA Modules:
  0.0 36.6 jit_solution(8502106483434986706)
XLA Ops:
  0.0 0.0 copy-start
  0.0 0.9 %copy-done = bf16[64,16,128]{2,1,0:T(8,128)(2,1)S(1)} copy-done((bf16[64,16,128]{2,1,0:T(8,128)(2,1)S(1)}, bf16[64,16,128]{2,1,0:T(8,128)(2,1)}, u32[]{:S(2)}) %copy-start) | copy-done | bytes 262168
  1.0 0.0 copy-start.1
  1.0 0.0 copy-start.2
  1.0 0.0 copy-start.3
  1.0 0.0 copy-start.4
  1.0 0.0 copy-start.5
  1.0 0.1 edge_rows.1
  1.1 0.0 copy-start.7
  1.1 0.0 copy-start.6
  1.1 5.5 %collective-permute-start = (bf16[8,16,128]{2,1,0:T(8,128)(2,1)S(1)}, bf16[8,16,128]{2,1,0:T(8,128)(2,1)S(1)}, u32[]{:S(2)}, u32[]{:S(2)}) collective-permute-start(bf16[8,16,128]{2,1,0:T(8,128)(2,1)S(1)} %get-tuple-element.31), channel_id=1, source_target_pairs={{16,32},{48,64},{80,96},{112,128},{144,160},{176,192},{208,224},{2... | collective-permute-start | bytes 98312 | tf_op jit(solution)/shard_map/ppermute | solution.py:28
  6.7 9.3 %collective-permute-start.1 = (bf16[8,16,128]{2,1,0:T(8,128)(2,1)S(1)}, bf16[8,16,128]{2,1,0:T(8,128)(2,1)S(1)}, u32[]{:S(2)}, u32[]{:S(2)}) collective-permute-start(bf16[8,16,128]{2,1,0:T(8,128)(2,1)S(1)} %get-tuple-element.32), channel_id=1, source_target_pairs={{0,16},{32,48},{64,80},{96,112},{128,144},{160,176},{192,208},{224... | collective-permute-start | bytes 98312 | tf_op jit(solution)/shard_map/ppermute | solution.py:28
  16.0 0.0 copy-done.1
  16.0 0.0 copy-done.2
  16.0 0.0 copy-done.3
  16.0 0.0 copy-done.4
  16.0 0.0 copy-done.5
  16.1 0.0 copy-done.7
  16.1 0.0 copy-done.6
  16.1 3.8 %own.1 = (f32[512,128]{1,0:T(8,128)S(1)}, f32[512,128]{1,0:T(8,128)S(1)}, bf16[512,128]{1,0:T(8,128)(2,1)S(1)}, bf16[512,128]{1,0:T(8,128)(2,1)S(1)}, bf16[256,1...) custom-call(bf16[64,16,128]{2,1,0:T(8,128)(2,1)S(1)} %copy-done, ...), custom_call_target="tpu_custom_call" | custom-call | flops 4000000000 | bytes 1048576 | tf_op jit(solution)/shard_map/own/pallas_call | solution.py:350
  19.8 0.0 collective-permute-done.rows_odd_ref
  19.9 0.0 collective-permute-done.1.rows_even_ref
  19.9 1.5 %halo.1 = (bf16[64,128]{1,0:T(8,128)(2,1)S(1)}, bf16[64,128]{1,0:T(8,128)(2,1)S(1)}, bf16[288,128]{1,0:T(8,128)(2,1)S(1)}, bf16[288,128]{1,0:T(8,128)(2,1)S(1)}) custom-call(bf16[8,16,128]{2,1,0:T(8,128)(2,1)S(1)} %collective-permute-done.rows_odd_ref, bf16[8,16,128]{2,1,0:T(8,128)(2,1)S(1)} %collective-permute-done.1.rows_even_ref, ...), custom_call_target="tpu_custom_call" | custom-call | flops 1000000000 | bytes 1048576 | tf_op jit(solution)/shard_map/halo/pallas_call | solution.py:350
  21.4 7.3 %collective-permute-start.2 = (bf16[288,128]{1,0:T(8,128)(2,1)S(1)}, bf16[288,128]{1,0:T(8,128)(2,1)S(1)}, u32[]{:S(2)}, u32[]{:S(2)}) collective-permute-start(bf16[288,128]{1,0:T(8,128)(2,1)S(1)} %get-tuple-element.42), channel_id=1, source_target_pairs={{1,2},{3,4},{5,6},{7,8},{9,10},{11,12},{13,14},{15,0},{2,1},{4,3},... | collective-permute-start | bytes 221192 | tf_op jit(solution)/shard_map/ppermute | solution.py:28
  28.7 1.9 %collective-permute-start.3 = (bf16[288,128]{1,0:T(8,128)(2,1)S(1)}, bf16[288,128]{1,0:T(8,128)(2,1)S(1)}, u32[]{:S(2)}, u32[]{:S(2)}) collective-permute-start(bf16[288,128]{1,0:T(8,128)(2,1)S(1)} %get-tuple-element.43), channel_id=1, source_target_pairs={{0,1},{2,3},{4,5},{6,7},{8,9},{10,11},{12,13},{14,15},{1,0},{3,2},... | collective-permute-start | bytes 221192 | tf_op jit(solution)/shard_map/ppermute | solution.py:28
  30.6 1.7 %middle.1 = (f32[512,128]{1,0:T(8,128)S(1)}, f32[64,512]{1,0:T(8,128)S(1)}, f32[64,512]{1,0:T(8,128)S(1)}, bf16[256,128]{1,0:T(8,128)(2,1)S(1)}, bf16[256,256]{1,0:T(8,128)(2,1)S(1)}) custom-call(f32[512,128]{1,0:T(8,128)S(1)} %get-tuple-element.44.fa_ref, bf16[512,128]{1,0:T(8,128)(2,1)S(1)} %get-tuple-element.45.na_ref, ...), custom_call_target="tpu_custom_call" | custom-call | flops 2000000000 | bytes 1048576 | tf_op jit(solution)/shard_map/middle/pallas_call | solution.py:350
  32.3 0.0 collective-permute-done.2.cols_odd_ref
  32.3 1.8 %collective-permute-done.3.cols_even_ref = bf16[288,128]{1,0:T(8,128)(2,1)S(1)} collective-permute-done((bf16[288,128]{1,0:T(8,128)(2,1)S(1)}, bf16[288,128]{1,0:T(8,128)(2,1)S(1)}, u32[]{:S(2)}, u32[]{:S(2)}) %collective-permute-start.3) | collective-permute-done | bytes 73760 | tf_op jit(solution)/shard_map/ppermute | solution.py:28
  34.1 2.4 %outer.1 = f32[64,16,128]{2,1,0:T(8,128)} custom-call(f32[512,128]{1,0:T(8,128)S(1)} %get-tuple-element.29.fb_ref, bf16[512,128]{1,0:T(8,128)(2,1)S(1)} %get-tuple-element.30.nb_ref, bf16[64,128]{1,0:T(8,128)(2,1)S(1)} %get-tuple-element.41.vb_ref, bf16[288,128]{1,0:T(8,128)(2,1)S(1)} %collective-permute-done.2.cols_odd_ref, ...), custom_call_target="tpu_custom_call" | custom-call | flops 2000000000 | bytes 1048576 | tf_op jit(solution)/shard_map/outer/pallas_call | solution.py:350
Async XLA Ops:
  0.0 0.9 %copy-start = (bf16[64,16,128]{2,1,0:T(8,128)(2,1)S(1)}, bf16[64,16,128]{2,1,0:T(8,128)(2,1)}, u32[]{:S(2)}) copy-start(bf16[64,16,128]{2,1,0:T(8,128)(2,1)} %x_ref.1) | copy-start | bytes 786436
  1.0 15.1 %copy-start.1 = (bf16[2,128,512]{2,1,0:T(8,128)(2,1)S(1)}, bf16[2,128,512]{2,1,0:T(8,128)(2,1)}, u32[]{:S(2)}) copy-start(bf16[2,128,512]{2,1,0:T(8,128)(2,1)} %we_hbm.1) | copy-start | bytes 786436
  1.0 15.1 %copy-start.2 = (bf16[2,512,128]{2,1,0:T(8,128)(2,1)S(1)}, bf16[2,512,128]{2,1,0:T(8,128)(2,1)}, u32[]{:S(2)}) copy-start(bf16[2,512,128]{2,1,0:T(8,128)(2,1)} %ws_hbm.1) | copy-start | bytes 786436
  1.0 15.1 %copy-start.3 = (bf16[2,128,384]{2,1,0:T(8,128)(2,1)S(1)}, bf16[2,128,384]{2,1,0:T(8,128)(2,1)}, u32[]{:S(2)}) copy-start(bf16[2,128,384]{2,1,0:T(8,128)(2,1)} %w_hbm.1) | copy-start | bytes 589828
  1.0 15.1 %copy-start.4 = (bf16[2,128,128]{2,1,0:T(8,128)(2,1)S(1)}, bf16[2,128,128]{2,1,0:T(8,128)(2,1)}, u32[]{:S(2)}) copy-start(bf16[2,128,128]{2,1,0:T(8,128)(2,1)} %wo_hbm.1) | copy-start | bytes 196612
  1.0 15.1 %copy-start.5 = (f32[2,4,225]{2,1,0:T(4,128)S(1)}, f32[2,4,225]{2,1,0:T(4,128)}, u32[]{:S(2)}) copy-start(f32[2,4,225]{2,1,0:T(4,128)} %pb_ref.3) | copy-start | bytes 21604
  1.1 15.0 %copy-start.7 = (f32[2,128]{1,0:T(2,128)S(1)}, f32[2,128]{1,0:T(2,128)}, u32[]{:S(2)}) copy-start(f32[2,128]{1,0:T(2,128)} %hg_ref.7) | copy-start | bytes 3076
  1.1 14.9 %copy-start.6 = (f32[2,128]{1,0:T(2,128)S(1)}, f32[2,128]{1,0:T(2,128)}, u32[]{:S(2)}) copy-start(f32[2,128]{1,0:T(2,128)} %ag_ref.3) | copy-start | bytes 3076
  1.1 18.7 %collective-permute-start = (bf16[8,16,128]{2,1,0:T(8,128)(2,1)S(1)}, bf16[8,16,128]{2,1,0:T(8,128)(2,1)S(1)}, u32[]{:S(2)}, u32[]{:S(2)}) collective-permute-start(bf16[8,16,128]{2,1,0:T(8,128)(2,1)S(1)} %get-tuple-element.31), channel_id=1, source_target_pairs={{16,32},{48,64},{80,96},{112,128},{144,160},{176,192},{208,224},{2... | collective-permute-start | bytes 98312 | tf_op jit(solution)/shard_map/ppermute | solution.py:28
  6.7 13.2 %collective-permute-start.1 = (bf16[8,16,128]{2,1,0:T(8,128)(2,1)S(1)}, bf16[8,16,128]{2,1,0:T(8,128)(2,1)S(1)}, u32[]{:S(2)}, u32[]{:S(2)}) collective-permute-start(bf16[8,16,128]{2,1,0:T(8,128)(2,1)S(1)} %get-tuple-element.32), channel_id=1, source_target_pairs={{0,16},{32,48},{64,80},{96,112},{128,144},{160,176},{192,208},{224... | collective-permute-start | bytes 98312 | tf_op jit(solution)/shard_map/ppermute | solution.py:28
  21.4 10.9 %collective-permute-start.2 = (bf16[288,128]{1,0:T(8,128)(2,1)S(1)}, bf16[288,128]{1,0:T(8,128)(2,1)S(1)}, u32[]{:S(2)}, u32[]{:S(2)}) collective-permute-start(bf16[288,128]{1,0:T(8,128)(2,1)S(1)} %get-tuple-element.42), channel_id=1, source_target_pairs={{1,2},{3,4},{5,6},{7,8},{9,10},{11,12},{13,14},{15,0},{2,1},{4,3},... | collective-permute-start | bytes 221192 | tf_op jit(solution)/shard_map/ppermute | solution.py:28
  28.7 5.5 %collective-permute-start.3 = (bf16[288,128]{1,0:T(8,128)(2,1)S(1)}, bf16[288,128]{1,0:T(8,128)(2,1)S(1)}, u32[]{:S(2)}, u32[]{:S(2)}) collective-permute-start(bf16[288,128]{1,0:T(8,128)(2,1)S(1)} %get-tuple-element.43), channel_id=1, source_target_pairs={{0,1},{2,3},{4,5},{6,7},{8,9},{10,11},{12,13},{14,15},{1,0},{3,2},... | collective-permute-start | bytes 221192 | tf_op jit(solution)/shard_map/ppermute | solution.py:28

commit v5 on v4

--- a/solution.py
+++ b/solution.py
@@ -172,9 +172,41 @@
     return right.astype(BF16), left.astype(BF16)
 
 
-def edge_rows_kernel(x_ref, odd_ref, even_ref, sems):
+def goes_first():
+    row, rows = lax.axis_index("gy"), lax.axis_size("gy")
+    return lax.rem(row, rows // 2) < rows // 4
+
+
+def own_block(
+    x_ref, w_ref, wo_ref, we_ref, ws_ref, ag_ref, pb_ref, hg_ref,
+    fa_ref, fb_ref, na_ref, nb_ref, right_ref, left_ref, bias_ref, wqv_ref, wk_ref,
+):
+    for head, yj, values in bias_rows(pb_ref, 0):
+        bias_ref[yj * 8 : yj * 8 + 8, head * 128 : head * 128 + 128] = values
+    fill_weights(w_ref[0], wqv_ref, wk_ref)
+    bands = x_ref.shape[0] // WIN
+    z = cat([t for b in range(bands) for t in windows_of(x_ref[WIN * b : WIN * b + WIN])])
+    normed = layer_norm(z, ag_ref[0:1, :]).astype(BF16)
+    qv = dot(wqv_ref[...], normed, NT).astype(BF16)
+    keys = side_by_side(normed, wk_ref[...])
+    masks = [mask("1"), mask("2")]
+    units = [([b], masks, bias_ref[...]) for b in range(bands)]
+    context = attention(qv[0:128], keys, qv[128:256], units)
+    out = finish(z, context, wo_ref[0], hg_ref[0:1, :], we_ref[0], ws_ref[0])
+    fa_ref[...], fb_ref[...] = shifted_columns(out)
+    na, nb = shifted_columns(layer_norm(out, ag_ref[1:2, :]))
+    na_ref[...] = na.astype(BF16)
+    nb_ref[...] = nb.astype(BF16)
+    right_ref[...], left_ref[...] = edges(nb)
+
+
+def parity_kernel(out_ref):
+    out_ref[...] = jnp.full(out_ref.shape, lax.rem(lax.axis_index("gy"), 2), jnp.int32)
+
+
+def edge_rows_kernel(x_ref, parity_ref, odd_ref, even_ref, sems):
     bottom = x_ref.shape[0] - WIN
-    is_odd = lax.rem(lax.axis_index("gy"), 2)
+    is_odd = parity_ref[0, 0]
     copies = [
         pltpu.make_async_copy(x_ref.at[pl.ds(is_odd * bottom, WIN)], odd_ref, sems.at[0]),
         pltpu.make_async_copy(x_ref.at[pl.ds((1 - is_odd) * bottom, WIN)], even_ref, sems.at[1]),
@@ -185,40 +217,16 @@
         copy.wait()
 
 
-def own_kernel(
-    x_hbm, w_hbm, wo_hbm, we_hbm, ws_hbm, ag_ref, pb_ref, hg_ref,
-    fa_ref, fb_ref, na_ref, nb_ref, right_ref, left_ref, bias_ref, wqv_ref, wk_ref, w_ref, wo_ref, we_ref, ws_ref,
-    x_ref, sems,
-):
-    copies = [
-        pltpu.make_async_copy(a, b, sems.at[i])
-        for i, (a, b) in enumerate(
-            [(w_hbm, w_ref), (x_hbm, x_ref), (wo_hbm, wo_ref), (we_hbm, we_ref), (ws_hbm, ws_ref)]
-        )
-    ]
-    for copy in copies:
-        copy.start()
-    for head, yj, values in bias_rows(pb_ref, 0):
-        bias_ref[yj * 8 : yj * 8 + 8, head * 128 : head * 128 + 128] = values
-    copies[0].wait()
-    fill_weights(w_ref[0], wqv_ref, wk_ref)
-    copies[1].wait()
-    bands = x_ref.shape[0] // WIN
-    z = cat([t for b in range(bands) for t in windows_of(x_ref[WIN * b : WIN * b + WIN])])
-    normed = layer_norm(z, ag_ref[0:1, :]).astype(BF16)
-    qv = dot(wqv_ref[...], normed, NT).astype(BF16)
-    keys = side_by_side(normed, wk_ref[...])
-    masks = [mask("1"), mask("2")]
-    units = [([b], masks, bias_ref[...]) for b in range(bands)]
-    context = attention(qv[0:128], keys, qv[128:256], units)
-    for copy in copies[2:]:
-        copy.wait()
-    out = finish(z, context, wo_ref[0], hg_ref[0:1, :], we_ref[0], ws_ref[0])
-    fa_ref[...], fb_ref[...] = shifted_columns(out)
-    na, nb = shifted_columns(layer_norm(out, ag_ref[1:2, :]))
-    na_ref[...] = na.astype(BF16)
-    nb_ref[...] = nb.astype(BF16)
-    right_ref[...], left_ref[...] = edges(nb)
+def first_kernel(*refs):
+    @pl.when(goes_first())
+    def _():
+        own_block(*refs[0:8], *refs[12:])
+
+
+def second_kernel(*refs):
+    @pl.when(jnp.logical_not(goes_first()))
+    def _():
+        own_block(*refs[0:8], *refs[17:])
 
 
 def halo_kernel(
@@ -345,14 +353,15 @@
     return [pl.BlockSpec(memory_space=pltpu.VMEM)] * count
 
 
-def call(kernel, name, operands, specs, outs, scratch=(), flops=0):
+def call(kernel, name, operands, outs, scratch=(), flops=0, aliases=None):
     shapes = [jax.ShapeDtypeStruct(shape, dtype) for shape, dtype in outs]
     return pl.pallas_call(
         kernel,
         out_shape=shapes,
-        in_specs=specs,
+        in_specs=vmem(len(operands)),
         out_specs=vmem(len(outs)),
         scratch_shapes=list(scratch),
+        input_output_aliases=aliases or {},
         compiler_params=pltpu.CompilerParams(vmem_limit_bytes=32 * 1024 * 1024),
         cost_estimate=pl.CostEstimate(flops=flops, bytes_accessed=1 << 20, transcendentals=0),
         name=name,
@@ -362,33 +371,34 @@
 def on_device(x, ag, tw, ow, pb, hg, ew, sw):
     height, breadth = x.shape[0], x.shape[1]
     n = height * WIN
-    hbm = [pl.BlockSpec(memory_space=pltpu.HBM)]
-    odd, even = call(
-        edge_rows_kernel, "edge_rows", (x,), hbm,
-        [((WIN, breadth, C), BF16)] * 2, [pltpu.SemaphoreType.DMA((2,))], 4 * 10**10,
-    )
-    odd, even = swap(odd, "gy", 1), swap(even, "gy", 0)
     table = ((64, HEADS * 128), F32)
     prepared = [((256, 128), BF16), ((256, 256), BF16)]
-    fa, fb, na, nb, right, left, bias, wqv, wk, w, wo, we, ws = call(
-        own_kernel, "own", (x, tw, ow, ew, sw, ag, pb, hg), hbm * 5 + vmem(3),
-        [((n, C), F32)] * 2 + [((n, C), BF16)] * 2 + [((n // 2, C), BF16)] * 2 + [table] + prepared
-        + [(tw.shape, BF16), (ow.shape, BF16), (ew.shape, BF16), (sw.shape, BF16)],
-        [pltpu.VMEM(x.shape, BF16), pltpu.SemaphoreType.DMA((5,))], 4 * 10**9,
-    )
+    weights = (x, tw, ow, ew, sw, ag, pb, hg)
+    kept = [((n, C), F32)] * 2 + [((n, C), BF16)] * 2 + [((n // 2, C), BF16)] * 2 + [table] + prepared
+    rows = [((WIN, breadth, C), BF16)] * 2
+    (parity,) = call(parity_kernel, "parity", (), [((8, 128), jnp.int32)], (), 4 * 10**10)
+    odd, even = call(
+        edge_rows_kernel, "edge_rows", (x, parity), rows, [pltpu.SemaphoreType.DMA((2,))]
+    )
+    odd, even, *state = call(
+        first_kernel, "first", (*weights, odd, even), rows + kept, (), 4 * 10**9, {8: 0, 9: 1}
+    )
+    odd, even = swap(odd, "gy", 1), swap(even, "gy", 0)
+    state = call(
+        second_kernel, "second", (*weights, *state), kept, (), 4 * 10**9, {8 + i: i for i in range(9)}
+    )
+    fa, fb, na, nb, right, left, bias, wqv, wk = state
     va, vb, odd, even = call(
-        halo_kernel, "halo", (odd, even, right, left, bias, wqv, wk, wo, we, ws, ag, hg), vmem(12),
+        halo_kernel, "halo", (odd, even, right, left, bias, wqv, wk, ow, ew, sw, ag, hg),
         [((64, C), BF16)] * 2 + [((n // 2 + 32, C), BF16)] * 2, (), 10**9,
     )
     odd, even = swap(odd, "gx", 1), swap(even, "gx", 0)
     oa, bias_b, bias_bv, wqv, wk = call(
-        middle_kernel, "middle", (fa, na, va, pb, w, wo, we, ws, hg),
-        vmem(9),
-        [((n, C), F32), table, table] + prepared,
-        [pltpu.VMEM(*table)] * 2, 2 * 10**9,
+        middle_kernel, "middle", (fa, na, va, pb, tw, ow, ew, sw, hg),
+        [((n, C), F32), table, table] + prepared, [pltpu.VMEM(*table)] * 2, 2 * 10**9,
     )
     return call(
-        outer_kernel, "outer", (fb, nb, vb, odd, even, oa, bias_b, bias_bv, wqv, wk, wo, we, ws, hg), vmem(14),
+        outer_kernel, "outer", (fb, nb, vb, odd, even, oa, bias_b, bias_bv, wqv, wk, ow, ew, sw, hg),
         [((height, breadth, C), F32)], (), 2 * 10**9,
     )[0]
 

time: 36.8 us -> 34.1 us (0.927)
  starting transfers between devices: 24 us -> 21 us
  Pallas kernels: 9.58 us -> 8.77 us
  local copies, waits for them, and re-layouts: 0.98 us -> 1.69 us
  waiting for transfers between devices: 1.82 us -> 2.24 us
    ppermute x4, starting transfers between devices: 24 us -> 21 us  [swap(): return lax.ppermute(x, axis, there + [(b, a) for a, b in there])]
    pallas_call x5 -> x7, Pallas kernels: 9.58 us -> 8.77 us  [call(): pl.pallas_call(kernel, out_shape=shapes, in_specs=vmem(len(operands)), ou...]
    unnamed x16, local copies, waits for them, and re-layouts: 0.98 us -> 1.69 us
    ppermute x4, waiting for transfers between devices: 1.82 us -> 2.24 us  [swap(): return lax.ppermute(x, axis, there + [(b, a) for a, b in there])]
  transfers between devices with their start and end apart: 4 -> 4, of which waited for: 1 -> 2; matrix products, arithmetic and copies ran while one was open for 0% -> 0% of each run, Pallas kernels for 15% -> 5%
where the time goes in v5:
time: 34.1 us; the launch traced here: 33.9 us
  starting transfers between devices  21 us (62%)
  Pallas kernels  8.77 us (26%)
  waiting for transfers between devices  2.24 us (7%)
  local copies, waits for them, and re-layouts  1.69 us (5%)
    ppermute x4, starting transfers between devices, swap(): return lax.ppermute(x, axis, there + [(b, a) for a, b in there])  21 us
    pallas_call x7, Pallas kernels, call(): pl.pallas_call(kernel, out_shape=shapes, in_specs=vmem(len(operands)), ou...  8.77 us
    ppermute x4, waiting for transfers between devices, swap(): return lax.ppermute(x, axis, there + [(b, a) for a, b in there])  2.24 us
    unnamed x16, local copies, waits for them, and re-layouts  1.69 us
  transfers between devices with their start and end apart: 4, of which 2 were waited for; matrix products, arithmetic and copies ran while one was open for 0% of the time, Pallas kernels for 5%

profile of v5, /device:TPU:1, one launch (start us, length us, event | category | flops | bytes accessed | tf_op | source)
XLA Modules:
  0.0 33.9 jit_solution(14505199992698136499)
XLA Ops:
  0.0 0.0 copy-start
  0.0 0.0 copy-start.2
  0.0 0.0 copy-start.3
  0.0 0.0 copy-start.4
  0.0 0.0 copy-start.5
  0.0 0.0 copy-start.7
  0.1 0.9 %copy-done = bf16[64,16,128]{2,1,0:T(8,128)(2,1)S(1)} copy-done((bf16[64,16,128]{2,1,0:T(8,128)(2,1)S(1)}, bf16[64,16,128]{2,1,0:T(8,128)(2,1)}, u32[]{:S(2)}) %copy-start) | copy-done | bytes 262168
  1.0 0.0 copy-start.1
  1.0 0.1 edge_rows.1
  1.1 0.0 copy-start.6
  1.1 0.0 copy-done.2
  1.1 0.0 copy-done.3
  1.1 0.0 copy-done.4
  1.1 0.0 copy-done.5
  1.2 0.0 copy-done.7
  1.2 0.8 %copy-done.1 = bf16[2,128,512]{2,1,0:T(8,128)(2,1)S(1)} copy-done((bf16[2,128,512]{2,1,0:T(8,128)(2,1)S(1)}, bf16[2,128,512]{2,1,0:T(8,128)(2,1)}, u32[]{:S(2)}) %copy-start.1) | copy-done | bytes 262168
  1.9 0.0 copy-done.6
  1.9 2.9 %first.1 = (bf16[8,16,128]{2,1,0:T(8,128)(2,1)S(1)}, bf16[8,16,128]{2,1,0:T(8,128)(2,1)S(1)}, f32[512,128]{1,0:T(8,128)S(1)}, f32[512,128]{1,0:T(8,128)S(1)}, bf...) custom-call(bf16[64,16,128]{2,1,0:T(8,128)(2,1)S(1)} %copy-done, ...), custom_call_target="tpu_custom_call", output_to_operand_aliasing={{0}: (8, {}), {1}: (9, {})} | custom-call | flops 4000000000 | bytes 1048576 | tf_op jit(solution)/shard_map/first/pallas_call | solution.py:358
  4.9 5.4 %collective-permute-start = (bf16[8,16,128]{2,1,0:T(8,128)(2,1)S(1)}, bf16[8,16,128]{2,1,0:T(8,128)(2,1)S(1)}, u32[]{:S(2)}, u32[]{:S(2)}) collective-permute-start(bf16[8,16,128]{2,1,0:T(8,128)(2,1)S(1)} %get-tuple-element.49), channel_id=1, source_target_pairs={{16,32},{48,64},{80,96},{112,128},{144,160},{176,192},{208,224},{2... | collective-permute-start | bytes 98312 | tf_op jit(solution)/shard_map/ppermute | solution.py:28
  10.3 6.4 %collective-permute-start.1 = (bf16[8,16,128]{2,1,0:T(8,128)(2,1)S(1)}, bf16[8,16,128]{2,1,0:T(8,128)(2,1)S(1)}, u32[]{:S(2)}, u32[]{:S(2)}) collective-permute-start(bf16[8,16,128]{2,1,0:T(8,128)(2,1)S(1)} %get-tuple-element.50), channel_id=1, source_target_pairs={{0,16},{32,48},{64,80},{96,112},{128,144},{160,176},{192,208},{224... | collective-permute-start | bytes 98312 | tf_op jit(solution)/shard_map/ppermute | solution.py:28
  16.7 0.0 collective-permute-done.rows_odd_ref
  16.7 0.8 %collective-permute-done.1.rows_even_ref = bf16[8,16,128]{2,1,0:T(8,128)(2,1)S(1)} collective-permute-done((bf16[8,16,128]{2,1,0:T(8,128)(2,1)S(1)}, bf16[8,16,128]{2,1,0:T(8,128)(2,1)S(1)}, u32[]{:S(2)}, u32[]{:S(2)}) %collective-permute-start.1) | collective-permute-done | bytes 32800 | tf_op jit(solution)/shard_map/ppermute | solution.py:28
  17.5 1.5 %halo.1 = (bf16[64,128]{1,0:T(8,128)(2,1)S(1)}, bf16[64,128]{1,0:T(8,128)(2,1)S(1)}, bf16[288,128]{1,0:T(8,128)(2,1)S(1)}, bf16[288,128]{1,0:T(8,128)(2,1)S(1)}) custom-call(bf16[8,16,128]{2,1,0:T(8,128)(2,1)S(1)} %collective-permute-done.rows_odd_ref, bf16[8,16,128]{2,1,0:T(8,128)(2,1)S(1)} %collective-permute-done.1.rows_even_ref, ...), custom_call_target="tpu_custom_call" | custom-call | flops 1000000000 | bytes 1048576 | tf_op jit(solution)/shard_map/halo/pallas_call | solution.py:358
  19.0 7.3 %collective-permute-start.2 = (bf16[288,128]{1,0:T(8,128)(2,1)S(1)}, bf16[288,128]{1,0:T(8,128)(2,1)S(1)}, u32[]{:S(2)}, u32[]{:S(2)}) collective-permute-start(bf16[288,128]{1,0:T(8,128)(2,1)S(1)} %get-tuple-element.57), channel_id=1, source_target_pairs={{1,2},{3,4},{5,6},{7,8},{9,10},{11,12},{13,14},{15,0},{2,1},{4,3},... | collective-permute-start | bytes 221192 | tf_op jit(solution)/shard_map/ppermute | solution.py:28
  26.3 1.9 %collective-permute-start.3 = (bf16[288,128]{1,0:T(8,128)(2,1)S(1)}, bf16[288,128]{1,0:T(8,128)(2,1)S(1)}, u32[]{:S(2)}, u32[]{:S(2)}) collective-permute-start(bf16[288,128]{1,0:T(8,128)(2,1)S(1)} %get-tuple-element.58), channel_id=1, source_target_pairs={{0,1},{2,3},{4,5},{6,7},{8,9},{10,11},{12,13},{14,15},{1,0},{3,2},... | collective-permute-start | bytes 221192 | tf_op jit(solution)/shard_map/ppermute | solution.py:28
  28.2 1.7 %middle.1 = (f32[512,128]{1,0:T(8,128)S(1)}, f32[64,512]{1,0:T(8,128)S(1)}, f32[64,512]{1,0:T(8,128)S(1)}, bf16[256,128]{1,0:T(8,128)(2,1)S(1)}, bf16[256,256]{1,0:T(8,128)(2,1)S(1)}) custom-call(f32[512,128]{1,0:T(8,128)S(1)} %get-tuple-element.59.fa_ref, bf16[512,128]{1,0:T(8,128)(2,1)S(1)} %get-tuple-element.60.na_ref, ...), custom_call_target="tpu_custom_call" | custom-call | flops 2000000000 | bytes 1048576 | tf_op jit(solution)/shard_map/middle/pallas_call | solution.py:358
  30.0 0.0 collective-permute-done.2.cols_odd_ref
  30.0 1.4 %collective-permute-done.3.cols_even_ref = bf16[288,128]{1,0:T(8,128)(2,1)S(1)} collective-permute-done((bf16[288,128]{1,0:T(8,128)(2,1)S(1)}, bf16[288,128]{1,0:T(8,128)(2,1)S(1)}, u32[]{:S(2)}, u32[]{:S(2)}) %collective-permute-start.3) | collective-permute-done | bytes 73760 | tf_op jit(solution)/shard_map/ppermute | solution.py:28
  31.4 2.4 %outer.1 = f32[64,16,128]{2,1,0:T(8,128)} custom-call(f32[512,128]{1,0:T(8,128)S(1)} %get-tuple-element.47.fb_ref, bf16[512,128]{1,0:T(8,128)(2,1)S(1)} %get-tuple-element.48.nb_ref, bf16[64,128]{1,0:T(8,128)(2,1)S(1)} %get-tuple-element.56.vb_ref, bf16[288,128]{1,0:T(8,128)(2,1)S(1)} %collective-permute-done.2.cols_odd_ref, ...), custom_call_target="tpu_custom_call" | custom-call | flops 2000000000 | bytes 1048576 | tf_op jit(solution)/shard_map/outer/pallas_call | solution.py:358
  (2 shorter events, 0.0 us)
Async XLA Ops:
  0.0 0.9 %copy-start = (bf16[64,16,128]{2,1,0:T(8,128)(2,1)S(1)}, bf16[64,16,128]{2,1,0:T(8,128)(2,1)}, u32[]{:S(2)}) copy-start(bf16[64,16,128]{2,1,0:T(8,128)(2,1)} %refs_0_.3) | copy-start | bytes 786436
  0.0 1.1 %copy-start.2 = (bf16[2,512,128]{2,1,0:T(8,128)(2,1)S(1)}, bf16[2,512,128]{2,1,0:T(8,128)(2,1)}, u32[]{:S(2)}) copy-start(bf16[2,512,128]{2,1,0:T(8,128)(2,1)} %ws_ref.5) | copy-start | bytes 786436
  0.0 1.1 %copy-start.3 = (bf16[2,128,384]{2,1,0:T(8,128)(2,1)S(1)}, bf16[2,128,384]{2,1,0:T(8,128)(2,1)}, u32[]{:S(2)}) copy-start(bf16[2,128,384]{2,1,0:T(8,128)(2,1)} %w_ref.1) | copy-start | bytes 589828
  0.0 1.1 %copy-start.4 = (bf16[2,128,128]{2,1,0:T(8,128)(2,1)S(1)}, bf16[2,128,128]{2,1,0:T(8,128)(2,1)}, u32[]{:S(2)}) copy-start(bf16[2,128,128]{2,1,0:T(8,128)(2,1)} %wo_ref.5) | copy-start | bytes 196612
  0.0 1.1 %copy-start.5 = (f32[2,4,225]{2,1,0:T(4,128)S(1)}, f32[2,4,225]{2,1,0:T(4,128)}, u32[]{:S(2)}) copy-start(f32[2,4,225]{2,1,0:T(4,128)} %pb_ref.1) | copy-start | bytes 21604
  0.0 1.1 %copy-start.7 = (f32[2,128]{1,0:T(2,128)S(1)}, f32[2,128]{1,0:T(2,128)}, u32[]{:S(2)}) copy-start(f32[2,128]{1,0:T(2,128)} %hg_ref.5) | copy-start | bytes 3076
  1.0 1.0 %copy-start.1 = (bf16[2,128,512]{2,1,0:T(8,128)(2,1)S(1)}, bf16[2,128,512]{2,1,0:T(8,128)(2,1)}, u32[]{:S(2)}) copy-start(bf16[2,128,512]{2,1,0:T(8,128)(2,1)} %we_ref.5) | copy-start | bytes 786436
  1.1 0.8 %copy-start.6 = (f32[2,128]{1,0:T(2,128)S(1)}, f32[2,128]{1,0:T(2,128)}, u32[]{:S(2)}) copy-start(f32[2,128]{1,0:T(2,128)} %ag_ref.1) | copy-start | bytes 3076
  4.9 11.9 %collective-permute-start = (bf16[8,16,128]{2,1,0:T(8,128)(2,1)S(1)}, bf16[8,16,128]{2,1,0:T(8,128)(2,1)S(1)}, u32[]{:S(2)}, u32[]{:S(2)}) collective-permute-start(bf16[8,16,128]{2,1,0:T(8,128)(2,1)S(1)} %get-tuple-element.49), channel_id=1, source_target_pairs={{16,32},{48,64},{80,96},{112,128},{144,160},{176,192},{208,224},{2... | collective-permute-start | bytes 98312 | tf_op jit(solution)/shard_map/ppermute | solution.py:28
  10.3 7.3 %collective-permute-start.1 = (bf16[8,16,128]{2,1,0:T(8,128)(2,1)S(1)}, bf16[8,16,128]{2,1,0:T(8,128)(2,1)S(1)}, u32[]{:S(2)}, u32[]{:S(2)}) collective-permute-start(bf16[8,16,128]{2,1,0:T(8,128)(2,1)S(1)} %get-tuple-element.50), channel_id=1, source_target_pairs={{0,16},{32,48},{64,80},{96,112},{128,144},{160,176},{192,208},{224... | collective-permute-start | bytes 98312 | tf_op jit(solution)/shard_map/ppermute | solution.py:28
  19.0 10.9 %collective-permute-start.2 = (bf16[288,128]{1,0:T(8,128)(2,1)S(1)}, bf16[288,128]{1,0:T(8,128)(2,1)S(1)}, u32[]{:S(2)}, u32[]{:S(2)}) collective-permute-start(bf16[288,128]{1,0:T(8,128)(2,1)S(1)} %get-tuple-element.57), channel_id=1, source_target_pairs={{1,2},{3,4},{5,6},{7,8},{9,10},{11,12},{13,14},{15,0},{2,1},{4,3},... | collective-permute-start | bytes 221192 | tf_op jit(solution)/shard_map/ppermute | solution.py:28
  26.3 5.1 %collective-permute-start.3 = (bf16[288,128]{1,0:T(8,128)(2,1)S(1)}, bf16[288,128]{1,0:T(8,128)(2,1)S(1)}, u32[]{:S(2)}, u32[]{:S(2)}) collective-permute-start(bf16[288,128]{1,0:T(8,128)(2,1)S(1)} %get-tuple-element.58), channel_id=1, source_target_pairs={{0,1},{2,3},{4,5},{6,7},{8,9},{10,11},{12,13},{14,15},{1,0},{3,2},... | collective-permute-start | bytes 221192 | tf_op jit(solution)/shard_map/ppermute | solution.py:28

commit v6 on v5

--- a/solution.py
+++ b/solution.py
@@ -204,7 +204,7 @@
     out_ref[...] = jnp.full(out_ref.shape, lax.rem(lax.axis_index("gy"), 2), jnp.int32)
 
 
-def edge_rows_kernel(x_ref, parity_ref, odd_ref, even_ref, sems):
+def edge_rows_kernel(x_ref, parity_ref, ag_ref, pb_ref, hg_ref, odd_ref, even_ref, sems):
     bottom = x_ref.shape[0] - WIN
     is_odd = parity_ref[0, 0]
     copies = [
@@ -218,9 +218,11 @@
 
 
 def first_kernel(*refs):
-    @pl.when(goes_first())
-    def _():
-        own_block(*refs[0:8], *refs[12:])
+    own_block(*refs[0:8], *refs[12:])
+
+
+def nothing_kernel(*refs):
+    pass
 
 
 def second_kernel(*refs):
@@ -378,12 +380,17 @@
     rows = [((WIN, breadth, C), BF16)] * 2
     (parity,) = call(parity_kernel, "parity", (), [((8, 128), jnp.int32)], (), 4 * 10**10)
     odd, even = call(
-        edge_rows_kernel, "edge_rows", (x, parity), rows, [pltpu.SemaphoreType.DMA((2,))]
+        edge_rows_kernel, "edge_rows", (x, parity, ag, pb, hg), rows, [pltpu.SemaphoreType.DMA((2,))]
     )
-    odd, even, *state = call(
-        first_kernel, "first", (*weights, odd, even), rows + kept, (), 4 * 10**9, {8: 0, 9: 1}
-    )
-    odd, even = swap(odd, "gy", 1), swap(even, "gy", 0)
+
+    def run(*operands):
+        return call(first_kernel, "first", operands, rows + kept, (), 4 * 10**9, {8: 0, 9: 1})
+
+    def skip(*operands):
+        return call(nothing_kernel, "nothing", operands[8:10], rows + kept, (), 0, {0: 0, 1: 1})
+
+    odd, even, *state = lax.cond(goes_first(), run, skip, *weights, odd, even)
+    even, odd = swap(even, "gy", 0), swap(odd, "gy", 1)
     state = call(
         second_kernel, "second", (*weights, *state), kept, (), 4 * 10**9, {8 + i: i for i in range(9)}
     )

time: 34.1 us -> 34 us (level)
  no operation moved by 1% of the time
where the time goes in v6:
time: 34 us; the launch traced here: 33.8 us
  starting transfers between devices  21 us (62%)
  Pallas kernels  8.79 us (26%)
  waiting for transfers between devices  2.24 us (7%)
  local copies, waits for them, and re-layouts  1.62 us (5%)
    ppermute x4, starting transfers between devices, swap(): return lax.ppermute(x, axis, there + [(b, a) for a, b in there])  21 us
    pallas_call x7, Pallas kernels, call(): pl.pallas_call(kernel, out_shape=shapes, in_specs=vmem(len(operands)), ou...  8.79 us
    ppermute x4, waiting for transfers between devices, swap(): return lax.ppermute(x, axis, there + [(b, a) for a, b in there])  2.24 us
    unnamed x16, local copies, waits for them, and re-layouts  1.62 us
  transfers between devices with their start and end apart: 4, of which 2 were waited for; matrix products, arithmetic and copies ran while one was open for 0% of the time, Pallas kernels for 5%

profile of v6, /device:TPU:1, one launch (start us, length us, event | category | flops | bytes accessed | tf_op | source)
XLA Modules:
  0.0 33.8 jit_solution(9921826335335136671)
XLA Ops:
  0.0 0.0 copy-start
  0.0 0.0 copy-start.3
  0.0 0.0 copy-start.4
  0.0 0.0 copy-start.5
  0.0 0.0 copy-start.6
  0.1 0.0 copy-start.1
  0.1 0.0 copy-start.2
  0.1 0.9 %copy-done = bf16[64,16,128]{2,1,0:T(8,128)(2,1)S(1)} copy-done((bf16[64,16,128]{2,1,0:T(8,128)(2,1)S(1)}, bf16[64,16,128]{2,1,0:T(8,128)(2,1)}, u32[]{:S(2)}) %copy-start) | copy-done | bytes 262168
  1.0 0.0 copy-done.3
  1.0 0.0 copy-done.1
  1.0 0.0 copy-done.2
  1.0 0.0 copy-start.7
  1.0 0.1 edge_rows.1
  1.1 0.0 copy-done.4
  1.1 0.0 copy-done.5
  1.2 0.1 copy-done.6
  1.2 0.6 %copy-done.7 = bf16[2,128,128]{2,1,0:T(8,128)(2,1)S(1)} copy-done((bf16[2,128,128]{2,1,0:T(8,128)(2,1)S(1)}, bf16[2,128,128]{2,1,0:T(8,128)(2,1)}, u32[]{:S(2)}) %copy-start.7) | copy-done | bytes 65560
  1.9 2.9 %conditional.1 = ((bf16[8,16,128]{2,1,0:T(8,128)(2,1)S(1)}, bf16[8,16,128]{2,1,0:T(8,128)(2,1)S(1)}, f32[512,128]{1,0:T(8,128)S(1)}, f32[512,128]{1,0:T(8,128)S(...) conditional(s32[]{:T(128)} %convert_element_type.3, ...), branch_computations={%region_0.0_spmd, %region_1.0_spmd} | conditional | flops 4000000000 | bytes 1048584 | solution.py:392
  1.9 2.9 %first.1 = (bf16[8,16,128]{2,1,0:T(8,128)(2,1)S(1)}, bf16[8,16,128]{2,1,0:T(8,128)(2,1)S(1)}, f32[512,128]{1,0:T(8,128)S(1)}, f32[512,128]{1,0:T(8,128)S(1)}, bf...) custom-call(bf16[64,16,128]{2,1,0:T(8,128)(2,1)S(1)} %get-tuple-elem, ...), custom_call_target="tpu_custom_call", output_to_operand_aliasing={{0}: (8, {}), {1}: (9, {})} | custom-call | flops 4000000000 | bytes 1048576 | tf_op jit(solution)/shard_map/cond/branch_1_fun/first/pallas_call | solution.py:360
  4.8 5.4 %collective-permute-start = (bf16[8,16,128]{2,1,0:T(8,128)(2,1)S(1)}, bf16[8,16,128]{2,1,0:T(8,128)(2,1)S(1)}, u32[]{:S(2)}, u32[]{:S(2)}) collective-permute-start(bf16[8,16,128]{2,1,0:T(8,128)(2,1)S(1)} %get-tuple-element.85), channel_id=1, source_target_pairs={{16,32},{48,64},{80,96},{112,128},{144,160},{176,192},{208,224},{2... | collective-permute-start | bytes 98312 | tf_op jit(solution)/shard_map/ppermute | solution.py:28
  10.2 6.4 %collective-permute-start.1 = (bf16[8,16,128]{2,1,0:T(8,128)(2,1)S(1)}, bf16[8,16,128]{2,1,0:T(8,128)(2,1)S(1)}, u32[]{:S(2)}, u32[]{:S(2)}) collective-permute-start(bf16[8,16,128]{2,1,0:T(8,128)(2,1)S(1)} %get-tuple-element.86), channel_id=1, source_target_pairs={{0,16},{32,48},{64,80},{96,112},{128,144},{160,176},{192,208},{224... | collective-permute-start | bytes 98312 | tf_op jit(solution)/shard_map/ppermute | solution.py:28
  16.6 0.0 collective-permute-done.rows_odd_ref
  16.6 0.8 %collective-permute-done.1.rows_even_ref = bf16[8,16,128]{2,1,0:T(8,128)(2,1)S(1)} collective-permute-done((bf16[8,16,128]{2,1,0:T(8,128)(2,1)S(1)}, bf16[8,16,128]{2,1,0:T(8,128)(2,1)S(1)}, u32[]{:S(2)}, u32[]{:S(2)}) %collective-permute-start.1) | collective-permute-done | bytes 32800 | tf_op jit(solution)/shard_map/ppermute | solution.py:28
  17.4 1.5 %halo.1 = (bf16[64,128]{1,0:T(8,128)(2,1)S(1)}, bf16[64,128]{1,0:T(8,128)(2,1)S(1)}, bf16[288,128]{1,0:T(8,128)(2,1)S(1)}, bf16[288,128]{1,0:T(8,128)(2,1)S(1)}) custom-call(bf16[8,16,128]{2,1,0:T(8,128)(2,1)S(1)} %collective-permute-done.rows_odd_ref, bf16[8,16,128]{2,1,0:T(8,128)(2,1)S(1)} %collective-permute-done.1.rows_even_ref, ...), custom_call_target="tpu_custom_call" | custom-call | flops 1000000000 | bytes 1048576 | tf_op jit(solution)/shard_map/halo/pallas_call | solution.py:360
  19.0 7.3 %collective-permute-start.2 = (bf16[288,128]{1,0:T(8,128)(2,1)S(1)}, bf16[288,128]{1,0:T(8,128)(2,1)S(1)}, u32[]{:S(2)}, u32[]{:S(2)}) collective-permute-start(bf16[288,128]{1,0:T(8,128)(2,1)S(1)} %get-tuple-element.93), channel_id=1, source_target_pairs={{1,2},{3,4},{5,6},{7,8},{9,10},{11,12},{13,14},{15,0},{2,1},{4,3},... | collective-permute-start | bytes 221192 | tf_op jit(solution)/shard_map/ppermute | solution.py:28
  26.2 1.9 %collective-permute-start.3 = (bf16[288,128]{1,0:T(8,128)(2,1)S(1)}, bf16[288,128]{1,0:T(8,128)(2,1)S(1)}, u32[]{:S(2)}, u32[]{:S(2)}) collective-permute-start(bf16[288,128]{1,0:T(8,128)(2,1)S(1)} %get-tuple-element.94), channel_id=1, source_target_pairs={{0,1},{2,3},{4,5},{6,7},{8,9},{10,11},{12,13},{14,15},{1,0},{3,2},... | collective-permute-start | bytes 221192 | tf_op jit(solution)/shard_map/ppermute | solution.py:28
  28.2 1.7 %middle.1 = (f32[512,128]{1,0:T(8,128)S(1)}, f32[64,512]{1,0:T(8,128)S(1)}, f32[64,512]{1,0:T(8,128)S(1)}, bf16[256,128]{1,0:T(8,128)(2,1)S(1)}, bf16[256,256]{1,0:T(8,128)(2,1)S(1)}) custom-call(f32[512,128]{1,0:T(8,128)S(1)} %get-tuple-element.95.fa_ref, bf16[512,128]{1,0:T(8,128)(2,1)S(1)} %get-tuple-element.96.na_ref, ...), custom_call_target="tpu_custom_call" | custom-call | flops 2000000000 | bytes 1048576 | tf_op jit(solution)/shard_map/middle/pallas_call | solution.py:360
  29.9 0.0 collective-permute-done.2.cols_odd_ref
  29.9 1.4 %collective-permute-done.3.cols_even_ref = bf16[288,128]{1,0:T(8,128)(2,1)S(1)} collective-permute-done((bf16[288,128]{1,0:T(8,128)(2,1)S(1)}, bf16[288,128]{1,0:T(8,128)(2,1)S(1)}, u32[]{:S(2)}, u32[]{:S(2)}) %collective-permute-start.3) | collective-permute-done | bytes 73760 | tf_op jit(solution)/shard_map/ppermute | solution.py:28
  31.3 2.4 %outer.1 = f32[64,16,128]{2,1,0:T(8,128)} custom-call(f32[512,128]{1,0:T(8,128)S(1)} %get-tuple-element.83.fb_ref, bf16[512,128]{1,0:T(8,128)(2,1)S(1)} %get-tuple-element.84.nb_ref, bf16[64,128]{1,0:T(8,128)(2,1)S(1)} %get-tuple-element.92.vb_ref, bf16[288,128]{1,0:T(8,128)(2,1)S(1)} %collective-permute-done.2.cols_odd_ref, ...), custom_call_target="tpu_custom_call" | custom-call | flops 2000000000 | bytes 1048576 | tf_op jit(solution)/shard_map/outer/pallas_call | solution.py:360
  (2 shorter events, 0.0 us)
Async XLA Ops:
  0.0 0.9 %copy-start = (bf16[64,16,128]{2,1,0:T(8,128)(2,1)S(1)}, bf16[64,16,128]{2,1,0:T(8,128)(2,1)}, u32[]{:S(2)}) copy-start(bf16[64,16,128]{2,1,0:T(8,128)(2,1)} %refs_0_.1) | copy-start | bytes 786436
  0.0 1.0 %copy-start.3 = (f32[2,128]{1,0:T(2,128)S(1)}, f32[2,128]{1,0:T(2,128)}, u32[]{:S(2)}) copy-start(f32[2,128]{1,0:T(2,128)} %hg_ref.7) | copy-start | bytes 3076
  0.0 1.1 %copy-start.4 = (bf16[2,128,512]{2,1,0:T(8,128)(2,1)S(1)}, bf16[2,128,512]{2,1,0:T(8,128)(2,1)}, u32[]{:S(2)}) copy-start(bf16[2,128,512]{2,1,0:T(8,128)(2,1)} %we_ref.5) | copy-start | bytes 786436
  0.0 1.1 %copy-start.5 = (bf16[2,512,128]{2,1,0:T(8,128)(2,1)S(1)}, bf16[2,512,128]{2,1,0:T(8,128)(2,1)}, u32[]{:S(2)}) copy-start(bf16[2,512,128]{2,1,0:T(8,128)(2,1)} %ws_ref.5) | copy-start | bytes 786436
  0.0 1.2 %copy-start.6 = (bf16[2,128,384]{2,1,0:T(8,128)(2,1)S(1)}, bf16[2,128,384]{2,1,0:T(8,128)(2,1)}, u32[]{:S(2)}) copy-start(bf16[2,128,384]{2,1,0:T(8,128)(2,1)} %w_ref.1) | copy-start | bytes 589828
  0.1 0.9 %copy-start.1 = (f32[2,4,225]{2,1,0:T(4,128)S(1)}, f32[2,4,225]{2,1,0:T(4,128)}, u32[]{:S(2)}) copy-start(f32[2,4,225]{2,1,0:T(4,128)} %pb_ref.3) | copy-start | bytes 21604
  0.1 0.9 %copy-start.2 = (f32[2,128]{1,0:T(2,128)S(1)}, f32[2,128]{1,0:T(2,128)}, u32[]{:S(2)}) copy-start(f32[2,128]{1,0:T(2,128)} %ag_ref.3) | copy-start | bytes 3076
  1.0 0.9 %copy-start.7 = (bf16[2,128,128]{2,1,0:T(8,128)(2,1)S(1)}, bf16[2,128,128]{2,1,0:T(8,128)(2,1)}, u32[]{:S(2)}) copy-start(bf16[2,128,128]{2,1,0:T(8,128)(2,1)} %wo_ref.5) | copy-start | bytes 196612
  4.8 11.8 %collective-permute-start = (bf16[8,16,128]{2,1,0:T(8,128)(2,1)S(1)}, bf16[8,16,128]{2,1,0:T(8,128)(2,1)S(1)}, u32[]{:S(2)}, u32[]{:S(2)}) collective-permute-start(bf16[8,16,128]{2,1,0:T(8,128)(2,1)S(1)} %get-tuple-element.85), channel_id=1, source_target_pairs={{16,32},{48,64},{80,96},{112,128},{144,160},{176,192},{208,224},{2... | collective-permute-start | bytes 98312 | tf_op jit(solution)/shard_map/ppermute | solution.py:28
  10.2 7.2 %collective-permute-start.1 = (bf16[8,16,128]{2,1,0:T(8,128)(2,1)S(1)}, bf16[8,16,128]{2,1,0:T(8,128)(2,1)S(1)}, u32[]{:S(2)}, u32[]{:S(2)}) collective-permute-start(bf16[8,16,128]{2,1,0:T(8,128)(2,1)S(1)} %get-tuple-element.86), channel_id=1, source_target_pairs={{0,16},{32,48},{64,80},{96,112},{128,144},{160,176},{192,208},{224... | collective-permute-start | bytes 98312 | tf_op jit(solution)/shard_map/ppermute | solution.py:28
  19.0 10.9 %collective-permute-start.2 = (bf16[288,128]{1,0:T(8,128)(2,1)S(1)}, bf16[288,128]{1,0:T(8,128)(2,1)S(1)}, u32[]{:S(2)}, u32[]{:S(2)}) collective-permute-start(bf16[288,128]{1,0:T(8,128)(2,1)S(1)} %get-tuple-element.93), channel_id=1, source_target_pairs={{1,2},{3,4},{5,6},{7,8},{9,10},{11,12},{13,14},{15,0},{2,1},{4,3},... | collective-permute-start | bytes 221192 | tf_op jit(solution)/shard_map/ppermute | solution.py:28
  26.2 5.1 %collective-permute-start.3 = (bf16[288,128]{1,0:T(8,128)(2,1)S(1)}, bf16[288,128]{1,0:T(8,128)(2,1)S(1)}, u32[]{:S(2)}, u32[]{:S(2)}) collective-permute-start(bf16[288,128]{1,0:T(8,128)(2,1)S(1)} %get-tuple-element.94), channel_id=1, source_target_pairs={{0,1},{2,3},{4,5},{6,7},{8,9},{10,11},{12,13},{14,15},{1,0},{3,2},... | collective-permute-start | bytes 221192 | tf_op jit(solution)/shard_map/ppermute | solution.py:28

commit v7 on v6

--- a/solution.py
+++ b/solution.py
@@ -218,7 +218,7 @@
 
 
 def first_kernel(*refs):
-    own_block(*refs[0:8], *refs[12:])
+    own_block(*refs[0:8], *refs[10:])
 
 
 def nothing_kernel(*refs):
@@ -232,7 +232,7 @@
 
 
 def halo_kernel(
-    rows_odd_ref, rows_even_ref, own_right_ref, own_left_ref, bias_ref, wqv_ref, wk_ref, wo_ref, we_ref, ws_ref, ag_ref, hg_ref,
+    rows_even_ref, rows_odd_ref, own_right_ref, own_left_ref, bias_ref, wqv_ref, wk_ref, wo_ref, we_ref, ws_ref, ag_ref, hg_ref,
     na_ref, nb_ref, cols_odd_ref, cols_even_ref,
 ):
     row_odd = lax.rem(lax.axis_index("gy"), 2) == 1
@@ -384,19 +384,20 @@
     )
 
     def run(*operands):
-        return call(first_kernel, "first", operands, rows + kept, (), 4 * 10**9, {8: 0, 9: 1})
+        return call(first_kernel, "first", operands, rows[0:1] + kept, (), 4 * 10**9, {8: 0})
 
     def skip(*operands):
-        return call(nothing_kernel, "nothing", operands[8:10], rows + kept, (), 0, {0: 0, 1: 1})
-
-    odd, even, *state = lax.cond(goes_first(), run, skip, *weights, odd, even)
-    even, odd = swap(even, "gy", 0), swap(odd, "gy", 1)
+        return call(nothing_kernel, "nothing", operands[8:9], rows[0:1] + kept, (), 0, {0: 0})
+
+    even = swap(even, "gy", 0)
+    odd, *state = lax.cond(goes_first(), run, skip, *weights, odd)
+    odd = swap(odd, "gy", 1)
     state = call(
         second_kernel, "second", (*weights, *state), kept, (), 4 * 10**9, {8 + i: i for i in range(9)}
     )
     fa, fb, na, nb, right, left, bias, wqv, wk = state
     va, vb, odd, even = call(
-        halo_kernel, "halo", (odd, even, right, left, bias, wqv, wk, ow, ew, sw, ag, hg),
+        halo_kernel, "halo", (even, odd, right, left, bias, wqv, wk, ow, ew, sw, ag, hg),
         [((64, C), BF16)] * 2 + [((n // 2 + 32, C), BF16)] * 2, (), 10**9,
     )
     odd, even = swap(odd, "gx", 1), swap(even, "gx", 0)

time: 34 us -> 33.5 us (0.985)
  the two profiles are of different devices: /device:TPU:1 before, /device:TPU:2 now
where the time goes in v7:
time: 33.5 us; the launch traced here: 33.2 us
  starting transfers between devices  19.2 us (57%)
  Pallas kernels  8.76 us (26%)
  waiting for transfers between devices  4.14 us (12%)
  local copies, waits for them, and re-layouts  0.95 us (3%)
    ppermute x4, starting transfers between devices, swap(): return lax.ppermute(x, axis, there + [(b, a) for a, b in there])  19.2 us
    pallas_call x7, Pallas kernels, call(): pl.pallas_call(kernel, out_shape=shapes, in_specs=vmem(len(operands)), ou...  8.76 us
    ppermute x4, waiting for transfers between devices, swap(): return lax.ppermute(x, axis, there + [(b, a) for a, b in there])  4.14 us
    unnamed x16, local copies, waits for them, and re-layouts  0.95 us
  transfers between devices with their start and end apart: 4, of which 2 were waited for; matrix products, arithmetic and copies ran while one was open for 0% of the time, Pallas kernels for 14%

profile of v7, /device:TPU:2, one launch (start us, length us, event | category | flops | bytes accessed | tf_op | source)
XLA Modules:
  0.0 33.2 jit_solution(15082044156211681023)
XLA Ops:
  0.0 0.0 copy-start.3
  0.0 0.0 copy-start.1
  0.0 0.0 copy-start.2
  0.0 0.0 copy-start
  0.0 0.0 copy-start.5
  0.0 0.0 copy-start.6
  0.0 0.0 copy-start.7
  0.1 0.6 %copy-done.3 = f32[2,128]{1,0:T(2,128)S(1)} copy-done((f32[2,128]{1,0:T(2,128)S(1)}, f32[2,128]{1,0:T(2,128)}, u32[]{:S(2)}) %copy-start.3) | copy-done | bytes 1048
  0.7 0.0 copy-done.1
  0.7 0.0 copy-done.2
  0.7 0.3 copy-done
  1.0 0.0 copy-start.4
  1.0 0.1 edge_rows.1
  1.1 1.9 %collective-permute-start = (bf16[8,16,128]{2,1,0:T(8,128)(2,1)S(1)}, bf16[8,16,128]{2,1,0:T(8,128)(2,1)S(1)}, u32[]{:S(2)}, u32[]{:S(2)}) collective-permute-start(bf16[8,16,128]{2,1,0:T(8,128)(2,1)S(1)} %get-tuple-element.75), channel_id=1, source_target_pairs={{0,16},{32,48},{64,80},{96,112},{128,144},{160,176},{192,208},{224... | collective-permute-start | bytes 98312 | tf_op jit(solution)/shard_map/ppermute | solution.py:28
  3.1 0.0 copy-done.5
  3.1 0.0 copy-done.6
  3.1 0.0 copy-done.7
  3.1 0.0 copy-done.4
  3.1 2.9 %conditional.1 = (bf16[8,16,128]{2,1,0:T(8,128)(2,1)S(1)}, f32[512,128]{1,0:T(8,128)S(1)}, f32[512,128]{1,0:T(8,128)S(1)}, bf16[512,128]{1,0:T(8,128)(2,1)S(1)},...) conditional(s32[]{:T(128)} %convert_element_type.3, ...), branch_computations={%region_0.0_spmd, %region_1.0_spmd} | conditional | flops 4000000000 | bytes 1114192 | solution.py:393
  3.1 2.9 %first.1 = (bf16[8,16,128]{2,1,0:T(8,128)(2,1)S(1)}, f32[512,128]{1,0:T(8,128)S(1)}, f32[512,128]{1,0:T(8,128)S(1)}, bf16[512,128]{1,0:T(8,128)(2,1)S(1)}, bf16[...) custom-call(bf16[64,16,128]{2,1,0:T(8,128)(2,1)S(1)} %get-tuple-elem, ...), custom_call_target="tpu_custom_call", output_to_operand_aliasing={{0}: (8, {})} | custom-call | flops 4000000000 | bytes 1048576 | tf_op jit(solution)/shard_map/cond/branch_1_fun/first/pallas_call | solution.py:360
  6.1 8.1 %collective-permute-start.1 = (bf16[8,16,128]{2,1,0:T(8,128)(2,1)S(1)}, bf16[8,16,128]{2,1,0:T(8,128)(2,1)S(1)}, u32[]{:S(2)}, u32[]{:S(2)}) collective-permute-start(bf16[8,16,128]{2,1,0:T(8,128)(2,1)S(1)} %get-tuple-element.76), channel_id=1, source_target_pairs={{16,32},{48,64},{80,96},{112,128},{144,160},{176,192},{208,224},{2... | collective-permute-start | bytes 98312 | tf_op jit(solution)/shard_map/ppermute | solution.py:28
  14.2 0.0 collective-permute-done.rows_even_ref
  14.2 1.5 %collective-permute-done.1.rows_odd_ref = bf16[8,16,128]{2,1,0:T(8,128)(2,1)S(1)} collective-permute-done((bf16[8,16,128]{2,1,0:T(8,128)(2,1)S(1)}, bf16[8,16,128]{2,1,0:T(8,128)(2,1)S(1)}, u32[]{:S(2)}, u32[]{:S(2)}) %collective-permute-start.1) | collective-permute-done | bytes 32800 | tf_op jit(solution)/shard_map/ppermute | solution.py:28
  15.8 1.5 %halo.1 = (bf16[64,128]{1,0:T(8,128)(2,1)S(1)}, bf16[64,128]{1,0:T(8,128)(2,1)S(1)}, bf16[288,128]{1,0:T(8,128)(2,1)S(1)}, bf16[288,128]{1,0:T(8,128)(2,1)S(1)}) custom-call(bf16[8,16,128]{2,1,0:T(8,128)(2,1)S(1)} %collective-permute-done.rows_even_ref, bf16[8,16,128]{2,1,0:T(8,128)(2,1)S(1)} %collective-permute-done.1.rows_odd_ref, ...), custom_call_target="tpu_custom_call" | custom-call | flops 1000000000 | bytes 1048576 | tf_op jit(solution)/shard_map/halo/pallas_call | solution.py:360
  17.3 7.2 %collective-permute-start.2 = (bf16[288,128]{1,0:T(8,128)(2,1)S(1)}, bf16[288,128]{1,0:T(8,128)(2,1)S(1)}, u32[]{:S(2)}, u32[]{:S(2)}) collective-permute-start(bf16[288,128]{1,0:T(8,128)(2,1)S(1)} %get-tuple-element.83), channel_id=1, source_target_pairs={{1,2},{3,4},{5,6},{7,8},{9,10},{11,12},{13,14},{15,0},{2,1},{4,3},... | collective-permute-start | bytes 221192 | tf_op jit(solution)/shard_map/ppermute | solution.py:28
  24.5 1.9 %collective-permute-start.3 = (bf16[288,128]{1,0:T(8,128)(2,1)S(1)}, bf16[288,128]{1,0:T(8,128)(2,1)S(1)}, u32[]{:S(2)}, u32[]{:S(2)}) collective-permute-start(bf16[288,128]{1,0:T(8,128)(2,1)S(1)} %get-tuple-element.84), channel_id=1, source_target_pairs={{0,1},{2,3},{4,5},{6,7},{8,9},{10,11},{12,13},{14,15},{1,0},{3,2},... | collective-permute-start | bytes 221192 | tf_op jit(solution)/shard_map/ppermute | solution.py:28
  26.5 1.7 %middle.1 = (f32[512,128]{1,0:T(8,128)S(1)}, f32[64,512]{1,0:T(8,128)S(1)}, f32[64,512]{1,0:T(8,128)S(1)}, bf16[256,128]{1,0:T(8,128)(2,1)S(1)}, bf16[256,256]{1,0:T(8,128)(2,1)S(1)}) custom-call(f32[512,128]{1,0:T(8,128)S(1)} %get-tuple-element.85.fa_ref, bf16[512,128]{1,0:T(8,128)(2,1)S(1)} %get-tuple-element.86.na_ref, ...), custom_call_target="tpu_custom_call" | custom-call | flops 2000000000 | bytes 1048576 | tf_op jit(solution)/shard_map/middle/pallas_call | solution.py:360
  28.2 0.0 collective-permute-done.2.cols_odd_ref
  28.2 2.6 %collective-permute-done.3.cols_even_ref = bf16[288,128]{1,0:T(8,128)(2,1)S(1)} collective-permute-done((bf16[288,128]{1,0:T(8,128)(2,1)S(1)}, bf16[288,128]{1,0:T(8,128)(2,1)S(1)}, u32[]{:S(2)}, u32[]{:S(2)}) %collective-permute-start.3) | collective-permute-done | bytes 73760 | tf_op jit(solution)/shard_map/ppermute | solution.py:28
  30.8 2.4 %outer.1 = f32[64,16,128]{2,1,0:T(8,128)} custom-call(f32[512,128]{1,0:T(8,128)S(1)} %get-tuple-element.73.fb_ref, bf16[512,128]{1,0:T(8,128)(2,1)S(1)} %get-tuple-element.74.nb_ref, bf16[64,128]{1,0:T(8,128)(2,1)S(1)} %get-tuple-element.82.vb_ref, bf16[288,128]{1,0:T(8,128)(2,1)S(1)} %collective-permute-done.2.cols_odd_ref, ...), custom_call_target="tpu_custom_call" | custom-call | flops 2000000000 | bytes 1048576 | tf_op jit(solution)/shard_map/outer/pallas_call | solution.py:360
  (3 shorter events, 0.0 us)
Async XLA Ops:
  0.0 0.7 %copy-start.3 = (f32[2,128]{1,0:T(2,128)S(1)}, f32[2,128]{1,0:T(2,128)}, u32[]{:S(2)}) copy-start(f32[2,128]{1,0:T(2,128)} %hg_ref.7) | copy-start | bytes 3076
  0.0 0.7 %copy-start.1 = (f32[2,4,225]{2,1,0:T(4,128)S(1)}, f32[2,4,225]{2,1,0:T(4,128)}, u32[]{:S(2)}) copy-start(f32[2,4,225]{2,1,0:T(4,128)} %pb_ref.3) | copy-start | bytes 21604
  0.0 0.7 %copy-start.2 = (f32[2,128]{1,0:T(2,128)S(1)}, f32[2,128]{1,0:T(2,128)}, u32[]{:S(2)}) copy-start(f32[2,128]{1,0:T(2,128)} %ag_ref.3) | copy-start | bytes 3076
  0.0 1.0 %copy-start = (bf16[64,16,128]{2,1,0:T(8,128)(2,1)S(1)}, bf16[64,16,128]{2,1,0:T(8,128)(2,1)}, u32[]{:S(2)}) copy-start(bf16[64,16,128]{2,1,0:T(8,128)(2,1)} %refs_0_.2) | copy-start | bytes 786436
  0.0 3.1 %copy-start.5 = (bf16[2,512,128]{2,1,0:T(8,128)(2,1)S(1)}, bf16[2,512,128]{2,1,0:T(8,128)(2,1)}, u32[]{:S(2)}) copy-start(bf16[2,512,128]{2,1,0:T(8,128)(2,1)} %ws_ref.5) | copy-start | bytes 786436
  0.0 3.1 %copy-start.6 = (bf16[2,128,384]{2,1,0:T(8,128)(2,1)S(1)}, bf16[2,128,384]{2,1,0:T(8,128)(2,1)}, u32[]{:S(2)}) copy-start(bf16[2,128,384]{2,1,0:T(8,128)(2,1)} %w_ref.1) | copy-start | bytes 589828
  0.0 3.1 %copy-start.7 = (bf16[2,128,128]{2,1,0:T(8,128)(2,1)S(1)}, bf16[2,128,128]{2,1,0:T(8,128)(2,1)}, u32[]{:S(2)}) copy-start(bf16[2,128,128]{2,1,0:T(8,128)(2,1)} %wo_ref.5) | copy-start | bytes 196612
  1.0 2.1 %copy-start.4 = (bf16[2,128,512]{2,1,0:T(8,128)(2,1)S(1)}, bf16[2,128,512]{2,1,0:T(8,128)(2,1)}, u32[]{:S(2)}) copy-start(bf16[2,128,512]{2,1,0:T(8,128)(2,1)} %we_ref.5) | copy-start | bytes 786436
  1.1 13.1 %collective-permute-start = (bf16[8,16,128]{2,1,0:T(8,128)(2,1)S(1)}, bf16[8,16,128]{2,1,0:T(8,128)(2,1)S(1)}, u32[]{:S(2)}, u32[]{:S(2)}) collective-permute-start(bf16[8,16,128]{2,1,0:T(8,128)(2,1)S(1)} %get-tuple-element.75), channel_id=1, source_target_pairs={{0,16},{32,48},{64,80},{96,112},{128,144},{160,176},{192,208},{224... | collective-permute-start | bytes 98312 | tf_op jit(solution)/shard_map/ppermute | solution.py:28
  6.1 9.7 %collective-permute-start.1 = (bf16[8,16,128]{2,1,0:T(8,128)(2,1)S(1)}, bf16[8,16,128]{2,1,0:T(8,128)(2,1)S(1)}, u32[]{:S(2)}, u32[]{:S(2)}) collective-permute-start(bf16[8,16,128]{2,1,0:T(8,128)(2,1)S(1)} %get-tuple-element.76), channel_id=1, source_target_pairs={{16,32},{48,64},{80,96},{112,128},{144,160},{176,192},{208,224},{2... | collective-permute-start | bytes 98312 | tf_op jit(solution)/shard_map/ppermute | solution.py:28
  17.3 10.9 %collective-permute-start.2 = (bf16[288,128]{1,0:T(8,128)(2,1)S(1)}, bf16[288,128]{1,0:T(8,128)(2,1)S(1)}, u32[]{:S(2)}, u32[]{:S(2)}) collective-permute-start(bf16[288,128]{1,0:T(8,128)(2,1)S(1)} %get-tuple-element.83), channel_id=1, source_target_pairs={{1,2},{3,4},{5,6},{7,8},{9,10},{11,12},{13,14},{15,0},{2,1},{4,3},... | collective-permute-start | bytes 221192 | tf_op jit(solution)/shard_map/ppermute | solution.py:28
  24.5 6.2 %collective-permute-start.3 = (bf16[288,128]{1,0:T(8,128)(2,1)S(1)}, bf16[288,128]{1,0:T(8,128)(2,1)S(1)}, u32[]{:S(2)}, u32[]{:S(2)}) collective-permute-start(bf16[288,128]{1,0:T(8,128)(2,1)S(1)} %get-tuple-element.84), channel_id=1, source_target_pairs={{0,1},{2,3},{4,5},{6,7},{8,9},{10,11},{12,13},{14,15},{1,0},{3,2},... | collective-permute-start | bytes 221192 | tf_op jit(solution)/shard_map/ppermute | solution.py:28

commit v8 on v7

--- a/solution.py
+++ b/solution.py
@@ -20,6 +20,11 @@
 NT = (((1,), (1,)), ((), ()))
 TN = (((0,), (0,)), ((), ()))
 CHUNK = 256
+
+
+def shift(x, axis, by):
+    length = lax.axis_size(axis)
+    return lax.ppermute(x, axis, [(i, (i + by) % length) for i in range(length)])
 
 
 def swap(x, axis, first):
@@ -174,7 +179,7 @@
 
 def goes_first():
     row, rows = lax.axis_index("gy"), lax.axis_size("gy")
-    return lax.rem(row, rows // 2) < rows // 4
+    return lax.rem(row, rows // 2) < rows // 8
 
 
 def own_block(
@@ -200,16 +205,15 @@
     right_ref[...], left_ref[...] = edges(nb)
 
 
-def parity_kernel(out_ref):
-    out_ref[...] = jnp.full(out_ref.shape, lax.rem(lax.axis_index("gy"), 2), jnp.int32)
-
-
-def edge_rows_kernel(x_ref, parity_ref, ag_ref, pb_ref, hg_ref, odd_ref, even_ref, sems):
+def start_kernel(out_ref):
+    out_ref[...] = jnp.zeros(out_ref.shape, jnp.int32)
+
+
+def edge_rows_kernel(x_ref, start_ref, ag_ref, pb_ref, hg_ref, last_ref, first_ref, sems):
     bottom = x_ref.shape[0] - WIN
-    is_odd = parity_ref[0, 0]
     copies = [
-        pltpu.make_async_copy(x_ref.at[pl.ds(is_odd * bottom, WIN)], odd_ref, sems.at[0]),
-        pltpu.make_async_copy(x_ref.at[pl.ds((1 - is_odd) * bottom, WIN)], even_ref, sems.at[1]),
+        pltpu.make_async_copy(x_ref.at[pl.ds(bottom, WIN)], last_ref, sems.at[0]),
+        pltpu.make_async_copy(x_ref.at[pl.ds(0, WIN)], first_ref, sems.at[1]),
     ]
     for copy in copies:
         copy.start()
@@ -232,14 +236,10 @@
 
 
 def halo_kernel(
-    rows_even_ref, rows_odd_ref, own_right_ref, own_left_ref, bias_ref, wqv_ref, wk_ref, wo_ref, we_ref, ws_ref, ag_ref, hg_ref,
+    up_ref, down_ref, own_right_ref, own_left_ref, bias_ref, wqv_ref, wk_ref, wo_ref, we_ref, ws_ref, ag_ref, hg_ref,
     na_ref, nb_ref, cols_odd_ref, cols_even_ref,
 ):
-    row_odd = lax.rem(lax.axis_index("gy"), 2) == 1
-    rows_odd, rows_even = rows_odd_ref[...].astype(F32), rows_even_ref[...].astype(F32)
-    down = jnp.where(row_odd, rows_odd, rows_even)
-    up = jnp.where(row_odd, rows_even, rows_odd)
-    z = cat(windows_of(down) + windows_of(up))
+    z = cat(windows_of(down_ref[...]) + windows_of(up_ref[...]))
     normed = layer_norm(z, ag_ref[0:1, :]).astype(BF16)
     keys = side_by_side(normed, wk_ref[...])
     values = dot(wqv_ref[128:256, :], normed, NT).astype(BF16)
@@ -378,9 +378,9 @@
     weights = (x, tw, ow, ew, sw, ag, pb, hg)
     kept = [((n, C), F32)] * 2 + [((n, C), BF16)] * 2 + [((n // 2, C), BF16)] * 2 + [table] + prepared
     rows = [((WIN, breadth, C), BF16)] * 2
-    (parity,) = call(parity_kernel, "parity", (), [((8, 128), jnp.int32)], (), 4 * 10**10)
-    odd, even = call(
-        edge_rows_kernel, "edge_rows", (x, parity, ag, pb, hg), rows, [pltpu.SemaphoreType.DMA((2,))]
+    (start,) = call(start_kernel, "start", (), [((8, 128), jnp.int32)], (), 4 * 10**10)
+    last, first = call(
+        edge_rows_kernel, "edge_rows", (x, start, ag, pb, hg), rows, [pltpu.SemaphoreType.DMA((2,))]
     )
 
     def run(*operands):
@@ -389,15 +389,15 @@
     def skip(*operands):
         return call(nothing_kernel, "nothing", operands[8:9], rows[0:1] + kept, (), 0, {0: 0})
 
-    even = swap(even, "gy", 0)
-    odd, *state = lax.cond(goes_first(), run, skip, *weights, odd)
-    odd = swap(odd, "gy", 1)
+    up = shift(last, "gy", 1)
+    first, *state = lax.cond(goes_first(), run, skip, *weights, first)
+    down = shift(first, "gy", -1)
     state = call(
         second_kernel, "second", (*weights, *state), kept, (), 4 * 10**9, {8 + i: i for i in range(9)}
     )
     fa, fb, na, nb, right, left, bias, wqv, wk = state
     va, vb, odd, even = call(
-        halo_kernel, "halo", (even, odd, right, left, bias, wqv, wk, ow, ew, sw, ag, hg),
+        halo_kernel, "halo", (up, down, right, left, bias, wqv, wk, ow, ew, sw, ag, hg),
         [((64, C), BF16)] * 2 + [((n // 2 + 32, C), BF16)] * 2, (), 10**9,
     )
     odd, even = swap(odd, "gx", 1), swap(even, "gx", 0)

time: 33.5 us -> 32.7 us (0.976)
  starting transfers between devices: 19.2 us -> 18.5 us
    ppermute x4 -> x2, starting transfers between devices: 19.2 us -> 9.15 us  [swap(): return lax.ppermute(x, axis, there + [(b, a) for a, b in there])]
    ppermute x0 -> x2, starting transfers between devices: none -> 9.38 us  [shift(): lax.ppermute(x, axis, [(i, (i + by) % length) for i in range(length)])]
    ppermute x4 -> x2, waiting for transfers between devices: 4.14 us -> 2.6 us  [swap(): return lax.ppermute(x, axis, there + [(b, a) for a, b in there])]
    ppermute x0 -> x2, waiting for transfers between devices: none -> 1.53 us  [shift(): lax.ppermute(x, axis, [(i, (i + by) % length) for i in range(length)])]
where the time goes in v8:
time: 32.7 us; the launch traced here: 32.5 us
  starting transfers between devices  18.5 us (57%)
  Pallas kernels  8.68 us (27%)
  waiting for transfers between devices  4.13 us (13%)
  local copies, waits for them, and re-layouts  0.96 us (3%)
    ppermute x2, starting transfers between devices, shift(): lax.ppermute(x, axis, [(i, (i + by) % length) for i in range(length)])  9.38 us
    ppermute x2, starting transfers between devices, swap(): return lax.ppermute(x, axis, there + [(b, a) for a, b in there])  9.15 us
    pallas_call x7, Pallas kernels, call(): pl.pallas_call(kernel, out_shape=shapes, in_specs=vmem(len(operands)), ou...  8.68 us
    ppermute x2, waiting for transfers between devices, swap(): return lax.ppermute(x, axis, there + [(b, a) for a, b in there])  2.6 us
    ppermute x2, waiting for transfers between devices, shift(): lax.ppermute(x, axis, [(i, (i + by) % length) for i in range(length)])  1.53 us
    unnamed x16, local copies, waits for them, and re-layouts  0.96 us
  transfers between devices with their start and end apart: 4, of which 2 were waited for; matrix products, arithmetic and copies ran while one was open for 0% of the time, Pallas kernels for 14%

profile of v8, /device:TPU:2, one launch (start us, length us, event | category | flops | bytes accessed | tf_op | source)
XLA Modules:
  0.0 32.5 jit_solution(7493780312065340382)
XLA Ops:
  0.0 0.0 copy-start.3
  0.0 0.0 copy-start.1
  0.0 0.0 copy-start.2
  0.0 0.0 copy-start
  0.0 0.0 copy-start.5
  0.0 0.0 copy-start.6
  0.0 0.0 copy-start.7
  0.1 0.6 %copy-done.3 = f32[2,128]{1,0:T(2,128)S(1)} copy-done((f32[2,128]{1,0:T(2,128)S(1)}, f32[2,128]{1,0:T(2,128)}, u32[]{:S(2)}) %copy-start.3) | copy-done | bytes 1048
  0.7 0.0 copy-done.1
  0.7 0.0 copy-done.2
  0.7 0.3 copy-done
  1.0 0.0 copy-start.4
  1.0 0.1 edge_rows.1
  1.1 1.9 %collective-permute-start = (bf16[8,16,128]{2,1,0:T(8,128)(2,1)S(1)}, bf16[8,16,128]{2,1,0:T(8,128)(2,1)S(1)}, u32[]{:S(2)}, u32[]{:S(2)}) collective-permute-start(bf16[8,16,128]{2,1,0:T(8,128)(2,1)S(1)} %get-tuple-element.75), channel_id=1, source_target_pairs={{0,16},{16,32},{32,48},{48,64},{64,80},{80,96},{96,112},{112,128},... | collective-permute-start | bytes 98312 | tf_op jit(solution)/shard_map/ppermute | solution.py:27
  3.0 0.0 copy-done.5
  3.0 0.0 copy-done.6
  3.0 0.0 copy-done.7
  3.1 0.0 copy-done.4
  3.1 2.9 %conditional.1 = (bf16[8,16,128]{2,1,0:T(8,128)(2,1)S(1)}, f32[512,128]{1,0:T(8,128)S(1)}, f32[512,128]{1,0:T(8,128)S(1)}, bf16[512,128]{1,0:T(8,128)(2,1)S(1)},...) conditional(s32[]{:T(128)} %convert_element_type.3, ...), branch_computations={%region_0.0_spmd, %region_1.0_spmd} | conditional | flops 4000000000 | bytes 1114192 | solution.py:393
  3.1 2.9 %first.1 = (bf16[8,16,128]{2,1,0:T(8,128)(2,1)S(1)}, f32[512,128]{1,0:T(8,128)S(1)}, f32[512,128]{1,0:T(8,128)S(1)}, bf16[512,128]{1,0:T(8,128)(2,1)S(1)}, bf16[...) custom-call(bf16[64,16,128]{2,1,0:T(8,128)(2,1)S(1)} %get-tuple-elem, ...), custom_call_target="tpu_custom_call", output_to_operand_aliasing={{0}: (8, {})} | custom-call | flops 4000000000 | bytes 1048576 | tf_op jit(solution)/shard_map/cond/branch_1_fun/first/pallas_call | solution.py:360
  6.0 7.5 %collective-permute-start.1 = (bf16[8,16,128]{2,1,0:T(8,128)(2,1)S(1)}, bf16[8,16,128]{2,1,0:T(8,128)(2,1)S(1)}, u32[]{:S(2)}, u32[]{:S(2)}) collective-permute-start(bf16[8,16,128]{2,1,0:T(8,128)(2,1)S(1)} %get-tuple-element.76), channel_id=1, source_target_pairs={{0,496},{16,0},{32,16},{48,32},{64,48},{80,64},{96,80},{112,96},{1... | collective-permute-start | bytes 98312 | tf_op jit(solution)/shard_map/ppermute | solution.py:27
  13.5 0.0 collective-permute-done.up_ref
  13.5 1.5 %collective-permute-done.1.down_ref = bf16[8,16,128]{2,1,0:T(8,128)(2,1)S(1)} collective-permute-done((bf16[8,16,128]{2,1,0:T(8,128)(2,1)S(1)}, bf16[8,16,128]{2,1,0:T(8,128)(2,1)S(1)}, u32[]{:S(2)}, u32[]{:S(2)}) %collective-permute-start.1) | collective-permute-done | bytes 32800 | tf_op jit(solution)/shard_map/ppermute | solution.py:27
  15.1 1.5 %halo.1 = (bf16[64,128]{1,0:T(8,128)(2,1)S(1)}, bf16[64,128]{1,0:T(8,128)(2,1)S(1)}, bf16[288,128]{1,0:T(8,128)(2,1)S(1)}, bf16[288,128]{1,0:T(8,128)(2,1)S(1)}) custom-call(bf16[8,16,128]{2,1,0:T(8,128)(2,1)S(1)} %collective-permute-done.up_ref, bf16[8,16,128]{2,1,0:T(8,128)(2,1)S(1)} %collective-permute-done.1.down_ref, ...), custom_call_target="tpu_custom_call" | custom-call | flops 1000000000 | bytes 1048576 | tf_op jit(solution)/shard_map/halo/pallas_call | solution.py:360
  16.6 7.2 %collective-permute-start.2 = (bf16[288,128]{1,0:T(8,128)(2,1)S(1)}, bf16[288,128]{1,0:T(8,128)(2,1)S(1)}, u32[]{:S(2)}, u32[]{:S(2)}) collective-permute-start(bf16[288,128]{1,0:T(8,128)(2,1)S(1)} %get-tuple-element.83), channel_id=1, source_target_pairs={{1,2},{3,4},{5,6},{7,8},{9,10},{11,12},{13,14},{15,0},{2,1},{4,3},... | collective-permute-start | bytes 221192 | tf_op jit(solution)/shard_map/ppermute | solution.py:33
  23.8 1.9 %collective-permute-start.3 = (bf16[288,128]{1,0:T(8,128)(2,1)S(1)}, bf16[288,128]{1,0:T(8,128)(2,1)S(1)}, u32[]{:S(2)}, u32[]{:S(2)}) collective-permute-start(bf16[288,128]{1,0:T(8,128)(2,1)S(1)} %get-tuple-element.84), channel_id=1, source_target_pairs={{0,1},{2,3},{4,5},{6,7},{8,9},{10,11},{12,13},{14,15},{1,0},{3,2},... | collective-permute-start | bytes 221192 | tf_op jit(solution)/shard_map/ppermute | solution.py:33
  25.7 1.7 %middle.1 = (f32[512,128]{1,0:T(8,128)S(1)}, f32[64,512]{1,0:T(8,128)S(1)}, f32[64,512]{1,0:T(8,128)S(1)}, bf16[256,128]{1,0:T(8,128)(2,1)S(1)}, bf16[256,256]{1,0:T(8,128)(2,1)S(1)}) custom-call(f32[512,128]{1,0:T(8,128)S(1)} %get-tuple-element.85.fa_ref, bf16[512,128]{1,0:T(8,128)(2,1)S(1)} %get-tuple-element.86.na_ref, ...), custom_call_target="tpu_custom_call" | custom-call | flops 2000000000 | bytes 1048576 | tf_op jit(solution)/shard_map/middle/pallas_call | solution.py:360
  27.5 0.0 collective-permute-done.2.cols_odd_ref
  27.5 2.6 %collective-permute-done.3.cols_even_ref = bf16[288,128]{1,0:T(8,128)(2,1)S(1)} collective-permute-done((bf16[288,128]{1,0:T(8,128)(2,1)S(1)}, bf16[288,128]{1,0:T(8,128)(2,1)S(1)}, u32[]{:S(2)}, u32[]{:S(2)}) %collective-permute-start.3) | collective-permute-done | bytes 73760 | tf_op jit(solution)/shard_map/ppermute | solution.py:33
  30.1 2.4 %outer.1 = f32[64,16,128]{2,1,0:T(8,128)} custom-call(f32[512,128]{1,0:T(8,128)S(1)} %get-tuple-element.73.fb_ref, bf16[512,128]{1,0:T(8,128)(2,1)S(1)} %get-tuple-element.74.nb_ref, bf16[64,128]{1,0:T(8,128)(2,1)S(1)} %get-tuple-element.82.vb_ref, bf16[288,128]{1,0:T(8,128)(2,1)S(1)} %collective-permute-done.2.cols_odd_ref, ...), custom_call_target="tpu_custom_call" | custom-call | flops 2000000000 | bytes 1048576 | tf_op jit(solution)/shard_map/outer/pallas_call | solution.py:360
  (3 shorter events, 0.0 us)
Async XLA Ops:
  0.0 0.7 %copy-start.3 = (f32[2,128]{1,0:T(2,128)S(1)}, f32[2,128]{1,0:T(2,128)}, u32[]{:S(2)}) copy-start(f32[2,128]{1,0:T(2,128)} %hg_ref.7) | copy-start | bytes 3076
  0.0 0.7 %copy-start.1 = (f32[2,4,225]{2,1,0:T(4,128)S(1)}, f32[2,4,225]{2,1,0:T(4,128)}, u32[]{:S(2)}) copy-start(f32[2,4,225]{2,1,0:T(4,128)} %pb_ref.3) | copy-start | bytes 21604
  0.0 0.7 %copy-start.2 = (f32[2,128]{1,0:T(2,128)S(1)}, f32[2,128]{1,0:T(2,128)}, u32[]{:S(2)}) copy-start(f32[2,128]{1,0:T(2,128)} %ag_ref.3) | copy-start | bytes 3076
  0.0 1.0 %copy-start = (bf16[64,16,128]{2,1,0:T(8,128)(2,1)S(1)}, bf16[64,16,128]{2,1,0:T(8,128)(2,1)}, u32[]{:S(2)}) copy-start(bf16[64,16,128]{2,1,0:T(8,128)(2,1)} %refs_0_.2) | copy-start | bytes 786436
  0.0 3.0 %copy-start.5 = (bf16[2,512,128]{2,1,0:T(8,128)(2,1)S(1)}, bf16[2,512,128]{2,1,0:T(8,128)(2,1)}, u32[]{:S(2)}) copy-start(bf16[2,512,128]{2,1,0:T(8,128)(2,1)} %ws_ref.5) | copy-start | bytes 786436
  0.0 3.0 %copy-start.6 = (bf16[2,128,384]{2,1,0:T(8,128)(2,1)S(1)}, bf16[2,128,384]{2,1,0:T(8,128)(2,1)}, u32[]{:S(2)}) copy-start(bf16[2,128,384]{2,1,0:T(8,128)(2,1)} %w_ref.1) | copy-start | bytes 589828
  0.0 3.0 %copy-start.7 = (bf16[2,128,128]{2,1,0:T(8,128)(2,1)S(1)}, bf16[2,128,128]{2,1,0:T(8,128)(2,1)}, u32[]{:S(2)}) copy-start(bf16[2,128,128]{2,1,0:T(8,128)(2,1)} %wo_ref.5) | copy-start | bytes 196612
  1.0 2.1 %copy-start.4 = (bf16[2,128,512]{2,1,0:T(8,128)(2,1)S(1)}, bf16[2,128,512]{2,1,0:T(8,128)(2,1)}, u32[]{:S(2)}) copy-start(bf16[2,128,512]{2,1,0:T(8,128)(2,1)} %we_ref.5) | copy-start | bytes 786436
  1.1 12.4 %collective-permute-start = (bf16[8,16,128]{2,1,0:T(8,128)(2,1)S(1)}, bf16[8,16,128]{2,1,0:T(8,128)(2,1)S(1)}, u32[]{:S(2)}, u32[]{:S(2)}) collective-permute-start(bf16[8,16,128]{2,1,0:T(8,128)(2,1)S(1)} %get-tuple-element.75), channel_id=1, source_target_pairs={{0,16},{16,32},{32,48},{48,64},{64,80},{80,96},{96,112},{112,128},... | collective-permute-start | bytes 98312 | tf_op jit(solution)/shard_map/ppermute | solution.py:27
  6.0 9.0 %collective-permute-start.1 = (bf16[8,16,128]{2,1,0:T(8,128)(2,1)S(1)}, bf16[8,16,128]{2,1,0:T(8,128)(2,1)S(1)}, u32[]{:S(2)}, u32[]{:S(2)}) collective-permute-start(bf16[8,16,128]{2,1,0:T(8,128)(2,1)S(1)} %get-tuple-element.76), channel_id=1, source_target_pairs={{0,496},{16,0},{32,16},{48,32},{64,48},{80,64},{96,80},{112,96},{1... | collective-permute-start | bytes 98312 | tf_op jit(solution)/shard_map/ppermute | solution.py:27
  16.6 10.9 %collective-permute-start.2 = (bf16[288,128]{1,0:T(8,128)(2,1)S(1)}, bf16[288,128]{1,0:T(8,128)(2,1)S(1)}, u32[]{:S(2)}, u32[]{:S(2)}) collective-permute-start(bf16[288,128]{1,0:T(8,128)(2,1)S(1)} %get-tuple-element.83), channel_id=1, source_target_pairs={{1,2},{3,4},{5,6},{7,8},{9,10},{11,12},{13,14},{15,0},{2,1},{4,3},... | collective-permute-start | bytes 221192 | tf_op jit(solution)/shard_map/ppermute | solution.py:33
  23.8 6.2 %collective-permute-start.3 = (bf16[288,128]{1,0:T(8,128)(2,1)S(1)}, bf16[288,128]{1,0:T(8,128)(2,1)S(1)}, u32[]{:S(2)}, u32[]{:S(2)}) collective-permute-start(bf16[288,128]{1,0:T(8,128)(2,1)S(1)} %get-tuple-element.84), channel_id=1, source_target_pairs={{0,1},{2,3},{4,5},{6,7},{8,9},{10,11},{12,13},{14,15},{1,0},{3,2},... | collective-permute-start | bytes 221192 | tf_op jit(solution)/shard_map/ppermute | solution.py:33

commit v9 on v8

--- a/solution.py
+++ b/solution.py
@@ -25,12 +25,6 @@
 def shift(x, axis, by):
     length = lax.axis_size(axis)
     return lax.ppermute(x, axis, [(i, (i + by) % length) for i in range(length)])
-
-
-def swap(x, axis, first):
-    length = lax.axis_size(axis)
-    there = [(i, (i + 1) % length) for i in range(first, length, 2)]
-    return lax.ppermute(x, axis, there + [(b, a) for a, b in there])
 
 
 def iota(shape, dim):
@@ -237,7 +231,7 @@
 
 def halo_kernel(
     up_ref, down_ref, own_right_ref, own_left_ref, bias_ref, wqv_ref, wk_ref, wo_ref, we_ref, ws_ref, ag_ref, hg_ref,
-    na_ref, nb_ref, cols_odd_ref, cols_even_ref,
+    na_ref, nb_ref, right_ref, left_ref,
 ):
     z = cat(windows_of(down_ref[...]) + windows_of(up_ref[...]))
     normed = layer_norm(z, ag_ref[0:1, :]).astype(BF16)
@@ -256,11 +250,10 @@
     nb_ref[...] = nb.astype(BF16)
     right, left = edges(nb)
     n = own_right_ref.shape[0]
-    col_odd = lax.rem(lax.axis_index("gx"), 2) == 1
-    for at, size, a, b in [(0, n, own_right_ref[...], own_left_ref[...]), (n, 32, right, left)]:
-        a, b = a.astype(F32), b.astype(F32)
-        cols_odd_ref[at : at + size, :] = jnp.where(col_odd, a, b).astype(BF16)
-        cols_even_ref[at : at + size, :] = jnp.where(col_odd, b, a).astype(BF16)
+    right_ref[0:n, :] = own_right_ref[...]
+    left_ref[0:n, :] = own_left_ref[...]
+    right_ref[n : n + 32, :] = right
+    left_ref[n : n + 32, :] = left
 
 
 def middle_kernel(
@@ -308,7 +301,7 @@
 
 
 def outer_kernel(
-    fb_ref, nb_ref, vb_ref, cols_odd_ref, cols_even_ref, oa_ref, bias_b, bias_bv, wqv_ref, wk_ref, wo_ref, we_ref, ws_ref, hg_ref,
+    fb_ref, nb_ref, vb_ref, hl_ref, hr_ref, oa_ref, bias_b, bias_bv, wqv_ref, wk_ref, wo_ref, we_ref, ws_ref, hg_ref,
     out_ref,
 ):
     n = nb_ref.shape[0]
@@ -319,9 +312,7 @@
         return rows.astype(F32).reshape(-1, 8, 128)
 
     own = cat([vb_ref[32:64, :], nb_ref[...], vb_ref[0:32, :]]).astype(F32).reshape(-1, 8, 128)
-    odd, even = in_order(cols_odd_ref, h, 16), in_order(cols_even_ref, h, 16)
-    col_odd = lax.rem(lax.axis_index("gx"), 2) == 1
-    hl, hr = jnp.where(col_odd, even, odd), jnp.where(col_odd, odd, even)
+    hl, hr = in_order(hl_ref, h, 16), in_order(hr_ref, h, 16)
     low = low_half(hl.shape)
     even = jnp.where(low, hl, pltpu.roll(hr, 4, 1))
     odd = jnp.where(low, pltpu.roll(hl, 4, 1), hr)
@@ -396,17 +387,18 @@
         second_kernel, "second", (*weights, *state), kept, (), 4 * 10**9, {8 + i: i for i in range(9)}
     )
     fa, fb, na, nb, right, left, bias, wqv, wk = state
-    va, vb, odd, even = call(
+    va, vb, right, left = call(
         halo_kernel, "halo", (up, down, right, left, bias, wqv, wk, ow, ew, sw, ag, hg),
         [((64, C), BF16)] * 2 + [((n // 2 + 32, C), BF16)] * 2, (), 10**9,
     )
-    odd, even = swap(odd, "gx", 1), swap(even, "gx", 0)
+    hl = shift(right, "gx", 1)
+    hr = shift(left, "gx", -1)
     oa, bias_b, bias_bv, wqv, wk = call(
         middle_kernel, "middle", (fa, na, va, pb, tw, ow, ew, sw, hg),
         [((n, C), F32), table, table] + prepared, [pltpu.VMEM(*table)] * 2, 2 * 10**9,
     )
     return call(
-        outer_kernel, "outer", (fb, nb, vb, odd, even, oa, bias_b, bias_bv, wqv, wk, ow, ew, sw, hg),
+        outer_kernel, "outer", (fb, nb, vb, hl, hr, oa, bias_b, bias_bv, wqv, wk, ow, ew, sw, hg),
         [((height, breadth, C), F32)], (), 2 * 10**9,
     )[0]
 

time: 32.7 us -> 33.9 us (1.037)
  the two profiles are of different devices: /device:TPU:2 before, /device:TPU:56 now
where the time goes in v9:
time: 33.9 us; the launch traced here: 33.7 us
  starting transfers between devices  16.2 us (48%)
  Pallas kernels  8.69 us (26%)
  waiting for transfers between devices  7.66 us (23%)
  local copies, waits for them, and re-layouts  0.96 us (3%)
    ppermute x4, starting transfers between devices, shift(): lax.ppermute(x, axis, [(i, (i + by) % length) for i in range(length)])  16.2 us
    pallas_call x7, Pallas kernels, call(): pl.pallas_call(kernel, out_shape=shapes, in_specs=vmem(len(operands)), ou...  8.69 us
    ppermute x4, waiting for transfers between devices, shift(): lax.ppermute(x, axis, [(i, (i + by) % length) for i in range(length)])  7.66 us
    unnamed x16, local copies, waits for them, and re-layouts  0.96 us
  transfers between devices with their start and end apart: 4, of which 2 were waited for; matrix products, arithmetic and copies ran while one was open for 0% of the time, Pallas kernels for 14%

profile of v9, /device:TPU:56, one launch (start us, length us, event | category | flops | bytes accessed | tf_op | source)
XLA Modules:
  0.0 33.7 jit_solution(4047800005001983395)
XLA Ops:
  0.0 0.0 copy-start.3
  0.0 0.0 copy-start.1
  0.0 0.0 copy-start.2
  0.0 0.0 copy-start
  0.0 0.0 copy-start.5
  0.0 0.0 copy-start.6
  0.0 0.0 copy-start.7
  0.1 0.6 %copy-done.3 = f32[2,128]{1,0:T(2,128)S(1)} copy-done((f32[2,128]{1,0:T(2,128)S(1)}, f32[2,128]{1,0:T(2,128)}, u32[]{:S(2)}) %copy-start.3) | copy-done | bytes 1048
  0.7 0.0 copy-done.1
  0.7 0.0 copy-done.2
  0.7 0.3 copy-done
  1.0 0.0 copy-start.4
  1.0 0.1 edge_rows.1
  1.1 1.9 %collective-permute-start = (bf16[8,16,128]{2,1,0:T(8,128)(2,1)S(1)}, bf16[8,16,128]{2,1,0:T(8,128)(2,1)S(1)}, u32[]{:S(2)}, u32[]{:S(2)}) collective-permute-start(bf16[8,16,128]{2,1,0:T(8,128)(2,1)S(1)} %get-tuple-element.75), channel_id=1, source_target_pairs={{0,16},{16,32},{32,48},{48,64},{64,80},{80,96},{96,112},{112,128},... | collective-permute-start | bytes 98312 | tf_op jit(solution)/shard_map/ppermute | solution.py:27
  3.0 0.0 copy-done.5
  3.0 0.0 copy-done.6
  3.0 0.0 copy-done.7
  3.1 0.0 copy-done.4
  3.1 2.9 %conditional.1 = (bf16[8,16,128]{2,1,0:T(8,128)(2,1)S(1)}, f32[512,128]{1,0:T(8,128)S(1)}, f32[512,128]{1,0:T(8,128)S(1)}, bf16[512,128]{1,0:T(8,128)(2,1)S(1)},...) conditional(s32[]{:T(128)} %convert_element_type.3, ...), branch_computations={%region_0.0_spmd, %region_1.0_spmd} | conditional | flops 4000000000 | bytes 1114192 | solution.py:384
  3.1 2.9 %first.1 = (bf16[8,16,128]{2,1,0:T(8,128)(2,1)S(1)}, f32[512,128]{1,0:T(8,128)S(1)}, f32[512,128]{1,0:T(8,128)S(1)}, bf16[512,128]{1,0:T(8,128)(2,1)S(1)}, bf16[...) custom-call(bf16[64,16,128]{2,1,0:T(8,128)(2,1)S(1)} %get-tuple-elem, ...), custom_call_target="tpu_custom_call", output_to_operand_aliasing={{0}: (8, {})} | custom-call | flops 4000000000 | bytes 1048576 | tf_op jit(solution)/shard_map/cond/branch_1_fun/first/pallas_call | solution.py:351
  6.0 8.4 %collective-permute-start.1 = (bf16[8,16,128]{2,1,0:T(8,128)(2,1)S(1)}, bf16[8,16,128]{2,1,0:T(8,128)(2,1)S(1)}, u32[]{:S(2)}, u32[]{:S(2)}) collective-permute-start(bf16[8,16,128]{2,1,0:T(8,128)(2,1)S(1)} %get-tuple-element.76), channel_id=1, source_target_pairs={{0,496},{16,0},{32,16},{48,32},{64,48},{80,64},{96,80},{112,96},{1... | collective-permute-start | bytes 98312 | tf_op jit(solution)/shard_map/ppermute | solution.py:27
  14.5 0.0 collective-permute-done.up_ref
  14.5 1.5 %collective-permute-done.1.down_ref = bf16[8,16,128]{2,1,0:T(8,128)(2,1)S(1)} collective-permute-done((bf16[8,16,128]{2,1,0:T(8,128)(2,1)S(1)}, bf16[8,16,128]{2,1,0:T(8,128)(2,1)S(1)}, u32[]{:S(2)}, u32[]{:S(2)}) %collective-permute-start.1) | collective-permute-done | bytes 32800 | tf_op jit(solution)/shard_map/ppermute | solution.py:27
  16.0 1.5 %halo.1 = (bf16[64,128]{1,0:T(8,128)(2,1)S(1)}, bf16[64,128]{1,0:T(8,128)(2,1)S(1)}, bf16[288,128]{1,0:T(8,128)(2,1)S(1)}, bf16[288,128]{1,0:T(8,128)(2,1)S(1)}) custom-call(bf16[8,16,128]{2,1,0:T(8,128)(2,1)S(1)} %collective-permute-done.up_ref, bf16[8,16,128]{2,1,0:T(8,128)(2,1)S(1)} %collective-permute-done.1.down_ref, ...), custom_call_target="tpu_custom_call" | custom-call | flops 1000000000 | bytes 1048576 | tf_op jit(solution)/shard_map/halo/pallas_call | solution.py:351
  17.5 3.8 %collective-permute-start.2 = (bf16[288,128]{1,0:T(8,128)(2,1)S(1)}, bf16[288,128]{1,0:T(8,128)(2,1)S(1)}, u32[]{:S(2)}, u32[]{:S(2)}) collective-permute-start(bf16[288,128]{1,0:T(8,128)(2,1)S(1)} %get-tuple-element.83), channel_id=1, source_target_pairs={{0,1},{1,2},{2,3},{3,4},{4,5},{5,6},{6,7},{7,8},{8,9},{9,10},{10,1... | collective-permute-start | bytes 221192 | tf_op jit(solution)/shard_map/ppermute | solution.py:27
  21.4 2.0 %collective-permute-start.3 = (bf16[288,128]{1,0:T(8,128)(2,1)S(1)}, bf16[288,128]{1,0:T(8,128)(2,1)S(1)}, u32[]{:S(2)}, u32[]{:S(2)}) collective-permute-start(bf16[288,128]{1,0:T(8,128)(2,1)S(1)} %get-tuple-element.84), channel_id=1, source_target_pairs={{0,15},{1,0},{2,1},{3,2},{4,3},{5,4},{6,5},{7,6},{8,7},{9,8},{10,9... | collective-permute-start | bytes 221192 | tf_op jit(solution)/shard_map/ppermute | solution.py:27
  23.4 1.7 %middle.1 = (f32[512,128]{1,0:T(8,128)S(1)}, f32[64,512]{1,0:T(8,128)S(1)}, f32[64,512]{1,0:T(8,128)S(1)}, bf16[256,128]{1,0:T(8,128)(2,1)S(1)}, bf16[256,256]{1,0:T(8,128)(2,1)S(1)}) custom-call(f32[512,128]{1,0:T(8,128)S(1)} %get-tuple-element.85.fa_ref, bf16[512,128]{1,0:T(8,128)(2,1)S(1)} %get-tuple-element.86.na_ref, ...), custom_call_target="tpu_custom_call" | custom-call | flops 2000000000 | bytes 1048576 | tf_op jit(solution)/shard_map/middle/pallas_call | solution.py:351
  25.1 0.0 collective-permute-done.2.hl_ref
  25.1 6.1 %collective-permute-done.3.hr_ref = bf16[288,128]{1,0:T(8,128)(2,1)S(1)} collective-permute-done((bf16[288,128]{1,0:T(8,128)(2,1)S(1)}, bf16[288,128]{1,0:T(8,128)(2,1)S(1)}, u32[]{:S(2)}, u32[]{:S(2)}) %collective-permute-start.3) | collective-permute-done | bytes 73760 | tf_op jit(solution)/shard_map/ppermute | solution.py:27
  31.2 2.5 %outer.1 = f32[64,16,128]{2,1,0:T(8,128)} custom-call(f32[512,128]{1,0:T(8,128)S(1)} %get-tuple-element.73.fb_ref, bf16[512,128]{1,0:T(8,128)(2,1)S(1)} %get-tuple-element.74.nb_ref, bf16[64,128]{1,0:T(8,128)(2,1)S(1)} %get-tuple-element.82.vb_ref, bf16[288,128]{1,0:T(8,128)(2,1)S(1)} %collective-permute-done.2.hl_ref, ...), custom_call_target="tpu_custom_call" | custom-call | flops 2000000000 | bytes 1048576 | tf_op jit(solution)/shard_map/outer/pallas_call | solution.py:351
  (3 shorter events, 0.0 us)
Async XLA Ops:
  0.0 0.7 %copy-start.3 = (f32[2,128]{1,0:T(2,128)S(1)}, f32[2,128]{1,0:T(2,128)}, u32[]{:S(2)}) copy-start(f32[2,128]{1,0:T(2,128)} %hg_ref.7) | copy-start | bytes 3076
  0.0 0.7 %copy-start.1 = (f32[2,4,225]{2,1,0:T(4,128)S(1)}, f32[2,4,225]{2,1,0:T(4,128)}, u32[]{:S(2)}) copy-start(f32[2,4,225]{2,1,0:T(4,128)} %pb_ref.3) | copy-start | bytes 21604
  0.0 0.7 %copy-start.2 = (f32[2,128]{1,0:T(2,128)S(1)}, f32[2,128]{1,0:T(2,128)}, u32[]{:S(2)}) copy-start(f32[2,128]{1,0:T(2,128)} %ag_ref.3) | copy-start | bytes 3076
  0.0 1.0 %copy-start = (bf16[64,16,128]{2,1,0:T(8,128)(2,1)S(1)}, bf16[64,16,128]{2,1,0:T(8,128)(2,1)}, u32[]{:S(2)}) copy-start(bf16[64,16,128]{2,1,0:T(8,128)(2,1)} %refs_0_.2) | copy-start | bytes 786436
  0.0 3.0 %copy-start.5 = (bf16[2,512,128]{2,1,0:T(8,128)(2,1)S(1)}, bf16[2,512,128]{2,1,0:T(8,128)(2,1)}, u32[]{:S(2)}) copy-start(bf16[2,512,128]{2,1,0:T(8,128)(2,1)} %ws_ref.5) | copy-start | bytes 786436
  0.0 3.0 %copy-start.6 = (bf16[2,128,384]{2,1,0:T(8,128)(2,1)S(1)}, bf16[2,128,384]{2,1,0:T(8,128)(2,1)}, u32[]{:S(2)}) copy-start(bf16[2,128,384]{2,1,0:T(8,128)(2,1)} %w_ref.1) | copy-start | bytes 589828
  0.0 3.0 %copy-start.7 = (bf16[2,128,128]{2,1,0:T(8,128)(2,1)S(1)}, bf16[2,128,128]{2,1,0:T(8,128)(2,1)}, u32[]{:S(2)}) copy-start(bf16[2,128,128]{2,1,0:T(8,128)(2,1)} %wo_ref.5) | copy-start | bytes 196612
  1.0 2.1 %copy-start.4 = (bf16[2,128,512]{2,1,0:T(8,128)(2,1)S(1)}, bf16[2,128,512]{2,1,0:T(8,128)(2,1)}, u32[]{:S(2)}) copy-start(bf16[2,128,512]{2,1,0:T(8,128)(2,1)} %we_ref.5) | copy-start | bytes 786436
  1.1 13.4 %collective-permute-start = (bf16[8,16,128]{2,1,0:T(8,128)(2,1)S(1)}, bf16[8,16,128]{2,1,0:T(8,128)(2,1)S(1)}, u32[]{:S(2)}, u32[]{:S(2)}) collective-permute-start(bf16[8,16,128]{2,1,0:T(8,128)(2,1)S(1)} %get-tuple-element.75), channel_id=1, source_target_pairs={{0,16},{16,32},{32,48},{48,64},{64,80},{80,96},{96,112},{112,128},... | collective-permute-start | bytes 98312 | tf_op jit(solution)/shard_map/ppermute | solution.py:27
  6.0 10.0 %collective-permute-start.1 = (bf16[8,16,128]{2,1,0:T(8,128)(2,1)S(1)}, bf16[8,16,128]{2,1,0:T(8,128)(2,1)S(1)}, u32[]{:S(2)}, u32[]{:S(2)}) collective-permute-start(bf16[8,16,128]{2,1,0:T(8,128)(2,1)S(1)} %get-tuple-element.76), channel_id=1, source_target_pairs={{0,496},{16,0},{32,16},{48,32},{64,48},{80,64},{96,80},{112,96},{1... | collective-permute-start | bytes 98312 | tf_op jit(solution)/shard_map/ppermute | solution.py:27
  17.5 7.6 %collective-permute-start.2 = (bf16[288,128]{1,0:T(8,128)(2,1)S(1)}, bf16[288,128]{1,0:T(8,128)(2,1)S(1)}, u32[]{:S(2)}, u32[]{:S(2)}) collective-permute-start(bf16[288,128]{1,0:T(8,128)(2,1)S(1)} %get-tuple-element.83), channel_id=1, source_target_pairs={{0,1},{1,2},{2,3},{3,4},{4,5},{5,6},{6,7},{7,8},{8,9},{9,10},{10,1... | collective-permute-start | bytes 221192 | tf_op jit(solution)/shard_map/ppermute | solution.py:27
  21.4 9.9 %collective-permute-start.3 = (bf16[288,128]{1,0:T(8,128)(2,1)S(1)}, bf16[288,128]{1,0:T(8,128)(2,1)S(1)}, u32[]{:S(2)}, u32[]{:S(2)}) collective-permute-start(bf16[288,128]{1,0:T(8,128)(2,1)S(1)} %get-tuple-element.84), channel_id=1, source_target_pairs={{0,15},{1,0},{2,1},{3,2},{4,3},{5,4},{6,5},{7,6},{8,7},{9,8},{10,9... | collective-permute-start | bytes 221192 | tf_op jit(solution)/shard_map/ppermute | solution.py:27

commit v10 on v8

--- a/solution.py
+++ b/solution.py
@@ -25,6 +25,21 @@
 def shift(x, axis, by):
     length = lax.axis_size(axis)
     return lax.ppermute(x, axis, [(i, (i + by) % length) for i in range(length)])
+
+
+def far(index, length):
+    place = index % (length // 2)
+    return (place == 0) | (place == length // 2 - 1)
+
+
+def near_first(x, axis):
+    length = lax.axis_size(axis)
+    return lax.ppermute(x, axis, [(i ^ 1, i) for i in range(length) if far(i, length)])
+
+
+def near_last(x, axis):
+    length = lax.axis_size(axis)
+    return lax.ppermute(x, axis, [(i ^ 1, i) for i in range(length) if not far(i, length)])
 
 
 def swap(x, axis, first):
@@ -237,7 +252,7 @@
 
 def halo_kernel(
     up_ref, down_ref, own_right_ref, own_left_ref, bias_ref, wqv_ref, wk_ref, wo_ref, we_ref, ws_ref, ag_ref, hg_ref,
-    na_ref, nb_ref, cols_odd_ref, cols_even_ref,
+    na_ref, nb_ref, cols_odd_ref, cols_even_ref, cols_early_ref,
 ):
     z = cat(windows_of(down_ref[...]) + windows_of(up_ref[...]))
     normed = layer_norm(z, ag_ref[0:1, :]).astype(BF16)
@@ -261,6 +276,7 @@
         a, b = a.astype(F32), b.astype(F32)
         cols_odd_ref[at : at + size, :] = jnp.where(col_odd, a, b).astype(BF16)
         cols_even_ref[at : at + size, :] = jnp.where(col_odd, b, a).astype(BF16)
+        cols_early_ref[at : at + size, :] = jnp.where(col_odd, b, a).astype(BF16)
 
 
 def middle_kernel(
@@ -308,7 +324,7 @@
 
 
 def outer_kernel(
-    fb_ref, nb_ref, vb_ref, cols_odd_ref, cols_even_ref, oa_ref, bias_b, bias_bv, wqv_ref, wk_ref, wo_ref, we_ref, ws_ref, hg_ref,
+    fb_ref, nb_ref, vb_ref, early_ref, odd_ref, even_ref, oa_ref, bias_b, bias_bv, wqv_ref, wk_ref, wo_ref, we_ref, ws_ref, hg_ref,
     out_ref,
 ):
     n = nb_ref.shape[0]
@@ -319,7 +335,9 @@
         return rows.astype(F32).reshape(-1, 8, 128)
 
     own = cat([vb_ref[32:64, :], nb_ref[...], vb_ref[0:32, :]]).astype(F32).reshape(-1, 8, 128)
-    odd, even = in_order(cols_odd_ref, h, 16), in_order(cols_even_ref, h, 16)
+    is_far = far(lax.axis_index("gx"), lax.axis_size("gx"))
+    odd = in_order(odd_ref, h, 16)
+    even = jnp.where(is_far, in_order(early_ref, h, 16), in_order(even_ref, h, 16))
     col_odd = lax.rem(lax.axis_index("gx"), 2) == 1
     hl, hr = jnp.where(col_odd, even, odd), jnp.where(col_odd, odd, even)
     low = low_half(hl.shape)
@@ -396,17 +414,19 @@
         second_kernel, "second", (*weights, *state), kept, (), 4 * 10**9, {8 + i: i for i in range(9)}
     )
     fa, fb, na, nb, right, left, bias, wqv, wk = state
-    va, vb, odd, even = call(
+    va, vb, odd, even, early = call(
         halo_kernel, "halo", (up, down, right, left, bias, wqv, wk, ow, ew, sw, ag, hg),
-        [((64, C), BF16)] * 2 + [((n // 2 + 32, C), BF16)] * 2, (), 10**9,
+        [((64, C), BF16)] * 2 + [((n // 2 + 32, C), BF16)] * 3, (), 10**9,
     )
-    odd, even = swap(odd, "gx", 1), swap(even, "gx", 0)
+    early = near_first(early, "gx")
+    odd = swap(odd, "gx", 1)
+    even = near_last(even, "gx")
     oa, bias_b, bias_bv, wqv, wk = call(
         middle_kernel, "middle", (fa, na, va, pb, tw, ow, ew, sw, hg),
         [((n, C), F32), table, table] + prepared, [pltpu.VMEM(*table)] * 2, 2 * 10**9,
     )
     return call(
-        outer_kernel, "outer", (fb, nb, vb, odd, even, oa, bias_b, bias_bv, wqv, wk, ow, ew, sw, hg),
+        outer_kernel, "outer", (fb, nb, vb, early, odd, even, oa, bias_b, bias_bv, wqv, wk, ow, ew, sw, hg),
         [((height, breadth, C), F32)], (), 2 * 10**9,
     )[0]
 

time: 32.7 us -> 33.1 us (1.012)
  the two profiles are of different devices: /device:TPU:2 before, /device:TPU:8 now
where the time goes in v10:
time: 33.1 us; the launch traced here: 32.9 us
  starting transfers between devices  15.9 us (48%)
  Pallas kernels  8.68 us (26%)
  waiting for transfers between devices  7.13 us (22%)
  local copies, waits for them, and re-layouts  0.96 us (3%)
    ppermute x2, starting transfers between devices, shift(): lax.ppermute(x, axis, [(i, (i + by) % length) for i in range(length)])  10.3 us
    pallas_call x7, Pallas kernels, call(): pl.pallas_call(kernel, out_shape=shapes, in_specs=vmem(len(operands)), ou...  8.68 us
    ppermute x1, waiting for transfers between devices, near_last(): lax.ppermute(x, axis, [(i ^ 1, i) for i in range(length) if not far(i, le...  4.3 us
    ppermute x1, starting transfers between devices, near_first(): lax.ppermute(x, axis, [(i ^ 1, i) for i in range(length) if far(i, length)])  2.36 us
    ppermute x1, starting transfers between devices, swap(): return lax.ppermute(x, axis, there + [(b, a) for a, b in there])  1.92 us
    ppermute x2, waiting for transfers between devices, shift(): lax.ppermute(x, axis, [(i, (i + by) % length) for i in range(length)])  1.53 us
    ppermute x1, waiting for transfers between devices, swap(): return lax.ppermute(x, axis, there + [(b, a) for a, b in there])  1.29 us
    ppermute x1, starting transfers between devices, near_last(): lax.ppermute(x, axis, [(i ^ 1, i) for i in range(length) if not far(i, le...  1.29 us
  transfers between devices with their start and end apart: 5, of which 3 were waited for; matrix products, arithmetic and copies ran while one was open for 0% of the time, Pallas kernels for 14%

profile of v10, /device:TPU:8, one launch (start us, length us, event | category | flops | bytes accessed | tf_op | source)
XLA Modules:
  0.0 32.9 jit_solution(10050773445940715309)
XLA Ops:
  0.0 0.0 copy-start.3
  0.0 0.0 copy-start.1
  0.0 0.0 copy-start.2
  0.0 0.0 copy-start
  0.0 0.0 copy-start.5
  0.0 0.0 copy-start.6
  0.0 0.0 copy-start.7
  0.1 0.6 %copy-done.3 = f32[2,128]{1,0:T(2,128)S(1)} copy-done((f32[2,128]{1,0:T(2,128)S(1)}, f32[2,128]{1,0:T(2,128)}, u32[]{:S(2)}) %copy-start.3) | copy-done | bytes 1048
  0.7 0.0 copy-done.1
  0.7 0.0 copy-done.2
  0.7 0.3 copy-done
  1.0 0.0 copy-start.4
  1.0 0.1 edge_rows.1
  1.1 1.9 %collective-permute-start = (bf16[8,16,128]{2,1,0:T(8,128)(2,1)S(1)}, bf16[8,16,128]{2,1,0:T(8,128)(2,1)S(1)}, u32[]{:S(2)}, u32[]{:S(2)}) collective-permute-start(bf16[8,16,128]{2,1,0:T(8,128)(2,1)S(1)} %get-tuple-element.76), channel_id=1, source_target_pairs={{0,16},{16,32},{32,48},{48,64},{64,80},{80,96},{96,112},{112,128},... | collective-permute-start | bytes 98312 | tf_op jit(solution)/shard_map/ppermute | solution.py:27
  3.0 0.0 copy-done.5
  3.0 0.0 copy-done.6
  3.0 0.0 copy-done.7
  3.1 0.0 copy-done.4
  3.1 2.9 %conditional.1 = (bf16[8,16,128]{2,1,0:T(8,128)(2,1)S(1)}, f32[512,128]{1,0:T(8,128)S(1)}, f32[512,128]{1,0:T(8,128)S(1)}, bf16[512,128]{1,0:T(8,128)(2,1)S(1)},...) conditional(s32[]{:T(128)} %convert_element_type.3, ...), branch_computations={%region_0.0_spmd, %region_1.0_spmd} | conditional | flops 4000000000 | bytes 1114192 | solution.py:411
  3.1 2.9 %first.1 = (bf16[8,16,128]{2,1,0:T(8,128)(2,1)S(1)}, f32[512,128]{1,0:T(8,128)S(1)}, f32[512,128]{1,0:T(8,128)S(1)}, bf16[512,128]{1,0:T(8,128)(2,1)S(1)}, bf16[...) custom-call(bf16[64,16,128]{2,1,0:T(8,128)(2,1)S(1)} %get-tuple-elem, ...), custom_call_target="tpu_custom_call", output_to_operand_aliasing={{0}: (8, {})} | custom-call | flops 4000000000 | bytes 1048576 | tf_op jit(solution)/shard_map/cond/branch_1_fun/first/pallas_call | solution.py:378
  6.0 8.4 %collective-permute-start.1 = (bf16[8,16,128]{2,1,0:T(8,128)(2,1)S(1)}, bf16[8,16,128]{2,1,0:T(8,128)(2,1)S(1)}, u32[]{:S(2)}, u32[]{:S(2)}) collective-permute-start(bf16[8,16,128]{2,1,0:T(8,128)(2,1)S(1)} %get-tuple-element.77), channel_id=1, source_target_pairs={{0,496},{16,0},{32,16},{48,32},{64,48},{80,64},{96,80},{112,96},{1... | collective-permute-start | bytes 98312 | tf_op jit(solution)/shard_map/ppermute | solution.py:27
  14.5 0.0 collective-permute-done.up_ref
  14.5 1.5 %collective-permute-done.1.down_ref = bf16[8,16,128]{2,1,0:T(8,128)(2,1)S(1)} collective-permute-done((bf16[8,16,128]{2,1,0:T(8,128)(2,1)S(1)}, bf16[8,16,128]{2,1,0:T(8,128)(2,1)S(1)}, u32[]{:S(2)}, u32[]{:S(2)}) %collective-permute-start.1) | collective-permute-done | bytes 32800 | tf_op jit(solution)/shard_map/ppermute | solution.py:27
  16.0 1.5 %halo.1 = (bf16[64,128]{1,0:T(8,128)(2,1)S(1)}, bf16[64,128]{1,0:T(8,128)(2,1)S(1)}, bf16[288,128]{1,0:T(8,128)(2,1)S(1)}, bf16[288,128]{1,0:T(8,128)(2,1)S(1)}, bf16[288,128]{1,0:T(8,128)(2,1)S(1)}) custom-call(bf16[8,16,128]{2,1,0:T(8,128)(2,1)S(1)} %collective-permute-done.up_ref, bf16[8,16,128]{2,1,0:T(8,128)(2,1)S(1)} %collective-permute-done.1.down_ref, ...), custom_call_target="tpu_custom_call" | custom-call | flops 1000000000 | bytes 1048576 | tf_op jit(solution)/shard_map/halo/pallas_call | solution.py:378
  17.5 2.4 %collective-permute-start.2 = (bf16[288,128]{1,0:T(8,128)(2,1)S(1)}, bf16[288,128]{1,0:T(8,128)(2,1)S(1)}, u32[]{:S(2)}, u32[]{:S(2)}) collective-permute-start(bf16[288,128]{1,0:T(8,128)(2,1)S(1)} %get-tuple-element.84), channel_id=1, source_target_pairs={{1,0},{6,7},{9,8},{14,15},{17,16},{22,23},{25,24},{30,31},{33,32},... | collective-permute-start | bytes 221192 | tf_op jit(solution)/shard_map/ppermute | solution.py:37
  19.9 1.9 %collective-permute-start.3 = (bf16[288,128]{1,0:T(8,128)(2,1)S(1)}, bf16[288,128]{1,0:T(8,128)(2,1)S(1)}, u32[]{:S(2)}, u32[]{:S(2)}) collective-permute-start(bf16[288,128]{1,0:T(8,128)(2,1)S(1)} %get-tuple-element.85), channel_id=1, source_target_pairs={{1,2},{3,4},{5,6},{7,8},{9,10},{11,12},{13,14},{15,0},{2,1},{4,3},... | collective-permute-start | bytes 221192 | tf_op jit(solution)/shard_map/ppermute | solution.py:48
  21.8 1.3 %collective-permute-start.4 = (bf16[288,128]{1,0:T(8,128)(2,1)S(1)}, bf16[288,128]{1,0:T(8,128)(2,1)S(1)}, u32[]{:S(2)}, u32[]{:S(2)}) collective-permute-start(bf16[288,128]{1,0:T(8,128)(2,1)S(1)} %get-tuple-element.86), channel_id=1, source_target_pairs={{0,1},{3,2},{2,3},{5,4},{4,5},{7,6},{8,9},{11,10},{10,11},{13,12},... | collective-permute-start | bytes 221192 | tf_op jit(solution)/shard_map/ppermute | solution.py:42
  23.1 1.7 %middle.1 = (f32[512,128]{1,0:T(8,128)S(1)}, f32[64,512]{1,0:T(8,128)S(1)}, f32[64,512]{1,0:T(8,128)S(1)}, bf16[256,128]{1,0:T(8,128)(2,1)S(1)}, bf16[256,256]{1,0:T(8,128)(2,1)S(1)}) custom-call(f32[512,128]{1,0:T(8,128)S(1)} %get-tuple-element.87.fa_ref, bf16[512,128]{1,0:T(8,128)(2,1)S(1)} %get-tuple-element.88.na_ref, ...), custom_call_target="tpu_custom_call" | custom-call | flops 2000000000 | bytes 1048576 | tf_op jit(solution)/shard_map/middle/pallas_call | solution.py:378
  24.8 0.0 collective-permute-done.2.early_ref
  24.8 1.3 %collective-permute-done.3.odd_ref = bf16[288,128]{1,0:T(8,128)(2,1)S(1)} collective-permute-done((bf16[288,128]{1,0:T(8,128)(2,1)S(1)}, bf16[288,128]{1,0:T(8,128)(2,1)S(1)}, u32[]{:S(2)}, u32[]{:S(2)}) %collective-permute-start.3) | collective-permute-done | bytes 73760 | tf_op jit(solution)/shard_map/ppermute | solution.py:48
  26.1 4.3 %collective-permute-done.4.even_ref = bf16[288,128]{1,0:T(8,128)(2,1)S(1)} collective-permute-done((bf16[288,128]{1,0:T(8,128)(2,1)S(1)}, bf16[288,128]{1,0:T(8,128)(2,1)S(1)}, u32[]{:S(2)}, u32[]{:S(2)}) %collective-permute-start.4) | collective-permute-done | bytes 73760 | tf_op jit(solution)/shard_map/ppermute | solution.py:42
  30.4 2.4 %outer.1 = f32[64,16,128]{2,1,0:T(8,128)} custom-call(f32[512,128]{1,0:T(8,128)S(1)} %get-tuple-element.74.fb_ref, bf16[512,128]{1,0:T(8,128)(2,1)S(1)} %get-tuple-element.75.nb_ref, bf16[64,128]{1,0:T(8,128)(2,1)S(1)} %get-tuple-element.83.vb_ref, bf16[288,128]{1,0:T(8,128)(2,1)S(1)} %collective-permute-done.2.early_ref, ...), custom_call_target="tpu_custom_call" | custom-call | flops 2000000000 | bytes 1048576 | tf_op jit(solution)/shard_map/outer/pallas_call | solution.py:378
  (3 shorter events, 0.0 us)
Async XLA Ops:
  0.0 0.7 %copy-start.3 = (f32[2,128]{1,0:T(2,128)S(1)}, f32[2,128]{1,0:T(2,128)}, u32[]{:S(2)}) copy-start(f32[2,128]{1,0:T(2,128)} %hg_ref.7) | copy-start | bytes 3076
  0.0 0.7 %copy-start.1 = (f32[2,4,225]{2,1,0:T(4,128)S(1)}, f32[2,4,225]{2,1,0:T(4,128)}, u32[]{:S(2)}) copy-start(f32[2,4,225]{2,1,0:T(4,128)} %pb_ref.3) | copy-start | bytes 21604
  0.0 0.7 %copy-start.2 = (f32[2,128]{1,0:T(2,128)S(1)}, f32[2,128]{1,0:T(2,128)}, u32[]{:S(2)}) copy-start(f32[2,128]{1,0:T(2,128)} %ag_ref.3) | copy-start | bytes 3076
  0.0 1.0 %copy-start = (bf16[64,16,128]{2,1,0:T(8,128)(2,1)S(1)}, bf16[64,16,128]{2,1,0:T(8,128)(2,1)}, u32[]{:S(2)}) copy-start(bf16[64,16,128]{2,1,0:T(8,128)(2,1)} %refs_0_.2) | copy-start | bytes 786436
  0.0 3.0 %copy-start.5 = (bf16[2,512,128]{2,1,0:T(8,128)(2,1)S(1)}, bf16[2,512,128]{2,1,0:T(8,128)(2,1)}, u32[]{:S(2)}) copy-start(bf16[2,512,128]{2,1,0:T(8,128)(2,1)} %ws_ref.5) | copy-start | bytes 786436
  0.0 3.0 %copy-start.6 = (bf16[2,128,384]{2,1,0:T(8,128)(2,1)S(1)}, bf16[2,128,384]{2,1,0:T(8,128)(2,1)}, u32[]{:S(2)}) copy-start(bf16[2,128,384]{2,1,0:T(8,128)(2,1)} %w_ref.1) | copy-start | bytes 589828
  0.0 3.0 %copy-start.7 = (bf16[2,128,128]{2,1,0:T(8,128)(2,1)S(1)}, bf16[2,128,128]{2,1,0:T(8,128)(2,1)}, u32[]{:S(2)}) copy-start(bf16[2,128,128]{2,1,0:T(8,128)(2,1)} %wo_ref.5) | copy-start | bytes 196612
  1.0 2.1 %copy-start.4 = (bf16[2,128,512]{2,1,0:T(8,128)(2,1)S(1)}, bf16[2,128,512]{2,1,0:T(8,128)(2,1)}, u32[]{:S(2)}) copy-start(bf16[2,128,512]{2,1,0:T(8,128)(2,1)} %we_ref.5) | copy-start | bytes 786436
  1.1 13.4 %collective-permute-start = (bf16[8,16,128]{2,1,0:T(8,128)(2,1)S(1)}, bf16[8,16,128]{2,1,0:T(8,128)(2,1)S(1)}, u32[]{:S(2)}, u32[]{:S(2)}) collective-permute-start(bf16[8,16,128]{2,1,0:T(8,128)(2,1)S(1)} %get-tuple-element.76), channel_id=1, source_target_pairs={{0,16},{16,32},{32,48},{48,64},{64,80},{80,96},{96,112},{112,128},... | collective-permute-start | bytes 98312 | tf_op jit(solution)/shard_map/ppermute | solution.py:27
  6.0 10.0 %collective-permute-start.1 = (bf16[8,16,128]{2,1,0:T(8,128)(2,1)S(1)}, bf16[8,16,128]{2,1,0:T(8,128)(2,1)S(1)}, u32[]{:S(2)}, u32[]{:S(2)}) collective-permute-start(bf16[8,16,128]{2,1,0:T(8,128)(2,1)S(1)} %get-tuple-element.77), channel_id=1, source_target_pairs={{0,496},{16,0},{32,16},{48,32},{64,48},{80,64},{96,80},{112,96},{1... | collective-permute-start | bytes 98312 | tf_op jit(solution)/shard_map/ppermute | solution.py:27
  17.5 7.3 %collective-permute-start.2 = (bf16[288,128]{1,0:T(8,128)(2,1)S(1)}, bf16[288,128]{1,0:T(8,128)(2,1)S(1)}, u32[]{:S(2)}, u32[]{:S(2)}) collective-permute-start(bf16[288,128]{1,0:T(8,128)(2,1)S(1)} %get-tuple-element.84), channel_id=1, source_target_pairs={{1,0},{6,7},{9,8},{14,15},{17,16},{22,23},{25,24},{30,31},{33,32},... | collective-permute-start | bytes 221192 | tf_op jit(solution)/shard_map/ppermute | solution.py:37
  19.9 6.2 %collective-permute-start.3 = (bf16[288,128]{1,0:T(8,128)(2,1)S(1)}, bf16[288,128]{1,0:T(8,128)(2,1)S(1)}, u32[]{:S(2)}, u32[]{:S(2)}) collective-permute-start(bf16[288,128]{1,0:T(8,128)(2,1)S(1)} %get-tuple-element.85), channel_id=1, source_target_pairs={{1,2},{3,4},{5,6},{7,8},{9,10},{11,12},{13,14},{15,0},{2,1},{4,3},... | collective-permute-start | bytes 221192 | tf_op jit(solution)/shard_map/ppermute | solution.py:48
  21.8 8.6 %collective-permute-start.4 = (bf16[288,128]{1,0:T(8,128)(2,1)S(1)}, bf16[288,128]{1,0:T(8,128)(2,1)S(1)}, u32[]{:S(2)}, u32[]{:S(2)}) collective-permute-start(bf16[288,128]{1,0:T(8,128)(2,1)S(1)} %get-tuple-element.86), channel_id=1, source_target_pairs={{0,1},{3,2},{2,3},{5,4},{4,5},{7,6},{8,9},{11,10},{10,11},{13,12},... | collective-permute-start | bytes 221192 | tf_op jit(solution)/shard_map/ppermute | solution.py:42

commit v11 on v8

--- a/solution.py
+++ b/solution.py
@@ -308,7 +308,7 @@
 
 
 def outer_kernel(
-    fb_ref, nb_ref, vb_ref, cols_odd_ref, cols_even_ref, oa_ref, bias_b, bias_bv, wqv_ref, wk_ref, wo_ref, we_ref, ws_ref, hg_ref,
+    fb_ref, nb_ref, vb_ref, cols_even_ref, cols_odd_ref, oa_ref, bias_b, bias_bv, wqv_ref, wk_ref, wo_ref, we_ref, ws_ref, hg_ref,
     out_ref,
 ):
     n = nb_ref.shape[0]
@@ -400,13 +400,13 @@
         halo_kernel, "halo", (up, down, right, left, bias, wqv, wk, ow, ew, sw, ag, hg),
         [((64, C), BF16)] * 2 + [((n // 2 + 32, C), BF16)] * 2, (), 10**9,
     )
-    odd, even = swap(odd, "gx", 1), swap(even, "gx", 0)
+    even, odd = swap(even, "gx", 0), swap(odd, "gx", 1)
     oa, bias_b, bias_bv, wqv, wk = call(
         middle_kernel, "middle", (fa, na, va, pb, tw, ow, ew, sw, hg),
         [((n, C), F32), table, table] + prepared, [pltpu.VMEM(*table)] * 2, 2 * 10**9,
     )
     return call(
-        outer_kernel, "outer", (fb, nb, vb, odd, even, oa, bias_b, bias_bv, wqv, wk, ow, ew, sw, hg),
+        outer_kernel, "outer", (fb, nb, vb, even, odd, oa, bias_b, bias_bv, wqv, wk, ow, ew, sw, hg),
         [((height, breadth, C), F32)], (), 2 * 10**9,
     )[0]
 

time: 32.7 us -> 33.3 us (1.018)
  the two profiles are of different devices: /device:TPU:2 before, /device:TPU:56 now
where the time goes in v11:
time: 33.3 us; the launch traced here: 33.1 us
  starting transfers between devices  17.7 us (53%)
  Pallas kernels  8.68 us (26%)
  waiting for transfers between devices  5.6 us (17%)
  local copies, waits for them, and re-layouts  0.96 us (3%)
    ppermute x2, starting transfers between devices, shift(): lax.ppermute(x, axis, [(i, (i + by) % length) for i in range(length)])  10.3 us
    pallas_call x7, Pallas kernels, call(): pl.pallas_call(kernel, out_shape=shapes, in_specs=vmem(len(operands)), ou...  8.68 us
    ppermute x2, starting transfers between devices, swap(): return lax.ppermute(x, axis, there + [(b, a) for a, b in there])  7.33 us
    ppermute x2, waiting for transfers between devices, swap(): return lax.ppermute(x, axis, there + [(b, a) for a, b in there])  4.06 us
    ppermute x2, waiting for transfers between devices, shift(): lax.ppermute(x, axis, [(i, (i + by) % length) for i in range(length)])  1.53 us
    unnamed x16, local copies, waits for them, and re-layouts  0.96 us
  transfers between devices with their start and end apart: 4, of which 2 were waited for; matrix products, arithmetic and copies ran while one was open for 0% of the time, Pallas kernels for 14%

profile of v11, /device:TPU:56, one launch (start us, length us, event | category | flops | bytes accessed | tf_op | source)
XLA Modules:
  0.0 33.1 jit_solution(2018206720020236735)
XLA Ops:
  0.0 0.0 copy-start.3
  0.0 0.0 copy-start.1
  0.0 0.0 copy-start.2
  0.0 0.0 copy-start
  0.0 0.0 copy-start.5
  0.0 0.0 copy-start.6
  0.0 0.0 copy-start.7
  0.1 0.6 %copy-done.3 = f32[2,128]{1,0:T(2,128)S(1)} copy-done((f32[2,128]{1,0:T(2,128)S(1)}, f32[2,128]{1,0:T(2,128)}, u32[]{:S(2)}) %copy-start.3) | copy-done | bytes 1048
  0.7 0.0 copy-done.1
  0.7 0.0 copy-done.2
  0.7 0.3 copy-done
  1.0 0.0 copy-start.4
  1.0 0.1 edge_rows.1
  1.1 1.9 %collective-permute-start = (bf16[8,16,128]{2,1,0:T(8,128)(2,1)S(1)}, bf16[8,16,128]{2,1,0:T(8,128)(2,1)S(1)}, u32[]{:S(2)}, u32[]{:S(2)}) collective-permute-start(bf16[8,16,128]{2,1,0:T(8,128)(2,1)S(1)} %get-tuple-element.75), channel_id=1, source_target_pairs={{0,16},{16,32},{32,48},{48,64},{64,80},{80,96},{96,112},{112,128},... | collective-permute-start | bytes 98312 | tf_op jit(solution)/shard_map/ppermute | solution.py:27
  3.0 0.0 copy-done.5
  3.0 0.0 copy-done.6
  3.0 0.0 copy-done.7
  3.1 0.0 copy-done.4
  3.1 2.9 %conditional.1 = (bf16[8,16,128]{2,1,0:T(8,128)(2,1)S(1)}, f32[512,128]{1,0:T(8,128)S(1)}, f32[512,128]{1,0:T(8,128)S(1)}, bf16[512,128]{1,0:T(8,128)(2,1)S(1)},...) conditional(s32[]{:T(128)} %convert_element_type.3, ...), branch_computations={%region_0.0_spmd, %region_1.0_spmd} | conditional | flops 4000000000 | bytes 1114192 | solution.py:393
  3.1 2.9 %first.1 = (bf16[8,16,128]{2,1,0:T(8,128)(2,1)S(1)}, f32[512,128]{1,0:T(8,128)S(1)}, f32[512,128]{1,0:T(8,128)S(1)}, bf16[512,128]{1,0:T(8,128)(2,1)S(1)}, bf16[...) custom-call(bf16[64,16,128]{2,1,0:T(8,128)(2,1)S(1)} %get-tuple-elem, ...), custom_call_target="tpu_custom_call", output_to_operand_aliasing={{0}: (8, {})} | custom-call | flops 4000000000 | bytes 1048576 | tf_op jit(solution)/shard_map/cond/branch_1_fun/first/pallas_call | solution.py:360
  6.0 8.4 %collective-permute-start.1 = (bf16[8,16,128]{2,1,0:T(8,128)(2,1)S(1)}, bf16[8,16,128]{2,1,0:T(8,128)(2,1)S(1)}, u32[]{:S(2)}, u32[]{:S(2)}) collective-permute-start(bf16[8,16,128]{2,1,0:T(8,128)(2,1)S(1)} %get-tuple-element.76), channel_id=1, source_target_pairs={{0,496},{16,0},{32,16},{48,32},{64,48},{80,64},{96,80},{112,96},{1... | collective-permute-start | bytes 98312 | tf_op jit(solution)/shard_map/ppermute | solution.py:27
  14.5 0.0 collective-permute-done.up_ref
  14.5 1.5 %collective-permute-done.1.down_ref = bf16[8,16,128]{2,1,0:T(8,128)(2,1)S(1)} collective-permute-done((bf16[8,16,128]{2,1,0:T(8,128)(2,1)S(1)}, bf16[8,16,128]{2,1,0:T(8,128)(2,1)S(1)}, u32[]{:S(2)}, u32[]{:S(2)}) %collective-permute-start.1) | collective-permute-done | bytes 32800 | tf_op jit(solution)/shard_map/ppermute | solution.py:27
  16.0 1.5 %halo.1 = (bf16[64,128]{1,0:T(8,128)(2,1)S(1)}, bf16[64,128]{1,0:T(8,128)(2,1)S(1)}, bf16[288,128]{1,0:T(8,128)(2,1)S(1)}, bf16[288,128]{1,0:T(8,128)(2,1)S(1)}) custom-call(bf16[8,16,128]{2,1,0:T(8,128)(2,1)S(1)} %collective-permute-done.up_ref, bf16[8,16,128]{2,1,0:T(8,128)(2,1)S(1)} %collective-permute-done.1.down_ref, ...), custom_call_target="tpu_custom_call" | custom-call | flops 1000000000 | bytes 1048576 | tf_op jit(solution)/shard_map/halo/pallas_call | solution.py:360
  17.5 3.3 %collective-permute-start.2 = (bf16[288,128]{1,0:T(8,128)(2,1)S(1)}, bf16[288,128]{1,0:T(8,128)(2,1)S(1)}, u32[]{:S(2)}, u32[]{:S(2)}) collective-permute-start(bf16[288,128]{1,0:T(8,128)(2,1)S(1)} %get-tuple-element.83), channel_id=1, source_target_pairs={{0,1},{2,3},{4,5},{6,7},{8,9},{10,11},{12,13},{14,15},{1,0},{3,2},... | collective-permute-start | bytes 221192 | tf_op jit(solution)/shard_map/ppermute | solution.py:33
  20.8 4.1 %collective-permute-start.3 = (bf16[288,128]{1,0:T(8,128)(2,1)S(1)}, bf16[288,128]{1,0:T(8,128)(2,1)S(1)}, u32[]{:S(2)}, u32[]{:S(2)}) collective-permute-start(bf16[288,128]{1,0:T(8,128)(2,1)S(1)} %get-tuple-element.84), channel_id=1, source_target_pairs={{1,2},{3,4},{5,6},{7,8},{9,10},{11,12},{13,14},{15,0},{2,1},{4,3},... | collective-permute-start | bytes 221192 | tf_op jit(solution)/shard_map/ppermute | solution.py:33
  24.9 1.7 %middle.1 = (f32[512,128]{1,0:T(8,128)S(1)}, f32[64,512]{1,0:T(8,128)S(1)}, f32[64,512]{1,0:T(8,128)S(1)}, bf16[256,128]{1,0:T(8,128)(2,1)S(1)}, bf16[256,256]{1,0:T(8,128)(2,1)S(1)}) custom-call(f32[512,128]{1,0:T(8,128)S(1)} %get-tuple-element.85.fa_ref, bf16[512,128]{1,0:T(8,128)(2,1)S(1)} %get-tuple-element.86.na_ref, ...), custom_call_target="tpu_custom_call" | custom-call | flops 2000000000 | bytes 1048576 | tf_op jit(solution)/shard_map/middle/pallas_call | solution.py:360
  26.6 0.0 collective-permute-done.2.cols_even_ref
  26.6 4.1 %collective-permute-done.3.cols_odd_ref = bf16[288,128]{1,0:T(8,128)(2,1)S(1)} collective-permute-done((bf16[288,128]{1,0:T(8,128)(2,1)S(1)}, bf16[288,128]{1,0:T(8,128)(2,1)S(1)}, u32[]{:S(2)}, u32[]{:S(2)}) %collective-permute-start.3) | collective-permute-done | bytes 73760 | tf_op jit(solution)/shard_map/ppermute | solution.py:33
  30.7 2.4 %outer.1 = f32[64,16,128]{2,1,0:T(8,128)} custom-call(f32[512,128]{1,0:T(8,128)S(1)} %get-tuple-element.73.fb_ref, bf16[512,128]{1,0:T(8,128)(2,1)S(1)} %get-tuple-element.74.nb_ref, bf16[64,128]{1,0:T(8,128)(2,1)S(1)} %get-tuple-element.82.vb_ref, bf16[288,128]{1,0:T(8,128)(2,1)S(1)} %collective-permute-done.2.cols_even_ref, ...), custom_call_target="tpu_custom_call" | custom-call | flops 2000000000 | bytes 1048576 | tf_op jit(solution)/shard_map/outer/pallas_call | solution.py:360
  (3 shorter events, 0.0 us)
Async XLA Ops:
  0.0 0.7 %copy-start.3 = (f32[2,128]{1,0:T(2,128)S(1)}, f32[2,128]{1,0:T(2,128)}, u32[]{:S(2)}) copy-start(f32[2,128]{1,0:T(2,128)} %hg_ref.7) | copy-start | bytes 3076
  0.0 0.7 %copy-start.1 = (f32[2,4,225]{2,1,0:T(4,128)S(1)}, f32[2,4,225]{2,1,0:T(4,128)}, u32[]{:S(2)}) copy-start(f32[2,4,225]{2,1,0:T(4,128)} %pb_ref.3) | copy-start | bytes 21604
  0.0 0.7 %copy-start.2 = (f32[2,128]{1,0:T(2,128)S(1)}, f32[2,128]{1,0:T(2,128)}, u32[]{:S(2)}) copy-start(f32[2,128]{1,0:T(2,128)} %ag_ref.3) | copy-start | bytes 3076
  0.0 1.0 %copy-start = (bf16[64,16,128]{2,1,0:T(8,128)(2,1)S(1)}, bf16[64,16,128]{2,1,0:T(8,128)(2,1)}, u32[]{:S(2)}) copy-start(bf16[64,16,128]{2,1,0:T(8,128)(2,1)} %refs_0_.2) | copy-start | bytes 786436
  0.0 3.0 %copy-start.5 = (bf16[2,512,128]{2,1,0:T(8,128)(2,1)S(1)}, bf16[2,512,128]{2,1,0:T(8,128)(2,1)}, u32[]{:S(2)}) copy-start(bf16[2,512,128]{2,1,0:T(8,128)(2,1)} %ws_ref.5) | copy-start | bytes 786436
  0.0 3.0 %copy-start.6 = (bf16[2,128,384]{2,1,0:T(8,128)(2,1)S(1)}, bf16[2,128,384]{2,1,0:T(8,128)(2,1)}, u32[]{:S(2)}) copy-start(bf16[2,128,384]{2,1,0:T(8,128)(2,1)} %w_ref.1) | copy-start | bytes 589828
  0.0 3.0 %copy-start.7 = (bf16[2,128,128]{2,1,0:T(8,128)(2,1)S(1)}, bf16[2,128,128]{2,1,0:T(8,128)(2,1)}, u32[]{:S(2)}) copy-start(bf16[2,128,128]{2,1,0:T(8,128)(2,1)} %wo_ref.5) | copy-start | bytes 196612
  1.0 2.1 %copy-start.4 = (bf16[2,128,512]{2,1,0:T(8,128)(2,1)S(1)}, bf16[2,128,512]{2,1,0:T(8,128)(2,1)}, u32[]{:S(2)}) copy-start(bf16[2,128,512]{2,1,0:T(8,128)(2,1)} %we_ref.5) | copy-start | bytes 786436
  1.1 13.4 %collective-permute-start = (bf16[8,16,128]{2,1,0:T(8,128)(2,1)S(1)}, bf16[8,16,128]{2,1,0:T(8,128)(2,1)S(1)}, u32[]{:S(2)}, u32[]{:S(2)}) collective-permute-start(bf16[8,16,128]{2,1,0:T(8,128)(2,1)S(1)} %get-tuple-element.75), channel_id=1, source_target_pairs={{0,16},{16,32},{32,48},{48,64},{64,80},{80,96},{96,112},{112,128},... | collective-permute-start | bytes 98312 | tf_op jit(solution)/shard_map/ppermute | solution.py:27
  6.0 10.0 %collective-permute-start.1 = (bf16[8,16,128]{2,1,0:T(8,128)(2,1)S(1)}, bf16[8,16,128]{2,1,0:T(8,128)(2,1)S(1)}, u32[]{:S(2)}, u32[]{:S(2)}) collective-permute-start(bf16[8,16,128]{2,1,0:T(8,128)(2,1)S(1)} %get-tuple-element.76), channel_id=1, source_target_pairs={{0,496},{16,0},{32,16},{48,32},{64,48},{80,64},{96,80},{112,96},{1... | collective-permute-start | bytes 98312 | tf_op jit(solution)/shard_map/ppermute | solution.py:27
  17.5 9.1 %collective-permute-start.2 = (bf16[288,128]{1,0:T(8,128)(2,1)S(1)}, bf16[288,128]{1,0:T(8,128)(2,1)S(1)}, u32[]{:S(2)}, u32[]{:S(2)}) collective-permute-start(bf16[288,128]{1,0:T(8,128)(2,1)S(1)} %get-tuple-element.83), channel_id=1, source_target_pairs={{0,1},{2,3},{4,5},{6,7},{8,9},{10,11},{12,13},{14,15},{1,0},{3,2},... | collective-permute-start | bytes 221192 | tf_op jit(solution)/shard_map/ppermute | solution.py:33
  20.8 9.9 %collective-permute-start.3 = (bf16[288,128]{1,0:T(8,128)(2,1)S(1)}, bf16[288,128]{1,0:T(8,128)(2,1)S(1)}, u32[]{:S(2)}, u32[]{:S(2)}) collective-permute-start(bf16[288,128]{1,0:T(8,128)(2,1)S(1)} %get-tuple-element.84), channel_id=1, source_target_pairs={{1,2},{3,4},{5,6},{7,8},{9,10},{11,12},{13,14},{15,0},{2,1},{4,3},... | collective-permute-start | bytes 221192 | tf_op jit(solution)/shard_map/ppermute | solution.py:33

commit v12 on v10

--- a/solution.py
+++ b/solution.py
@@ -27,19 +27,18 @@
     return lax.ppermute(x, axis, [(i, (i + by) % length) for i in range(length)])
 
 
-def far(index, length):
-    place = index % (length // 2)
-    return (place == 0) | (place == length // 2 - 1)
+def swaps_early(index, length):
+    return index % (length // 2) < 2
 
 
 def near_first(x, axis):
     length = lax.axis_size(axis)
-    return lax.ppermute(x, axis, [(i ^ 1, i) for i in range(length) if far(i, length)])
+    return lax.ppermute(x, axis, [(i ^ 1, i) for i in range(length) if swaps_early(i, length)])
 
 
 def near_last(x, axis):
     length = lax.axis_size(axis)
-    return lax.ppermute(x, axis, [(i ^ 1, i) for i in range(length) if not far(i, length)])
+    return lax.ppermute(x, axis, [(i ^ 1, i) for i in range(length) if not swaps_early(i, length)])
 
 
 def swap(x, axis, first):
@@ -335,9 +334,9 @@
         return rows.astype(F32).reshape(-1, 8, 128)
 
     own = cat([vb_ref[32:64, :], nb_ref[...], vb_ref[0:32, :]]).astype(F32).reshape(-1, 8, 128)
-    is_far = far(lax.axis_index("gx"), lax.axis_size("gx"))
+    is_early = swaps_early(lax.axis_index("gx"), lax.axis_size("gx"))
     odd = in_order(odd_ref, h, 16)
-    even = jnp.where(is_far, in_order(early_ref, h, 16), in_order(even_ref, h, 16))
+    even = jnp.where(is_early, in_order(early_ref, h, 16), in_order(even_ref, h, 16))
     col_odd = lax.rem(lax.axis_index("gx"), 2) == 1
     hl, hr = jnp.where(col_odd, even, odd), jnp.where(col_odd, odd, even)
     low = low_half(hl.shape)

time: 33.1 us -> 33.8 us (1.021)
  the two profiles are of different devices: /device:TPU:8 before, /device:TPU:56 now
where the time goes in v12:
time: 33.8 us; the launch traced here: 33.6 us
  starting transfers between devices  19.6 us (58%)
  Pallas kernels  8.69 us (26%)
  waiting for transfers between devices  4.12 us (12%)
  local copies, waits for them, and re-layouts  0.96 us (3%)
    ppermute x2, starting transfers between devices, shift(): lax.ppermute(x, axis, [(i, (i + by) % length) for i in range(length)])  10.3 us
    pallas_call x7, Pallas kernels, call(): pl.pallas_call(kernel, out_shape=shapes, in_specs=vmem(len(operands)), ou...  8.69 us
    ppermute x1, starting transfers between devices, swap(): return lax.ppermute(x, axis, there + [(b, a) for a, b in there])  6.66 us
    ppermute x1, waiting for transfers between devices, near_last(): lax.ppermute(x, axis, [(i ^ 1, i) for i in range(length) if not swaps_ear...  2.58 us
    ppermute x1, starting transfers between devices, near_last(): lax.ppermute(x, axis, [(i ^ 1, i) for i in range(length) if not swaps_ear...  1.92 us
    ppermute x2, waiting for transfers between devices, shift(): lax.ppermute(x, axis, [(i, (i + by) % length) for i in range(length)])  1.53 us
    unnamed x16, local copies, waits for them, and re-layouts  0.96 us
  transfers between devices with their start and end apart: 5, of which 2 were waited for; matrix products, arithmetic and copies ran while one was open for 0% of the time, Pallas kernels for 14%

profile of v12, /device:TPU:56, one launch (start us, length us, event | category | flops | bytes accessed | tf_op | source)
XLA Modules:
  0.0 33.6 jit_solution(5801960047222206799)
XLA Ops:
  0.0 0.0 copy-start.3
  0.0 0.0 copy-start.1
  0.0 0.0 copy-start.2
  0.0 0.0 copy-start
  0.0 0.0 copy-start.5
  0.0 0.0 copy-start.6
  0.0 0.0 copy-start.7
  0.1 0.6 %copy-done.3 = f32[2,128]{1,0:T(2,128)S(1)} copy-done((f32[2,128]{1,0:T(2,128)S(1)}, f32[2,128]{1,0:T(2,128)}, u32[]{:S(2)}) %copy-start.3) | copy-done | bytes 1048
  0.7 0.0 copy-done.1
  0.7 0.0 copy-done.2
  0.7 0.3 copy-done
  1.0 0.0 copy-start.4
  1.0 0.1 edge_rows.1
  1.1 1.9 %collective-permute-start = (bf16[8,16,128]{2,1,0:T(8,128)(2,1)S(1)}, bf16[8,16,128]{2,1,0:T(8,128)(2,1)S(1)}, u32[]{:S(2)}, u32[]{:S(2)}) collective-permute-start(bf16[8,16,128]{2,1,0:T(8,128)(2,1)S(1)} %get-tuple-element.76), channel_id=1, source_target_pairs={{0,16},{16,32},{32,48},{48,64},{64,80},{80,96},{96,112},{112,128},... | collective-permute-start | bytes 98312 | tf_op jit(solution)/shard_map/ppermute | solution.py:27
  3.0 0.0 copy-done.5
  3.0 0.0 copy-done.6
  3.0 0.0 copy-done.7
  3.1 0.0 copy-done.4
  3.1 2.9 %conditional.1 = (bf16[8,16,128]{2,1,0:T(8,128)(2,1)S(1)}, f32[512,128]{1,0:T(8,128)S(1)}, f32[512,128]{1,0:T(8,128)S(1)}, bf16[512,128]{1,0:T(8,128)(2,1)S(1)},...) conditional(s32[]{:T(128)} %convert_element_type.3, ...), branch_computations={%region_0.0_spmd, %region_1.0_spmd} | conditional | flops 4000000000 | bytes 1114192 | solution.py:410
  3.1 2.9 %first.1 = (bf16[8,16,128]{2,1,0:T(8,128)(2,1)S(1)}, f32[512,128]{1,0:T(8,128)S(1)}, f32[512,128]{1,0:T(8,128)S(1)}, bf16[512,128]{1,0:T(8,128)(2,1)S(1)}, bf16[...) custom-call(bf16[64,16,128]{2,1,0:T(8,128)(2,1)S(1)} %get-tuple-elem, ...), custom_call_target="tpu_custom_call", output_to_operand_aliasing={{0}: (8, {})} | custom-call | flops 4000000000 | bytes 1048576 | tf_op jit(solution)/shard_map/cond/branch_1_fun/first/pallas_call | solution.py:377
  6.0 8.4 %collective-permute-start.1 = (bf16[8,16,128]{2,1,0:T(8,128)(2,1)S(1)}, bf16[8,16,128]{2,1,0:T(8,128)(2,1)S(1)}, u32[]{:S(2)}, u32[]{:S(2)}) collective-permute-start(bf16[8,16,128]{2,1,0:T(8,128)(2,1)S(1)} %get-tuple-element.77), channel_id=1, source_target_pairs={{0,496},{16,0},{32,16},{48,32},{64,48},{80,64},{96,80},{112,96},{1... | collective-permute-start | bytes 98312 | tf_op jit(solution)/shard_map/ppermute | solution.py:27
  14.5 0.0 collective-permute-done.up_ref
  14.5 1.5 %collective-permute-done.1.down_ref = bf16[8,16,128]{2,1,0:T(8,128)(2,1)S(1)} collective-permute-done((bf16[8,16,128]{2,1,0:T(8,128)(2,1)S(1)}, bf16[8,16,128]{2,1,0:T(8,128)(2,1)S(1)}, u32[]{:S(2)}, u32[]{:S(2)}) %collective-permute-start.1) | collective-permute-done | bytes 32800 | tf_op jit(solution)/shard_map/ppermute | solution.py:27
  16.0 1.5 %halo.1 = (bf16[64,128]{1,0:T(8,128)(2,1)S(1)}, bf16[64,128]{1,0:T(8,128)(2,1)S(1)}, bf16[288,128]{1,0:T(8,128)(2,1)S(1)}, bf16[288,128]{1,0:T(8,128)(2,1)S(1)}, bf16[288,128]{1,0:T(8,128)(2,1)S(1)}) custom-call(bf16[8,16,128]{2,1,0:T(8,128)(2,1)S(1)} %collective-permute-done.up_ref, bf16[8,16,128]{2,1,0:T(8,128)(2,1)S(1)} %collective-permute-done.1.down_ref, ...), custom_call_target="tpu_custom_call" | custom-call | flops 1000000000 | bytes 1048576 | tf_op jit(solution)/shard_map/halo/pallas_call | solution.py:377
  17.5 0.7 %collective-permute-start.2 = (bf16[288,128]{1,0:T(8,128)(2,1)S(1)}, bf16[288,128]{1,0:T(8,128)(2,1)S(1)}, u32[]{:S(2)}, u32[]{:S(2)}) collective-permute-start(bf16[288,128]{1,0:T(8,128)(2,1)S(1)} %get-tuple-element.84), channel_id=1, source_target_pairs={{1,0},{0,1},{9,8},{8,9},{17,16},{16,17},{25,24},{24,25},{33,32},{3... | collective-permute-start | bytes 221192 | tf_op jit(solution)/shard_map/ppermute | solution.py:36
  18.2 6.7 %collective-permute-start.3 = (bf16[288,128]{1,0:T(8,128)(2,1)S(1)}, bf16[288,128]{1,0:T(8,128)(2,1)S(1)}, u32[]{:S(2)}, u32[]{:S(2)}) collective-permute-start(bf16[288,128]{1,0:T(8,128)(2,1)S(1)} %get-tuple-element.85), channel_id=1, source_target_pairs={{1,2},{3,4},{5,6},{7,8},{9,10},{11,12},{13,14},{15,0},{2,1},{4,3},... | collective-permute-start | bytes 221192 | tf_op jit(solution)/shard_map/ppermute | solution.py:47
  24.9 1.9 %collective-permute-start.4 = (bf16[288,128]{1,0:T(8,128)(2,1)S(1)}, bf16[288,128]{1,0:T(8,128)(2,1)S(1)}, u32[]{:S(2)}, u32[]{:S(2)}) collective-permute-start(bf16[288,128]{1,0:T(8,128)(2,1)S(1)} %get-tuple-element.86), channel_id=1, source_target_pairs={{3,2},{2,3},{5,4},{4,5},{7,6},{6,7},{11,10},{10,11},{13,12},{12,13... | collective-permute-start | bytes 221192 | tf_op jit(solution)/shard_map/ppermute | solution.py:41
  26.8 1.7 %middle.1 = (f32[512,128]{1,0:T(8,128)S(1)}, f32[64,512]{1,0:T(8,128)S(1)}, f32[64,512]{1,0:T(8,128)S(1)}, bf16[256,128]{1,0:T(8,128)(2,1)S(1)}, bf16[256,256]{1,0:T(8,128)(2,1)S(1)}) custom-call(f32[512,128]{1,0:T(8,128)S(1)} %get-tuple-element.87.fa_ref, bf16[512,128]{1,0:T(8,128)(2,1)S(1)} %get-tuple-element.88.na_ref, ...), custom_call_target="tpu_custom_call" | custom-call | flops 2000000000 | bytes 1048576 | tf_op jit(solution)/shard_map/middle/pallas_call | solution.py:377
  28.5 0.0 collective-permute-done.2.early_ref
  28.5 0.0 collective-permute-done.3.odd_ref
  28.5 2.6 %collective-permute-done.4.even_ref = bf16[288,128]{1,0:T(8,128)(2,1)S(1)} collective-permute-done((bf16[288,128]{1,0:T(8,128)(2,1)S(1)}, bf16[288,128]{1,0:T(8,128)(2,1)S(1)}, u32[]{:S(2)}, u32[]{:S(2)}) %collective-permute-start.4) | collective-permute-done | bytes 73760 | tf_op jit(solution)/shard_map/ppermute | solution.py:41
  31.1 2.4 %outer.1 = f32[64,16,128]{2,1,0:T(8,128)} custom-call(f32[512,128]{1,0:T(8,128)S(1)} %get-tuple-element.74.fb_ref, bf16[512,128]{1,0:T(8,128)(2,1)S(1)} %get-tuple-element.75.nb_ref, bf16[64,128]{1,0:T(8,128)(2,1)S(1)} %get-tuple-element.83.vb_ref, bf16[288,128]{1,0:T(8,128)(2,1)S(1)} %collective-permute-done.2.early_ref, ...), custom_call_target="tpu_custom_call" | custom-call | flops 2000000000 | bytes 1048576 | tf_op jit(solution)/shard_map/outer/pallas_call | solution.py:377
  (3 shorter events, 0.0 us)
Async XLA Ops:
  0.0 0.7 %copy-start.3 = (f32[2,128]{1,0:T(2,128)S(1)}, f32[2,128]{1,0:T(2,128)}, u32[]{:S(2)}) copy-start(f32[2,128]{1,0:T(2,128)} %hg_ref.7) | copy-start | bytes 3076
  0.0 0.7 %copy-start.1 = (f32[2,4,225]{2,1,0:T(4,128)S(1)}, f32[2,4,225]{2,1,0:T(4,128)}, u32[]{:S(2)}) copy-start(f32[2,4,225]{2,1,0:T(4,128)} %pb_ref.3) | copy-start | bytes 21604
  0.0 0.7 %copy-start.2 = (f32[2,128]{1,0:T(2,128)S(1)}, f32[2,128]{1,0:T(2,128)}, u32[]{:S(2)}) copy-start(f32[2,128]{1,0:T(2,128)} %ag_ref.3) | copy-start | bytes 3076
  0.0 1.0 %copy-start = (bf16[64,16,128]{2,1,0:T(8,128)(2,1)S(1)}, bf16[64,16,128]{2,1,0:T(8,128)(2,1)}, u32[]{:S(2)}) copy-start(bf16[64,16,128]{2,1,0:T(8,128)(2,1)} %refs_0_.2) | copy-start | bytes 786436
  0.0 3.0 %copy-start.5 = (bf16[2,512,128]{2,1,0:T(8,128)(2,1)S(1)}, bf16[2,512,128]{2,1,0:T(8,128)(2,1)}, u32[]{:S(2)}) copy-start(bf16[2,512,128]{2,1,0:T(8,128)(2,1)} %ws_ref.5) | copy-start | bytes 786436
  0.0 3.0 %copy-start.6 = (bf16[2,128,384]{2,1,0:T(8,128)(2,1)S(1)}, bf16[2,128,384]{2,1,0:T(8,128)(2,1)}, u32[]{:S(2)}) copy-start(bf16[2,128,384]{2,1,0:T(8,128)(2,1)} %w_ref.1) | copy-start | bytes 589828
  0.0 3.0 %copy-start.7 = (bf16[2,128,128]{2,1,0:T(8,128)(2,1)S(1)}, bf16[2,128,128]{2,1,0:T(8,128)(2,1)}, u32[]{:S(2)}) copy-start(bf16[2,128,128]{2,1,0:T(8,128)(2,1)} %wo_ref.5) | copy-start | bytes 196612
  1.0 2.1 %copy-start.4 = (bf16[2,128,512]{2,1,0:T(8,128)(2,1)S(1)}, bf16[2,128,512]{2,1,0:T(8,128)(2,1)}, u32[]{:S(2)}) copy-start(bf16[2,128,512]{2,1,0:T(8,128)(2,1)} %we_ref.5) | copy-start | bytes 786436
  1.1 13.4 %collective-permute-start = (bf16[8,16,128]{2,1,0:T(8,128)(2,1)S(1)}, bf16[8,16,128]{2,1,0:T(8,128)(2,1)S(1)}, u32[]{:S(2)}, u32[]{:S(2)}) collective-permute-start(bf16[8,16,128]{2,1,0:T(8,128)(2,1)S(1)} %get-tuple-element.76), channel_id=1, source_target_pairs={{0,16},{16,32},{32,48},{48,64},{64,80},{80,96},{96,112},{112,128},... | collective-permute-start | bytes 98312 | tf_op jit(solution)/shard_map/ppermute | solution.py:27
  6.0 10.0 %collective-permute-start.1 = (bf16[8,16,128]{2,1,0:T(8,128)(2,1)S(1)}, bf16[8,16,128]{2,1,0:T(8,128)(2,1)S(1)}, u32[]{:S(2)}, u32[]{:S(2)}) collective-permute-start(bf16[8,16,128]{2,1,0:T(8,128)(2,1)S(1)} %get-tuple-element.77), channel_id=1, source_target_pairs={{0,496},{16,0},{32,16},{48,32},{64,48},{80,64},{96,80},{112,96},{1... | collective-permute-start | bytes 98312 | tf_op jit(solution)/shard_map/ppermute | solution.py:27
  17.5 11.0 %collective-permute-start.2 = (bf16[288,128]{1,0:T(8,128)(2,1)S(1)}, bf16[288,128]{1,0:T(8,128)(2,1)S(1)}, u32[]{:S(2)}, u32[]{:S(2)}) collective-permute-start(bf16[288,128]{1,0:T(8,128)(2,1)S(1)} %get-tuple-element.84), channel_id=1, source_target_pairs={{1,0},{0,1},{9,8},{8,9},{17,16},{16,17},{25,24},{24,25},{33,32},{3... | collective-permute-start | bytes 221192 | tf_op jit(solution)/shard_map/ppermute | solution.py:36
  18.2 10.3 %collective-permute-start.3 = (bf16[288,128]{1,0:T(8,128)(2,1)S(1)}, bf16[288,128]{1,0:T(8,128)(2,1)S(1)}, u32[]{:S(2)}, u32[]{:S(2)}) collective-permute-start(bf16[288,128]{1,0:T(8,128)(2,1)S(1)} %get-tuple-element.85), channel_id=1, source_target_pairs={{1,2},{3,4},{5,6},{7,8},{9,10},{11,12},{13,14},{15,0},{2,1},{4,3},... | collective-permute-start | bytes 221192 | tf_op jit(solution)/shard_map/ppermute | solution.py:47
  24.9 6.2 %collective-permute-start.4 = (bf16[288,128]{1,0:T(8,128)(2,1)S(1)}, bf16[288,128]{1,0:T(8,128)(2,1)S(1)}, u32[]{:S(2)}, u32[]{:S(2)}) collective-permute-start(bf16[288,128]{1,0:T(8,128)(2,1)S(1)} %get-tuple-element.86), channel_id=1, source_target_pairs={{3,2},{2,3},{5,4},{4,5},{7,6},{6,7},{11,10},{10,11},{13,12},{12,13... | collective-permute-start | bytes 221192 | tf_op jit(solution)/shard_map/ppermute | solution.py:41

commit v13 on v11

--- a/solution.py
+++ b/solution.py
@@ -174,7 +174,7 @@
     low = low_half(even.shape)
     right = jnp.where(low, even, pltpu.roll(odd, 4, 1)).reshape(-1, 128)
     left = jnp.where(low, pltpu.roll(even, 4, 1), odd).reshape(-1, 128)
-    return right.astype(BF16), left.astype(BF16)
+    return right, left
 
 
 def goes_first():
@@ -184,7 +184,7 @@
 
 def own_block(
     x_ref, w_ref, wo_ref, we_ref, ws_ref, ag_ref, pb_ref, hg_ref,
-    fa_ref, fb_ref, na_ref, nb_ref, right_ref, left_ref, bias_ref, wqv_ref, wk_ref,
+    fa_ref, fright_ref, fleft_ref, na_ref, right_ref, left_ref, bias_ref, wqv_ref, wk_ref,
 ):
     for head, yj, values in bias_rows(pb_ref, 0):
         bias_ref[yj * 8 : yj * 8 + 8, head * 128 : head * 128 + 128] = values
@@ -198,11 +198,13 @@
     units = [([b], masks, bias_ref[...]) for b in range(bands)]
     context = attention(qv[0:128], keys, qv[128:256], units)
     out = finish(z, context, wo_ref[0], hg_ref[0:1, :], we_ref[0], ws_ref[0])
-    fa_ref[...], fb_ref[...] = shifted_columns(out)
+    fa_ref[...], fb = shifted_columns(out)
+    fright_ref[...], fleft_ref[...] = edges(fb)
     na, nb = shifted_columns(layer_norm(out, ag_ref[1:2, :]))
     na_ref[...] = na.astype(BF16)
-    nb_ref[...] = nb.astype(BF16)
-    right_ref[...], left_ref[...] = edges(nb)
+    right, left = edges(nb)
+    right_ref[...] = right.astype(BF16)
+    left_ref[...] = left.astype(BF16)
 
 
 def start_kernel(out_ref):
@@ -237,7 +239,7 @@
 
 def halo_kernel(
     up_ref, down_ref, own_right_ref, own_left_ref, bias_ref, wqv_ref, wk_ref, wo_ref, we_ref, ws_ref, ag_ref, hg_ref,
-    na_ref, nb_ref, cols_odd_ref, cols_even_ref,
+    na_ref, cols_odd_ref, cols_even_ref,
 ):
     z = cat(windows_of(down_ref[...]) + windows_of(up_ref[...]))
     normed = layer_norm(z, ag_ref[0:1, :]).astype(BF16)
@@ -253,7 +255,6 @@
     out = finish(wanted(z), context, wo_ref[0], hg_ref[0:1, :], we_ref[0], ws_ref[0])
     na, nb = shifted_columns(layer_norm(out, ag_ref[1:2, :]))
     na_ref[...] = na.astype(BF16)
-    nb_ref[...] = nb.astype(BF16)
     right, left = edges(nb)
     n = own_right_ref.shape[0]
     col_odd = lax.rem(lax.axis_index("gx"), 2) == 1
@@ -263,27 +264,63 @@
         cols_even_ref[at : at + size, :] = jnp.where(col_odd, b, a).astype(BF16)
 
 
+def border_bias(pb_ref, block, tables):
+    sub = iota((8, 128), 0)
+    lane = iota((8, 128), 1)
+    yi = (lane >> 2) & 7
+    row, rows = lax.axis_index("gy"), lax.axis_size("gy")
+    col, cols = lax.axis_index("gx"), lax.axis_size("gx")
+    is_odd = lax.rem(col, 2) == 1
+    last_row = (lane >= 96) & (jnp.where(yi < 4, rows - 1, 0) == row)
+    for head in range(HEADS):
+        low = jnp.broadcast_to(pb_ref[block, head : head + 1, 0:128], (8, 128))
+        high = jnp.broadcast_to(pb_ref[block, head : head + 1, 97:225], (8, 128))
+        for group in range(8):
+            yj = 2 * (group % 4) + (sub >> 2)
+            cut_row = last_row & ((yi < 4) != (yj < 4))
+            plain = (7 + yi - yj) * 15 + 7 + (lane & 3) - (sub & 3)
+            for number, (table, table_v) in enumerate(tables):
+                if group < 4 and number == 1:
+                    values = kept
+                    cut = values
+                else:
+                    is_right = is_odd if number == 0 else jnp.logical_not(is_odd)
+                    place = plain if group < 4 else plain + jnp.where(is_right, -4, 4)
+                    values = LOG2E * jnp.where(
+                        place < 128,
+                        jnp.take_along_axis(low, lax.clamp(0, place, 127), axis=1),
+                        jnp.take_along_axis(high, lax.clamp(0, place - 97, 127), axis=1),
+                    )
+                    if group >= 4:
+                        outside = jnp.where(is_right, cols - 1, 0) == col
+                        values = values - jnp.where(outside, 100.0 * LOG2E, 0.0)
+                    kept = values
+                at = (slice(group * 8, group * 8 + 8), slice(head * 128, head * 128 + 128))
+                table[at] = values
+                if group < 4:
+                    cut = values - 100.0 * LOG2E
+                else:
+                    outside = jnp.where(is_right, cols - 1, 0) == col
+                    cut = values - jnp.where(outside, 0.0, 100.0 * LOG2E)
+                table_v[at] = jnp.where(cut_row, cut, values)
+
+
 def middle_kernel(
     fa_ref, na_ref, va_ref, pb_ref, w_ref, wo_ref, we_ref, ws_ref, hg_ref,
-    out_ref, bias_b, bias_bv, wqv_ref, wk_ref,
+    out_ref, bias_odd, bias_oddv, bias_even, bias_evenv, wqv_ref, wk_ref,
     bias_a, bias_av,
 ):
     sub = iota((8, 128), 0)
     lane = iota((8, 128), 1)
-    query_left = (lane & 4) == 0
     query_up = (lane & 32) == 0
-    row, col = lax.axis_index("gy"), lax.axis_index("gx")
-    last_col = jnp.where(query_left, lax.axis_size("gx") - 1, 0) == col
+    row = lax.axis_index("gy")
     last_row = jnp.where(query_up, lax.axis_size("gy") - 1, 0) == row
-    cut_col = last_col & (query_left != (sub < 4))
     for head, yj, values in bias_rows(pb_ref, 1):
         at = (slice(yj * 8, yj * 8 + 8), slice(head * 128, head * 128 + 128))
-        cut = values - 100.0 * LOG2E
         cut_row = (lane >= 64) & last_row & (jnp.logical_not(query_up) if yj < 4 else query_up)
         bias_a[at] = values
-        bias_av[at] = jnp.where(cut_row, cut, values)
-        bias_b[at] = jnp.where(cut_col, cut, values)
-        bias_bv[at] = jnp.where(cut_row | cut_col, cut, values)
+        bias_av[at] = jnp.where(cut_row, values - 100.0 * LOG2E, values)
+    border_bias(pb_ref, 1, ((bias_odd, bias_oddv), (bias_even, bias_evenv)))
     fill_weights(w_ref[1], wqv_ref, wk_ref)
     n = na_ref.shape[0]
     inner = na_ref[32 : n - 32, :]
@@ -307,48 +344,56 @@
     out_ref[0:32, :] = out[n - 32 : n]
 
 
-def outer_kernel(
-    fb_ref, nb_ref, vb_ref, cols_even_ref, cols_odd_ref, oa_ref, bias_b, bias_bv, wqv_ref, wk_ref, wo_ref, we_ref, ws_ref, hg_ref,
-    out_ref,
-):
-    n = nb_ref.shape[0]
-    h = n // 2
-
-    def in_order(ref, end, size):
-        rows = cat([ref[end + size : end + 2 * size, :], ref[0:end, :], ref[end : end + size, :]])
-        return rows.astype(F32).reshape(-1, 8, 128)
-
-    own = cat([vb_ref[32:64, :], nb_ref[...], vb_ref[0:32, :]]).astype(F32).reshape(-1, 8, 128)
-    odd, even = in_order(cols_odd_ref, h, 16), in_order(cols_even_ref, h, 16)
-    col_odd = lax.rem(lax.axis_index("gx"), 2) == 1
-    hl, hr = jnp.where(col_odd, even, odd), jnp.where(col_odd, odd, even)
-    low = low_half(hl.shape)
-    even = jnp.where(low, hl, pltpu.roll(hr, 4, 1))
-    odd = jnp.where(low, pltpu.roll(hl, 4, 1), hr)
-    halo = jnp.stack([even, odd], axis=1).reshape(own.shape)
-    low = low_half(own.shape)
-    right = jnp.where(low, own, halo).reshape(-1, 64, 128).astype(BF16)
-    left = jnp.where(low, halo, own).reshape(-1, 64, 128).astype(BF16)
-    count = right.shape[0]
-    looked_at = cat([t for w in range(count) for t in (right[w], left[w])])
+def border_block(z_ref, own_ref, other_ref, bias_ref, bias_v_ref, wqv_ref, wk_ref, wo_ref, we_ref, ws_ref, hg_ref):
+    n = z_ref[0].shape[0]
+
+    def in_order(ref):
+        return cat([ref[n + 16 : n + 32, :], ref[0:n, :], ref[n : n + 16, :]])
+
+    own, other = in_order(own_ref), in_order(other_ref)
+    count = own.shape[0] // 32
+    order = [*range(1, count), 0, 0]
+    looked_at = cat([t[32 * w : 32 * w + 32] for w in order for t in (own, other)])
     keys = side_by_side(looked_at, wk_ref[...])
     values = dot(wqv_ref[128:256, :], looked_at, NT).astype(BF16)
-    wanted = cat([nb_ref[32:n, :], nb_ref[0:32, :]])
+    wanted = cat([own_ref[16:n, :], own_ref[0:16, :]])
     queries = dot(wqv_ref[0:128, :], wanted, NT).astype(BF16)
-    masks = [mask(w, s) for w in "12" for s in ("left", "right")]
-    units = [([w, w + 1], masks, bias_b[...]) for w in range(1, count - 2, 2)]
-    masks = masks[0:2] + [mask("2", v, s) for v in ("up", "down") for s in ("left", "right")]
-    units.append(([count - 2, count - 1, 0], masks, bias_bv[...]))
+    lane = iota((64, 128), 1)
+
+    def keep(condition):
+        return jnp.where(condition, 1.0, 0.0).astype(BF16)
+
+    masks = [keep((lane >> 5) == k) for k in range(4)]
+    up = (lane & 16) == 0
+    last = [keep((lane >= 96) & up), keep((lane >= 96) & jnp.logical_not(up)), keep(lane < 0)]
+    units = [([2 * u, 2 * u + 1], masks, bias_ref[...]) for u in range(n // 128 - 1)]
+    first = 2 * len(units)
+    units.append(([first, first + 1, first + 2], masks[0:3] + last, bias_v_ref[...]))
     context = attention(queries, keys, values, units)
-    z = cat([fb_ref[32:n, :], fb_ref[0:32, :]])
+    is_odd = lax.rem(lax.axis_index("gx"), 2) == 1
+    z = jnp.where(is_odd, z_ref[0][...], z_ref[1][...])
+    z = cat([z[16:n], z[0:16]])
     out = finish(z, context, wo_ref[1], hg_ref[1:2, :], we_ref[1], ws_ref[1])
-    out = half_turn(out)
-    rows = n // 8
-    out = cat([out[rows - 4 :], out[: rows - 4]])
-    inner = oa_ref[...].reshape(rows, 8, 128)
-    low = low_half(out.shape)
-    out_ref[:, 0:8, :] = jnp.where(low, out, inner)
-    out_ref[:, 8:16, :] = jnp.where(low, inner, out)
+    return cat([out[n - 16 : n], out[0 : n - 16]])
+
+
+def odd_border_kernel(fright_ref, fleft_ref, *refs):
+    refs[-1][...] = border_block((fright_ref, fleft_ref), *refs[:-2])
+
+
+def even_border_kernel(fright_ref, fleft_ref, *refs):
+    inner_ref, odd_ref, out_ref = refs[-3:]
+    even = border_block((fleft_ref, fright_ref), *refs[:-3])
+    odd = odd_ref[...]
+    is_odd = lax.rem(lax.axis_index("gx"), 2) == 1
+    right = jnp.where(is_odd, odd, even).reshape(-1, 8, 128)
+    left = jnp.where(is_odd, even, odd).reshape(-1, 8, 128)
+    inner = inner_ref[...].reshape(-1, 8, 128)
+    right = jnp.stack([pltpu.roll(right, 4, 1), right], axis=1).reshape(inner.shape)
+    left = jnp.stack([left, pltpu.roll(left, 4, 1)], axis=1).reshape(inner.shape)
+    low = low_half(inner.shape)
+    out_ref[:, 0:8, :] = jnp.where(low, left, inner)
+    out_ref[:, 8:16, :] = jnp.where(low, inner, right)
 
 
 def vmem(count):
@@ -376,7 +421,8 @@
     table = ((64, HEADS * 128), F32)
     prepared = [((256, 128), BF16), ((256, 256), BF16)]
     weights = (x, tw, ow, ew, sw, ag, pb, hg)
-    kept = [((n, C), F32)] * 2 + [((n, C), BF16)] * 2 + [((n // 2, C), BF16)] * 2 + [table] + prepared
+    kept = [((n, C), F32)] + [((n // 2, C), F32)] * 2 + [((n, C), BF16)] + [((n // 2, C), BF16)] * 2
+    kept += [table] + prepared
     rows = [((WIN, breadth, C), BF16)] * 2
     (start,) = call(start_kernel, "start", (), [((8, 128), jnp.int32)], (), 4 * 10**10)
     last, first = call(
@@ -395,19 +441,24 @@
     state = call(
         second_kernel, "second", (*weights, *state), kept, (), 4 * 10**9, {8 + i: i for i in range(9)}
     )
-    fa, fb, na, nb, right, left, bias, wqv, wk = state
-    va, vb, odd, even = call(
+    fa, fright, fleft, na, right, left, bias, wqv, wk = state
+    va, odd, even = call(
         halo_kernel, "halo", (up, down, right, left, bias, wqv, wk, ow, ew, sw, ag, hg),
-        [((64, C), BF16)] * 2 + [((n // 2 + 32, C), BF16)] * 2, (), 10**9,
-    )
-    even, odd = swap(even, "gx", 0), swap(odd, "gx", 1)
-    oa, bias_b, bias_bv, wqv, wk = call(
+        [((64, C), BF16)] + [((n // 2 + 32, C), BF16)] * 2, (), 10**9,
+    )
+    from_odd, from_even = swap(odd, "gx", 1), swap(even, "gx", 0)
+    oa, *tables, wqv, wk = call(
         middle_kernel, "middle", (fa, na, va, pb, tw, ow, ew, sw, hg),
-        [((n, C), F32), table, table] + prepared, [pltpu.VMEM(*table)] * 2, 2 * 10**9,
+        [((n, C), F32)] + [table] * 4 + prepared, [pltpu.VMEM(*table)] * 2, 2 * 10**9,
+    )
+    rest = (wqv, wk, ow, ew, sw, hg)
+    (ob,) = call(
+        odd_border_kernel, "odd_border", (fright, fleft, odd, from_odd, *tables[0:2], *rest, even),
+        [((n // 2, C), F32)], (), 10**9,
     )
     return call(
-        outer_kernel, "outer", (fb, nb, vb, even, odd, oa, bias_b, bias_bv, wqv, wk, ow, ew, sw, hg),
-        [((height, breadth, C), F32)], (), 2 * 10**9,
+        even_border_kernel, "even_border", (fright, fleft, even, from_even, *tables[2:4], *rest, oa, ob),
+        [((height, breadth, C), F32)], (), 10**9,
     )[0]
 
 

time: 33.3 us -> 33.2 us (level)
  the two profiles are of different devices: /device:TPU:56 before, /device:TPU:8 now
where the time goes in v13:
time: 33.2 us; the launch traced here: 32.9 us
  starting transfers between devices  20.2 us (61%)
  Pallas kernels  10 us (30%)
  waiting for transfers between devices  1.54 us (5%)
  local copies, waits for them, and re-layouts  0.96 us (3%)
    ppermute x2, starting transfers between devices, shift(): lax.ppermute(x, axis, [(i, (i + by) % length) for i in range(length)])  10.3 us
    pallas_call x8, Pallas kernels, call(): pl.pallas_call(kernel, out_shape=shapes, in_specs=vmem(len(operands)), ou...  10 us
    ppermute x2, starting transfers between devices, swap(): return lax.ppermute(x, axis, there + [(b, a) for a, b in there])  9.9 us
    ppermute x2, waiting for transfers between devices, shift(): lax.ppermute(x, axis, [(i, (i + by) % length) for i in range(length)])  1.53 us
    unnamed x16, local copies, waits for them, and re-layouts  0.96 us
  transfers between devices with their start and end apart: 4, of which 1 were waited for; matrix products, arithmetic and copies ran while one was open for 0% of the time, Pallas kernels for 19%

profile of v13, /device:TPU:8, one launch (start us, length us, event | category | flops | bytes accessed | tf_op | source)
XLA Modules:
  0.0 32.9 jit_solution(15823791541450472125)
XLA Ops:
  0.0 0.0 copy-start.3
  0.0 0.0 copy-start.1
  0.0 0.0 copy-start.2
  0.0 0.0 copy-start
  0.0 0.0 copy-start.5
  0.0 0.0 copy-start.6
  0.0 0.0 copy-start.7
  0.1 0.6 %copy-done.3 = f32[2,128]{1,0:T(2,128)S(1)} copy-done((f32[2,128]{1,0:T(2,128)S(1)}, f32[2,128]{1,0:T(2,128)}, u32[]{:S(2)}) %copy-start.3) | copy-done | bytes 1048
  0.7 0.0 copy-done.1
  0.7 0.0 copy-done.2
  0.7 0.3 copy-done
  1.0 0.0 copy-start.4
  1.0 0.1 edge_rows.1
  1.1 1.9 %collective-permute-start = (bf16[8,16,128]{2,1,0:T(8,128)(2,1)S(1)}, bf16[8,16,128]{2,1,0:T(8,128)(2,1)S(1)}, u32[]{:S(2)}, u32[]{:S(2)}) collective-permute-start(bf16[8,16,128]{2,1,0:T(8,128)(2,1)S(1)} %get-tuple-element.76), channel_id=1, source_target_pairs={{0,16},{16,32},{32,48},{48,64},{64,80},{80,96},{96,112},{112,128},... | collective-permute-start | bytes 98312 | tf_op jit(solution)/shard_map/ppermute | solution.py:27
  3.0 0.0 copy-done.5
  3.0 0.0 copy-done.6
  3.0 0.0 copy-done.7
  3.1 0.0 copy-done.4
  3.1 2.9 %conditional.1 = (bf16[8,16,128]{2,1,0:T(8,128)(2,1)S(1)}, f32[512,128]{1,0:T(8,128)S(1)}, f32[256,128]{1,0:T(8,128)S(1)}, f32[256,128]{1,0:T(8,128)S(1)}, bf16[...) conditional(s32[]{:T(128)} %convert_element_type.3, ...), branch_computations={%region_0.0_spmd, %region_1.0_spmd} | conditional | flops 4000000000 | bytes 1114192 | solution.py:439
  3.1 2.9 %first.1 = (bf16[8,16,128]{2,1,0:T(8,128)(2,1)S(1)}, f32[512,128]{1,0:T(8,128)S(1)}, f32[256,128]{1,0:T(8,128)S(1)}, f32[256,128]{1,0:T(8,128)S(1)}, bf16[512,12...) custom-call(bf16[64,16,128]{2,1,0:T(8,128)(2,1)S(1)} %get-tuple-elem, ...), custom_call_target="tpu_custom_call", output_to_operand_aliasing={{0}: (8, {})} | custom-call | flops 4000000000 | bytes 1048576 | tf_op jit(solution)/shard_map/cond/branch_1_fun/first/pallas_call | solution.py:405
  6.0 8.4 %collective-permute-start.1 = (bf16[8,16,128]{2,1,0:T(8,128)(2,1)S(1)}, bf16[8,16,128]{2,1,0:T(8,128)(2,1)S(1)}, u32[]{:S(2)}, u32[]{:S(2)}) collective-permute-start(bf16[8,16,128]{2,1,0:T(8,128)(2,1)S(1)} %get-tuple-element.77), channel_id=1, source_target_pairs={{0,496},{16,0},{32,16},{48,32},{64,48},{80,64},{96,80},{112,96},{1... | collective-permute-start | bytes 98312 | tf_op jit(solution)/shard_map/ppermute | solution.py:27
  14.5 0.0 collective-permute-done.up_ref
  14.5 1.5 %collective-permute-done.1.down_ref = bf16[8,16,128]{2,1,0:T(8,128)(2,1)S(1)} collective-permute-done((bf16[8,16,128]{2,1,0:T(8,128)(2,1)S(1)}, bf16[8,16,128]{2,1,0:T(8,128)(2,1)S(1)}, u32[]{:S(2)}, u32[]{:S(2)}) %collective-permute-start.1) | collective-permute-done | bytes 32800 | tf_op jit(solution)/shard_map/ppermute | solution.py:27
  16.0 1.5 %halo.1 = (bf16[64,128]{1,0:T(8,128)(2,1)S(1)}, bf16[288,128]{1,0:T(8,128)(2,1)S(1)}, bf16[288,128]{1,0:T(8,128)(2,1)S(1)}) custom-call(bf16[8,16,128]{2,1,0:T(8,128)(2,1)S(1)} %collective-permute-done.up_ref, bf16[8,16,128]{2,1,0:T(8,128)(2,1)S(1)} %collective-permute-done.1.down_ref, bf16[256,128]{1,0:T(8,128)(2,1)S(1)} %get-tuple-element.78.own_right_ref, ...), custom_call_target="tpu_custom_call" | custom-call | flops 1000000000 | bytes 1048576 | tf_op jit(solution)/shard_map/halo/pallas_call | solution.py:405
  17.5 3.5 %collective-permute-start.3 = (bf16[288,128]{1,0:T(8,128)(2,1)S(1)}, bf16[288,128]{1,0:T(8,128)(2,1)S(1)}, u32[]{:S(2)}, u32[]{:S(2)}) collective-permute-start(bf16[288,128]{1,0:T(8,128)(2,1)S(1)} %get-tuple-element.92.refs_0_), channel_id=1, source_target_pairs={{1,2},{3,4},{5,6},{7,8},{9,10},{11,12},{13,14},{15,0},{2,1},{4,3},... | collective-permute-start | bytes 221192 | tf_op jit(solution)/shard_map/ppermute | solution.py:33
  21.0 6.4 %collective-permute-start.2 = (bf16[288,128]{1,0:T(8,128)(2,1)S(1)}, bf16[288,128]{1,0:T(8,128)(2,1)S(1)}, u32[]{:S(2)}, u32[]{:S(2)}) collective-permute-start(bf16[288,128]{1,0:T(8,128)(2,1)S(1)} %get-tuple-element.83.refs_10_.refs_0_), channel_id=1, source_target_pairs={{0,1},{2,3},{4,5},{6,7},{8,9},{10,11},{12,13},{14,15},{1,0},{3,2},... | collective-permute-start | bytes 221192 | tf_op jit(solution)/shard_map/ppermute | solution.py:33
  27.4 1.9 %middle.1 = (f32[512,128]{1,0:T(8,128)S(1)}, f32[64,512]{1,0:T(8,128)S(1)}, f32[64,512]{1,0:T(8,128)S(1)}, f32[64,512]{1,0:T(8,128)S(1)}, f32[64,512]{1,0:T(8,12...) custom-call(f32[512,128]{1,0:T(8,128)S(1)} %get-tuple-element.84.fa_ref, ...), custom_call_target="tpu_custom_call" | custom-call | flops 2000000000 | bytes 1048576 | tf_op jit(solution)/shard_map/middle/pallas_call | solution.py:405
  29.4 0.0 collective-permute-done.3.refs_1_
  29.4 1.4 %odd_border.1.refs_11_ = f32[256,128]{1,0:T(8,128)S(1)} custom-call(f32[256,128]{1,0:T(8,128)S(1)} %get-tuple-element.74.fright_ref, f32[256,128]{1,0:T(8,128)S(1)} %get-tuple-element.75.fleft_ref, bf16[288,128]{1,0:T(8,128)(2,1)S(1)} %get-tuple-element.92.refs_0_, bf16[288,128]{1,0:T(8,128)(2,1)S(1)} %collective-permute-done.3.refs_1_, ...), custom_call_target="tpu_custom_call" | custom-call | flops 1000000000 | bytes 1048576 | tf_op jit(solution)/shard_map/odd_border/pallas_call | solution.py:405
  30.8 0.0 collective-permute-done.2.refs_1_
  30.8 2.2 %even_border.1 = f32[64,16,128]{2,1,0:T(8,128)} custom-call(f32[256,128]{1,0:T(8,128)S(1)} %get-tuple-element.74.fright_ref, f32[256,128]{1,0:T(8,128)S(1)} %get-tuple-element.75.fleft_ref, bf16[288,128]{1,0:T(8,128)(2,1)S(1)} %get-tuple-element.83.refs_10_.refs_0_, bf16[288,128]{1,0:T(8,128)(2,1)S(1)} %collective-permute-done.2.refs_1_, ...), custom_call_target="tpu_custom_call" | custom-call | flops 1000000000 | bytes 1048576 | tf_op jit(solution)/shard_map/even_border/pallas_call | solution.py:405
  (3 shorter events, 0.0 us)
Async XLA Ops:
  0.0 0.7 %copy-start.3 = (f32[2,128]{1,0:T(2,128)S(1)}, f32[2,128]{1,0:T(2,128)}, u32[]{:S(2)}) copy-start(f32[2,128]{1,0:T(2,128)} %refs_9_.3) | copy-start | bytes 3076
  0.0 0.7 %copy-start.1 = (f32[2,4,225]{2,1,0:T(4,128)S(1)}, f32[2,4,225]{2,1,0:T(4,128)}, u32[]{:S(2)}) copy-start(f32[2,4,225]{2,1,0:T(4,128)} %pb_ref.3) | copy-start | bytes 21604
  0.0 0.7 %copy-start.2 = (f32[2,128]{1,0:T(2,128)S(1)}, f32[2,128]{1,0:T(2,128)}, u32[]{:S(2)}) copy-start(f32[2,128]{1,0:T(2,128)} %ag_ref.3) | copy-start | bytes 3076
  0.0 1.0 %copy-start = (bf16[64,16,128]{2,1,0:T(8,128)(2,1)S(1)}, bf16[64,16,128]{2,1,0:T(8,128)(2,1)}, u32[]{:S(2)}) copy-start(bf16[64,16,128]{2,1,0:T(8,128)(2,1)} %refs_0_.2) | copy-start | bytes 786436
  0.0 3.0 %copy-start.5 = (bf16[2,512,128]{2,1,0:T(8,128)(2,1)S(1)}, bf16[2,512,128]{2,1,0:T(8,128)(2,1)}, u32[]{:S(2)}) copy-start(bf16[2,512,128]{2,1,0:T(8,128)(2,1)} %refs_8_.3) | copy-start | bytes 786436
  0.0 3.0 %copy-start.6 = (bf16[2,128,384]{2,1,0:T(8,128)(2,1)S(1)}, bf16[2,128,384]{2,1,0:T(8,128)(2,1)}, u32[]{:S(2)}) copy-start(bf16[2,128,384]{2,1,0:T(8,128)(2,1)} %w_ref.1) | copy-start | bytes 589828
  0.0 3.0 %copy-start.7 = (bf16[2,128,128]{2,1,0:T(8,128)(2,1)S(1)}, bf16[2,128,128]{2,1,0:T(8,128)(2,1)}, u32[]{:S(2)}) copy-start(bf16[2,128,128]{2,1,0:T(8,128)(2,1)} %refs_6_.5) | copy-start | bytes 196612
  1.0 2.1 %copy-start.4 = (bf16[2,128,512]{2,1,0:T(8,128)(2,1)S(1)}, bf16[2,128,512]{2,1,0:T(8,128)(2,1)}, u32[]{:S(2)}) copy-start(bf16[2,128,512]{2,1,0:T(8,128)(2,1)} %refs_7_.5) | copy-start | bytes 786436
  1.1 13.4 %collective-permute-start = (bf16[8,16,128]{2,1,0:T(8,128)(2,1)S(1)}, bf16[8,16,128]{2,1,0:T(8,128)(2,1)S(1)}, u32[]{:S(2)}, u32[]{:S(2)}) collective-permute-start(bf16[8,16,128]{2,1,0:T(8,128)(2,1)S(1)} %get-tuple-element.76), channel_id=1, source_target_pairs={{0,16},{16,32},{32,48},{48,64},{64,80},{80,96},{96,112},{112,128},... | collective-permute-start | bytes 98312 | tf_op jit(solution)/shard_map/ppermute | solution.py:27
  6.0 10.0 %collective-permute-start.1 = (bf16[8,16,128]{2,1,0:T(8,128)(2,1)S(1)}, bf16[8,16,128]{2,1,0:T(8,128)(2,1)S(1)}, u32[]{:S(2)}, u32[]{:S(2)}) collective-permute-start(bf16[8,16,128]{2,1,0:T(8,128)(2,1)S(1)} %get-tuple-element.77), channel_id=1, source_target_pairs={{0,496},{16,0},{32,16},{48,32},{64,48},{80,64},{96,80},{112,96},{1... | collective-permute-start | bytes 98312 | tf_op jit(solution)/shard_map/ppermute | solution.py:27
  17.5 11.9 %collective-permute-start.3 = (bf16[288,128]{1,0:T(8,128)(2,1)S(1)}, bf16[288,128]{1,0:T(8,128)(2,1)S(1)}, u32[]{:S(2)}, u32[]{:S(2)}) collective-permute-start(bf16[288,128]{1,0:T(8,128)(2,1)S(1)} %get-tuple-element.92.refs_0_), channel_id=1, source_target_pairs={{1,2},{3,4},{5,6},{7,8},{9,10},{11,12},{13,14},{15,0},{2,1},{4,3},... | collective-permute-start | bytes 221192 | tf_op jit(solution)/shard_map/ppermute | solution.py:33
  21.0 9.8 %collective-permute-start.2 = (bf16[288,128]{1,0:T(8,128)(2,1)S(1)}, bf16[288,128]{1,0:T(8,128)(2,1)S(1)}, u32[]{:S(2)}, u32[]{:S(2)}) collective-permute-start(bf16[288,128]{1,0:T(8,128)(2,1)S(1)} %get-tuple-element.83.refs_10_.refs_0_), channel_id=1, source_target_pairs={{0,1},{2,3},{4,5},{6,7},{8,9},{10,11},{12,13},{14,15},{1,0},{3,2},... | collective-permute-start | bytes 221192 | tf_op jit(solution)/shard_map/ppermute | solution.py:33

commit v14 on v13

--- a/solution.py
+++ b/solution.py
@@ -344,6 +344,24 @@
     out_ref[0:32, :] = out[n - 32 : n]
 
 
+def beside_far_border():
+    col, cols = lax.axis_index("gx"), lax.axis_size("gx")
+    place = lax.rem(col, cols // 2)
+    return (place == 0) | (place == cols // 2 - 1)
+
+
+def middle_early_kernel(*refs):
+    @pl.when(jnp.logical_not(beside_far_border()))
+    def _():
+        middle_kernel(*refs[0:9], *refs[11:])
+
+
+def middle_late_kernel(*refs):
+    @pl.when(beside_far_border())
+    def _():
+        middle_kernel(*refs[0:9], *refs[16:])
+
+
 def border_block(z_ref, own_ref, other_ref, bias_ref, bias_v_ref, wqv_ref, wk_ref, wo_ref, we_ref, ws_ref, hg_ref):
     n = z_ref[0].shape[0]
 
@@ -446,10 +464,18 @@
         halo_kernel, "halo", (up, down, right, left, bias, wqv, wk, ow, ew, sw, ag, hg),
         [((64, C), BF16)] + [((n // 2 + 32, C), BF16)] * 2, (), 10**9,
     )
-    from_odd, from_even = swap(odd, "gx", 1), swap(even, "gx", 0)
+    from_odd = swap(odd, "gx", 1)
+    inputs = (fa, na, va, pb, tw, ow, ew, sw, hg)
+    made = [((n, C), F32)] + [table] * 4 + prepared
+    scratch = [pltpu.VMEM(*table)] * 2
+    even, *state = call(
+        middle_early_kernel, "middle_early", (*inputs, even), [(even.shape, BF16)] + made, scratch,
+        2 * 10**9, {9: 0},
+    )
+    from_even = swap(even, "gx", 0)
     oa, *tables, wqv, wk = call(
-        middle_kernel, "middle", (fa, na, va, pb, tw, ow, ew, sw, hg),
-        [((n, C), F32)] + [table] * 4 + prepared, [pltpu.VMEM(*table)] * 2, 2 * 10**9,
+        middle_late_kernel, "middle_late", (*inputs, *state), made, scratch, 2 * 10**9,
+        {9 + i: i for i in range(7)},
     )
     rest = (wqv, wk, ow, ew, sw, hg)
     (ob,) = call(

time: 33.2 us -> 37.4 us (1.13)
  the two profiles are of different devices: /device:TPU:8 before, /device:TPU:24 now
where the time goes in v14:
time: 37.4 us; the launch traced here: 37.1 us
  starting transfers between devices  16.9 us (45%)
  Pallas kernels  10.1 us (27%)
  waiting for transfers between devices  8.28 us (22%)
  local copies, waits for them, and re-layouts  1.67 us (4%)
    ppermute x2, starting transfers between devices, shift(): lax.ppermute(x, axis, [(i, (i + by) % length) for i in range(length)])  10.3 us
    pallas_call x9, Pallas kernels, call(): pl.pallas_call(kernel, out_shape=shapes, in_specs=vmem(len(operands)), ou...  10.1 us
    ppermute x2, starting transfers between devices, swap(): return lax.ppermute(x, axis, there + [(b, a) for a, b in there])  6.61 us
    ppermute x2, waiting for transfers between devices, shift(): lax.ppermute(x, axis, [(i, (i + by) % length) for i in range(length)])  5.37 us
    ppermute x2, waiting for transfers between devices, swap(): return lax.ppermute(x, axis, there + [(b, a) for a, b in there])  2.91 us
    unnamed x16, local copies, waits for them, and re-layouts  1.67 us
  transfers between devices with their start and end apart: 4, of which 2 were waited for; matrix products, arithmetic and copies ran while one was open for 0% of the time, Pallas kernels for 9%

profile of v14, /device:TPU:24, one launch (start us, length us, event | category | flops | bytes accessed | tf_op | source)
XLA Modules:
  0.0 37.1 jit_solution(14275581280496994929)
XLA Ops:
  0.0 0.0 copy-start
  0.0 0.0 copy-start.3
  0.0 0.0 copy-start.4
  0.0 0.0 copy-start.5
  0.0 0.0 copy-start.6
  0.0 0.0 copy-start.1
  0.1 0.0 copy-start.2
  0.1 0.9 %copy-done = bf16[64,16,128]{2,1,0:T(8,128)(2,1)S(1)} copy-done((bf16[64,16,128]{2,1,0:T(8,128)(2,1)S(1)}, bf16[64,16,128]{2,1,0:T(8,128)(2,1)}, u32[]{:S(2)}) %copy-start) | copy-done | bytes 262168
  1.0 0.0 copy-done.3
  1.0 0.0 copy-done.1
  1.0 0.0 copy-done.2
  1.0 0.0 copy-start.7
  1.0 0.1 edge_rows.1
  1.1 0.0 copy-done.4
  1.1 0.1 copy-done.5
  1.2 0.1 copy-done.6
  1.2 0.6 %copy-done.7 = bf16[2,128,128]{2,1,0:T(8,128)(2,1)S(1)} copy-done((bf16[2,128,128]{2,1,0:T(8,128)(2,1)S(1)}, bf16[2,128,128]{2,1,0:T(8,128)(2,1)}, u32[]{:S(2)}) %copy-start.7) | copy-done | bytes 65560
  1.9 2.9 %conditional.1 = (bf16[8,16,128]{2,1,0:T(8,128)(2,1)S(1)}, f32[512,128]{1,0:T(8,128)S(1)}, f32[256,128]{1,0:T(8,128)S(1)}, f32[256,128]{1,0:T(8,128)S(1)}, bf16[...) conditional(s32[]{:T(128)} %convert_element_type.3, ...), branch_computations={%region_0.0_spmd, %region_1.0_spmd} | conditional | flops 4000000000 | bytes 1114192 | solution.py:457
  1.9 2.9 %first.1 = (bf16[8,16,128]{2,1,0:T(8,128)(2,1)S(1)}, f32[512,128]{1,0:T(8,128)S(1)}, f32[256,128]{1,0:T(8,128)S(1)}, f32[256,128]{1,0:T(8,128)S(1)}, bf16[512,12...) custom-call(bf16[64,16,128]{2,1,0:T(8,128)(2,1)S(1)} %get-tuple-elem, ...), custom_call_target="tpu_custom_call", output_to_operand_aliasing={{0}: (8, {})} | custom-call | flops 4000000000 | bytes 1048576 | tf_op jit(solution)/shard_map/cond/branch_1_fun/first/pallas_call | solution.py:423
  4.8 8.4 %collective-permute-start.1 = (bf16[8,16,128]{2,1,0:T(8,128)(2,1)S(1)}, bf16[8,16,128]{2,1,0:T(8,128)(2,1)S(1)}, u32[]{:S(2)}, u32[]{:S(2)}) collective-permute-start(bf16[8,16,128]{2,1,0:T(8,128)(2,1)S(1)} %get-tuple-element.87), channel_id=1, source_target_pairs={{0,496},{16,0},{32,16},{48,32},{64,48},{80,64},{96,80},{112,96},{1... | collective-permute-start | bytes 98312 | tf_op jit(solution)/shard_map/ppermute | solution.py:27
  13.2 1.9 %collective-permute-start = (bf16[8,16,128]{2,1,0:T(8,128)(2,1)S(1)}, bf16[8,16,128]{2,1,0:T(8,128)(2,1)S(1)}, u32[]{:S(2)}, u32[]{:S(2)}) collective-permute-start(bf16[8,16,128]{2,1,0:T(8,128)(2,1)S(1)} %get-tuple-element.86), channel_id=1, source_target_pairs={{0,16},{16,32},{32,48},{48,64},{64,80},{80,96},{96,112},{112,128},... | collective-permute-start | bytes 98312 | tf_op jit(solution)/shard_map/ppermute | solution.py:27
  15.1 0.0 collective-permute-done.1.down_ref
  15.1 5.4 %collective-permute-done.up_ref = bf16[8,16,128]{2,1,0:T(8,128)(2,1)S(1)} collective-permute-done((bf16[8,16,128]{2,1,0:T(8,128)(2,1)S(1)}, bf16[8,16,128]{2,1,0:T(8,128)(2,1)S(1)}, u32[]{:S(2)}, u32[]{:S(2)}) %collective-permute-start) | collective-permute-done | bytes 32800 | tf_op jit(solution)/shard_map/ppermute | solution.py:27
  20.5 1.5 %halo.1 = (bf16[64,128]{1,0:T(8,128)(2,1)S(1)}, bf16[288,128]{1,0:T(8,128)(2,1)S(1)}, bf16[288,128]{1,0:T(8,128)(2,1)S(1)}) custom-call(bf16[8,16,128]{2,1,0:T(8,128)(2,1)S(1)} %collective-permute-done.up_ref, bf16[8,16,128]{2,1,0:T(8,128)(2,1)S(1)} %collective-permute-done.1.down_ref, bf16[256,128]{1,0:T(8,128)(2,1)S(1)} %get-tuple-element.88.own_right_ref, ...), custom_call_target="tpu_custom_call" | custom-call | flops 1000000000 | bytes 1048576 | tf_op jit(solution)/shard_map/halo/pallas_call | solution.py:423
  22.0 4.7 %collective-permute-start.3 = (bf16[288,128]{1,0:T(8,128)(2,1)S(1)}, bf16[288,128]{1,0:T(8,128)(2,1)S(1)}, u32[]{:S(2)}, u32[]{:S(2)}) collective-permute-start(bf16[288,128]{1,0:T(8,128)(2,1)S(1)} %get-tuple-element.108.refs_0_), channel_id=1, source_target_pairs={{1,2},{3,4},{5,6},{7,8},{9,10},{11,12},{13,14},{15,0},{2,1},{4,3},... | collective-permute-start | bytes 221192 | tf_op jit(solution)/shard_map/ppermute | solution.py:33
  26.7 2.0 %middle_early.1 = (bf16[288,128]{1,0:T(8,128)(2,1)S(1)}, f32[512,128]{1,0:T(8,128)S(1)}, f32[64,512]{1,0:T(8,128)S(1)}, f32[64,512]{1,0:T(8,128)S(1)}, f32[64,51...) custom-call(f32[512,128]{1,0:T(8,128)S(1)} %get-tuple-element.84.ref, ...), custom_call_target="tpu_custom_call", output_to_operand_aliasing={{0}: (9, {})} | custom-call | flops 2000000000 | bytes 1048576 | tf_op jit(solution)/shard_map/middle_early/pallas_call | solution.py:423
  28.7 1.9 %collective-permute-start.2 = (bf16[288,128]{1,0:T(8,128)(2,1)S(1)}, bf16[288,128]{1,0:T(8,128)(2,1)S(1)}, u32[]{:S(2)}, u32[]{:S(2)}) collective-permute-start(bf16[288,128]{1,0:T(8,128)(2,1)S(1)} %get-tuple-element.95.refs_10_.refs_0_), channel_id=1, source_target_pairs={{0,1},{2,3},{4,5},{6,7},{8,9},{10,11},{12,13},{14,15},{1,0},{3,2},... | collective-permute-start | bytes 221192 | tf_op jit(solution)/shard_map/ppermute | solution.py:33
  30.7 0.0 collective-permute-done.3.refs_1_
  30.7 1.4 %odd_border.1.refs_11_ = f32[256,128]{1,0:T(8,128)S(1)} custom-call(f32[256,128]{1,0:T(8,128)S(1)} %get-tuple-element.82.fright_ref, f32[256,128]{1,0:T(8,128)S(1)} %get-tuple-element.83.fleft_ref, bf16[288,128]{1,0:T(8,128)(2,1)S(1)} %get-tuple-element.108.refs_0_, bf16[288,128]{1,0:T(8,128)(2,1)S(1)} %collective-permute-done.3.refs_1_, ...), custom_call_target="tpu_custom_call" | custom-call | flops 1000000000 | bytes 1048576 | tf_op jit(solution)/shard_map/odd_border/pallas_call | solution.py:423
  32.1 2.9 %collective-permute-done.2.refs_1_ = bf16[288,128]{1,0:T(8,128)(2,1)S(1)} collective-permute-done((bf16[288,128]{1,0:T(8,128)(2,1)S(1)}, bf16[288,128]{1,0:T(8,128)(2,1)S(1)}, u32[]{:S(2)}, u32[]{:S(2)}) %collective-permute-start.2) | collective-permute-done | bytes 73760 | tf_op jit(solution)/shard_map/ppermute | solution.py:33
  35.0 2.2 %even_border.1 = f32[64,16,128]{2,1,0:T(8,128)} custom-call(f32[256,128]{1,0:T(8,128)S(1)} %get-tuple-element.82.fright_ref, f32[256,128]{1,0:T(8,128)S(1)} %get-tuple-element.83.fleft_ref, bf16[288,128]{1,0:T(8,128)(2,1)S(1)} %get-tuple-element.95.refs_10_.refs_0_, bf16[288,128]{1,0:T(8,128)(2,1)S(1)} %collective-permute-done.2.refs_1_, ...), custom_call_target="tpu_custom_call" | custom-call | flops 1000000000 | bytes 1048576 | tf_op jit(solution)/shard_map/even_border/pallas_call | solution.py:423
  (4 shorter events, 0.1 us)
Async XLA Ops:
  0.0 0.9 %copy-start = (bf16[64,16,128]{2,1,0:T(8,128)(2,1)S(1)}, bf16[64,16,128]{2,1,0:T(8,128)(2,1)}, u32[]{:S(2)}) copy-start(bf16[64,16,128]{2,1,0:T(8,128)(2,1)} %refs_0_.2) | copy-start | bytes 786436
  0.0 1.0 %copy-start.3 = (f32[2,128]{1,0:T(2,128)S(1)}, f32[2,128]{1,0:T(2,128)}, u32[]{:S(2)}) copy-start(f32[2,128]{1,0:T(2,128)} %refs_9_.3) | copy-start | bytes 3076
  0.0 1.1 %copy-start.4 = (bf16[2,128,512]{2,1,0:T(8,128)(2,1)S(1)}, bf16[2,128,512]{2,1,0:T(8,128)(2,1)}, u32[]{:S(2)}) copy-start(bf16[2,128,512]{2,1,0:T(8,128)(2,1)} %refs_7_.9) | copy-start | bytes 786436
  0.0 1.1 %copy-start.5 = (bf16[2,512,128]{2,1,0:T(8,128)(2,1)S(1)}, bf16[2,512,128]{2,1,0:T(8,128)(2,1)}, u32[]{:S(2)}) copy-start(bf16[2,512,128]{2,1,0:T(8,128)(2,1)} %refs_8_.7) | copy-start | bytes 786436
  0.0 1.2 %copy-start.6 = (bf16[2,128,384]{2,1,0:T(8,128)(2,1)S(1)}, bf16[2,128,384]{2,1,0:T(8,128)(2,1)}, u32[]{:S(2)}) copy-start(bf16[2,128,384]{2,1,0:T(8,128)(2,1)} %refs_4_.5) | copy-start | bytes 589828
  0.0 0.9 %copy-start.1 = (f32[2,4,225]{2,1,0:T(4,128)S(1)}, f32[2,4,225]{2,1,0:T(4,128)}, u32[]{:S(2)}) copy-start(f32[2,4,225]{2,1,0:T(4,128)} %refs_3_.5) | copy-start | bytes 21604
  0.1 0.9 %copy-start.2 = (f32[2,128]{1,0:T(2,128)S(1)}, f32[2,128]{1,0:T(2,128)}, u32[]{:S(2)}) copy-start(f32[2,128]{1,0:T(2,128)} %ag_ref.3) | copy-start | bytes 3076
  1.0 0.9 %copy-start.7 = (bf16[2,128,128]{2,1,0:T(8,128)(2,1)S(1)}, bf16[2,128,128]{2,1,0:T(8,128)(2,1)}, u32[]{:S(2)}) copy-start(bf16[2,128,128]{2,1,0:T(8,128)(2,1)} %refs_6_.9) | copy-start | bytes 196612
  4.8 10.3 %collective-permute-start.1 = (bf16[8,16,128]{2,1,0:T(8,128)(2,1)S(1)}, bf16[8,16,128]{2,1,0:T(8,128)(2,1)S(1)}, u32[]{:S(2)}, u32[]{:S(2)}) collective-permute-start(bf16[8,16,128]{2,1,0:T(8,128)(2,1)S(1)} %get-tuple-element.87), channel_id=1, source_target_pairs={{0,496},{16,0},{32,16},{48,32},{64,48},{80,64},{96,80},{112,96},{1... | collective-permute-start | bytes 98312 | tf_op jit(solution)/shard_map/ppermute | solution.py:27
  13.2 7.3 %collective-permute-start = (bf16[8,16,128]{2,1,0:T(8,128)(2,1)S(1)}, bf16[8,16,128]{2,1,0:T(8,128)(2,1)S(1)}, u32[]{:S(2)}, u32[]{:S(2)}) collective-permute-start(bf16[8,16,128]{2,1,0:T(8,128)(2,1)S(1)} %get-tuple-element.86), channel_id=1, source_target_pairs={{0,16},{16,32},{32,48},{48,64},{64,80},{80,96},{96,112},{112,128},... | collective-permute-start | bytes 98312 | tf_op jit(solution)/shard_map/ppermute | solution.py:27
  22.0 8.7 %collective-permute-start.3 = (bf16[288,128]{1,0:T(8,128)(2,1)S(1)}, bf16[288,128]{1,0:T(8,128)(2,1)S(1)}, u32[]{:S(2)}, u32[]{:S(2)}) collective-permute-start(bf16[288,128]{1,0:T(8,128)(2,1)S(1)} %get-tuple-element.108.refs_0_), channel_id=1, source_target_pairs={{1,2},{3,4},{5,6},{7,8},{9,10},{11,12},{13,14},{15,0},{2,1},{4,3},... | collective-permute-start | bytes 221192 | tf_op jit(solution)/shard_map/ppermute | solution.py:33
  28.7 6.2 %collective-permute-start.2 = (bf16[288,128]{1,0:T(8,128)(2,1)S(1)}, bf16[288,128]{1,0:T(8,128)(2,1)S(1)}, u32[]{:S(2)}, u32[]{:S(2)}) collective-permute-start(bf16[288,128]{1,0:T(8,128)(2,1)S(1)} %get-tuple-element.95.refs_10_.refs_0_), channel_id=1, source_target_pairs={{0,1},{2,3},{4,5},{6,7},{8,9},{10,11},{12,13},{14,15},{1,0},{3,2},... | collective-permute-start | bytes 221192 | tf_op jit(solution)/shard_map/ppermute | solution.py:33

commit v15 on v14

--- a/solution.py
+++ b/solution.py
@@ -234,7 +234,7 @@
 def second_kernel(*refs):
     @pl.when(jnp.logical_not(goes_first()))
     def _():
-        own_block(*refs[0:8], *refs[17:])
+        own_block(*refs[0:8], *refs[18:])
 
 
 def halo_kernel(
@@ -457,7 +457,7 @@
     first, *state = lax.cond(goes_first(), run, skip, *weights, first)
     down = shift(first, "gy", -1)
     state = call(
-        second_kernel, "second", (*weights, *state), kept, (), 4 * 10**9, {8 + i: i for i in range(9)}
+        second_kernel, "second", (*weights, *state, up), kept, (), 4 * 10**9, {8 + i: i for i in range(9)}
     )
     fa, fright, fleft, na, right, left, bias, wqv, wk = state
     va, odd, even = call(

time: 37.4 us -> 32.8 us (0.88)
  waiting for transfers between devices: 8.28 us -> 4.44 us
  local copies, waits for them, and re-layouts: 1.67 us -> 0.92 us
    ppermute x2, waiting for transfers between devices: 5.37 us -> 1.53 us  [shift(): lax.ppermute(x, axis, [(i, (i + by) % length) for i in range(length)])]
    unnamed x16, local copies, waits for them, and re-layouts: 1.67 us -> 0.92 us
  transfers between devices with their start and end apart: 4 -> 4, of which waited for: 2 -> 2; matrix products, arithmetic and copies ran while one was open for 0% -> 0% of each run, Pallas kernels for 9% -> 19%
where the time goes in v15:
time: 32.8 us; the launch traced here: 32.6 us
  starting transfers between devices  16.9 us (52%)
  Pallas kernels  10.1 us (31%)
  waiting for transfers between devices  4.44 us (14%)
  local copies, waits for them, and re-layouts  0.92 us (3%)
    ppermute x2, starting transfers between devices, shift(): lax.ppermute(x, axis, [(i, (i + by) % length) for i in range(length)])  10.3 us
    pallas_call x9, Pallas kernels, call(): pl.pallas_call(kernel, out_shape=shapes, in_specs=vmem(len(operands)), ou...  10.1 us
    ppermute x2, starting transfers between devices, swap(): return lax.ppermute(x, axis, there + [(b, a) for a, b in there])  6.62 us
    ppermute x2, waiting for transfers between devices, swap(): return lax.ppermute(x, axis, there + [(b, a) for a, b in there])  2.91 us
    ppermute x2, waiting for transfers between devices, shift(): lax.ppermute(x, axis, [(i, (i + by) % length) for i in range(length)])  1.53 us
    unnamed x16, local copies, waits for them, and re-layouts  0.92 us
  transfers between devices with their start and end apart: 4, of which 2 were waited for; matrix products, arithmetic and copies ran while one was open for 0% of the time, Pallas kernels for 19%

profile of v15, /device:TPU:24, one launch (start us, length us, event | category | flops | bytes accessed | tf_op | source)
XLA Modules:
  0.0 32.6 jit_solution(7482516650593436010)
XLA Ops:
  0.0 0.0 copy-start
  0.0 0.0 copy-start.2
  0.0 0.0 copy-start.1
  0.0 0.0 copy-start.3
  0.0 0.0 copy-start.5
  0.0 0.0 copy-start.6
  0.0 0.0 copy-start.7
  0.1 0.9 %copy-done = bf16[64,16,128]{2,1,0:T(8,128)(2,1)S(1)} copy-done((bf16[64,16,128]{2,1,0:T(8,128)(2,1)S(1)}, bf16[64,16,128]{2,1,0:T(8,128)(2,1)}, u32[]{:S(2)}) %copy-start) | copy-done | bytes 262168
  1.0 0.0 copy-done.2
  1.0 0.0 copy-done.1
  1.0 0.0 copy-done.3
  1.0 0.0 copy-start.4
  1.0 0.1 edge_rows.1
  1.1 1.9 %collective-permute-start = (bf16[8,16,128]{2,1,0:T(8,128)(2,1)S(1)}, bf16[8,16,128]{2,1,0:T(8,128)(2,1)S(1)}, u32[]{:S(2)}, u32[]{:S(2)}) collective-permute-start(bf16[8,16,128]{2,1,0:T(8,128)(2,1)S(1)} %get-tuple-element.82), channel_id=1, source_target_pairs={{0,16},{16,32},{32,48},{48,64},{64,80},{80,96},{96,112},{112,128},... | collective-permute-start | bytes 98312 | tf_op jit(solution)/shard_map/ppermute | solution.py:27
  3.0 0.0 copy-done.5
  3.0 0.0 copy-done.6
  3.0 0.0 copy-done.7
  3.0 0.0 copy-done.4
  3.1 2.9 %conditional.1 = (bf16[8,16,128]{2,1,0:T(8,128)(2,1)S(1)}, f32[512,128]{1,0:T(8,128)S(1)}, f32[256,128]{1,0:T(8,128)S(1)}, f32[256,128]{1,0:T(8,128)S(1)}, bf16[...) conditional(s32[]{:T(128)} %convert_element_type.3, ...), branch_computations={%region_0.0_spmd, %region_1.0_spmd} | conditional | flops 4000000000 | bytes 1114192 | solution.py:457
  3.1 2.9 %first.1 = (bf16[8,16,128]{2,1,0:T(8,128)(2,1)S(1)}, f32[512,128]{1,0:T(8,128)S(1)}, f32[256,128]{1,0:T(8,128)S(1)}, f32[256,128]{1,0:T(8,128)S(1)}, bf16[512,12...) custom-call(bf16[64,16,128]{2,1,0:T(8,128)(2,1)S(1)} %get-tuple-elem, ...), custom_call_target="tpu_custom_call", output_to_operand_aliasing={{0}: (8, {})} | custom-call | flops 4000000000 | bytes 1048576 | tf_op jit(solution)/shard_map/cond/branch_1_fun/first/pallas_call | solution.py:423
  6.0 8.4 %collective-permute-start.1 = (bf16[8,16,128]{2,1,0:T(8,128)(2,1)S(1)}, bf16[8,16,128]{2,1,0:T(8,128)(2,1)S(1)}, u32[]{:S(2)}, u32[]{:S(2)}) collective-permute-start(bf16[8,16,128]{2,1,0:T(8,128)(2,1)S(1)} %get-tuple-element.87), channel_id=1, source_target_pairs={{0,496},{16,0},{32,16},{48,32},{64,48},{80,64},{96,80},{112,96},{1... | collective-permute-start | bytes 98312 | tf_op jit(solution)/shard_map/ppermute | solution.py:27
  14.4 0.0 collective-permute-done.refs_17_.up_ref
  14.5 1.5 %collective-permute-done.1.down_ref = bf16[8,16,128]{2,1,0:T(8,128)(2,1)S(1)} collective-permute-done((bf16[8,16,128]{2,1,0:T(8,128)(2,1)S(1)}, bf16[8,16,128]{2,1,0:T(8,128)(2,1)S(1)}, u32[]{:S(2)}, u32[]{:S(2)}) %collective-permute-start.1) | collective-permute-done | bytes 32800 | tf_op jit(solution)/shard_map/ppermute | solution.py:27
  16.0 1.5 %halo.1 = (bf16[64,128]{1,0:T(8,128)(2,1)S(1)}, bf16[288,128]{1,0:T(8,128)(2,1)S(1)}, bf16[288,128]{1,0:T(8,128)(2,1)S(1)}) custom-call(bf16[8,16,128]{2,1,0:T(8,128)(2,1)S(1)} %collective-permute-done.refs_17_.up_ref, bf16[8,16,128]{2,1,0:T(8,128)(2,1)S(1)} %collective-permute-done.1.down_ref, bf16[256,128]{1,0:T(8,128)(2,1)S(1)} %get-tuple-element.88.own_right_ref, ...), custom_call_target="tpu_custom_call" | custom-call | flops 1000000000 | bytes 1048576 | tf_op jit(solution)/shard_map/halo/pallas_call | solution.py:423
  17.5 4.7 %collective-permute-start.3 = (bf16[288,128]{1,0:T(8,128)(2,1)S(1)}, bf16[288,128]{1,0:T(8,128)(2,1)S(1)}, u32[]{:S(2)}, u32[]{:S(2)}) collective-permute-start(bf16[288,128]{1,0:T(8,128)(2,1)S(1)} %get-tuple-element.108.refs_0_), channel_id=1, source_target_pairs={{1,2},{3,4},{5,6},{7,8},{9,10},{11,12},{13,14},{15,0},{2,1},{4,3},... | collective-permute-start | bytes 221192 | tf_op jit(solution)/shard_map/ppermute | solution.py:33
  22.2 2.0 %middle_early.1 = (bf16[288,128]{1,0:T(8,128)(2,1)S(1)}, f32[512,128]{1,0:T(8,128)S(1)}, f32[64,512]{1,0:T(8,128)S(1)}, f32[64,512]{1,0:T(8,128)S(1)}, f32[64,51...) custom-call(f32[512,128]{1,0:T(8,128)S(1)} %get-tuple-element.85.ref, ...), custom_call_target="tpu_custom_call", output_to_operand_aliasing={{0}: (9, {})} | custom-call | flops 2000000000 | bytes 1048576 | tf_op jit(solution)/shard_map/middle_early/pallas_call | solution.py:423
  24.2 1.9 %collective-permute-start.2 = (bf16[288,128]{1,0:T(8,128)(2,1)S(1)}, bf16[288,128]{1,0:T(8,128)(2,1)S(1)}, u32[]{:S(2)}, u32[]{:S(2)}) collective-permute-start(bf16[288,128]{1,0:T(8,128)(2,1)S(1)} %get-tuple-element.95.refs_10_.refs_0_), channel_id=1, source_target_pairs={{0,1},{2,3},{4,5},{6,7},{8,9},{10,11},{12,13},{14,15},{1,0},{3,2},... | collective-permute-start | bytes 221192 | tf_op jit(solution)/shard_map/ppermute | solution.py:33
  26.1 0.0 collective-permute-done.3.refs_1_
  26.2 1.4 %odd_border.1.refs_11_ = f32[256,128]{1,0:T(8,128)S(1)} custom-call(f32[256,128]{1,0:T(8,128)S(1)} %get-tuple-element.83.fright_ref, f32[256,128]{1,0:T(8,128)S(1)} %get-tuple-element.84.fleft_ref, bf16[288,128]{1,0:T(8,128)(2,1)S(1)} %get-tuple-element.108.refs_0_, bf16[288,128]{1,0:T(8,128)(2,1)S(1)} %collective-permute-done.3.refs_1_, ...), custom_call_target="tpu_custom_call" | custom-call | flops 1000000000 | bytes 1048576 | tf_op jit(solution)/shard_map/odd_border/pallas_call | solution.py:423
  27.5 2.9 %collective-permute-done.2.refs_1_ = bf16[288,128]{1,0:T(8,128)(2,1)S(1)} collective-permute-done((bf16[288,128]{1,0:T(8,128)(2,1)S(1)}, bf16[288,128]{1,0:T(8,128)(2,1)S(1)}, u32[]{:S(2)}, u32[]{:S(2)}) %collective-permute-start.2) | collective-permute-done | bytes 73760 | tf_op jit(solution)/shard_map/ppermute | solution.py:33
  30.4 2.2 %even_border.1 = f32[64,16,128]{2,1,0:T(8,128)} custom-call(f32[256,128]{1,0:T(8,128)S(1)} %get-tuple-element.83.fright_ref, f32[256,128]{1,0:T(8,128)S(1)} %get-tuple-element.84.fleft_ref, bf16[288,128]{1,0:T(8,128)(2,1)S(1)} %get-tuple-element.95.refs_10_.refs_0_, bf16[288,128]{1,0:T(8,128)(2,1)S(1)} %collective-permute-done.2.refs_1_, ...), custom_call_target="tpu_custom_call" | custom-call | flops 1000000000 | bytes 1048576 | tf_op jit(solution)/shard_map/even_border/pallas_call | solution.py:423
  (4 shorter events, 0.1 us)
Async XLA Ops:
  0.0 0.9 %copy-start = (bf16[64,16,128]{2,1,0:T(8,128)(2,1)S(1)}, bf16[64,16,128]{2,1,0:T(8,128)(2,1)}, u32[]{:S(2)}) copy-start(bf16[64,16,128]{2,1,0:T(8,128)(2,1)} %refs_0_.2) | copy-start | bytes 786436
  0.0 1.0 %copy-start.2 = (f32[2,128]{1,0:T(2,128)S(1)}, f32[2,128]{1,0:T(2,128)}, u32[]{:S(2)}) copy-start(f32[2,128]{1,0:T(2,128)} %ag_ref.3) | copy-start | bytes 3076
  0.0 1.0 %copy-start.1 = (f32[2,4,225]{2,1,0:T(4,128)S(1)}, f32[2,4,225]{2,1,0:T(4,128)}, u32[]{:S(2)}) copy-start(f32[2,4,225]{2,1,0:T(4,128)} %refs_3_.5) | copy-start | bytes 21604
  0.0 0.9 %copy-start.3 = (f32[2,128]{1,0:T(2,128)S(1)}, f32[2,128]{1,0:T(2,128)}, u32[]{:S(2)}) copy-start(f32[2,128]{1,0:T(2,128)} %refs_9_.3) | copy-start | bytes 3076
  0.0 3.0 %copy-start.5 = (bf16[2,512,128]{2,1,0:T(8,128)(2,1)S(1)}, bf16[2,512,128]{2,1,0:T(8,128)(2,1)}, u32[]{:S(2)}) copy-start(bf16[2,512,128]{2,1,0:T(8,128)(2,1)} %refs_8_.7) | copy-start | bytes 786436
  0.0 3.0 %copy-start.6 = (bf16[2,128,384]{2,1,0:T(8,128)(2,1)S(1)}, bf16[2,128,384]{2,1,0:T(8,128)(2,1)}, u32[]{:S(2)}) copy-start(bf16[2,128,384]{2,1,0:T(8,128)(2,1)} %refs_4_.5) | copy-start | bytes 589828
  0.0 3.0 %copy-start.7 = (bf16[2,128,128]{2,1,0:T(8,128)(2,1)S(1)}, bf16[2,128,128]{2,1,0:T(8,128)(2,1)}, u32[]{:S(2)}) copy-start(bf16[2,128,128]{2,1,0:T(8,128)(2,1)} %refs_6_.9) | copy-start | bytes 196612
  1.0 2.1 %copy-start.4 = (bf16[2,128,512]{2,1,0:T(8,128)(2,1)S(1)}, bf16[2,128,512]{2,1,0:T(8,128)(2,1)}, u32[]{:S(2)}) copy-start(bf16[2,128,512]{2,1,0:T(8,128)(2,1)} %refs_7_.9) | copy-start | bytes 786436
  1.1 13.3 %collective-permute-start = (bf16[8,16,128]{2,1,0:T(8,128)(2,1)S(1)}, bf16[8,16,128]{2,1,0:T(8,128)(2,1)S(1)}, u32[]{:S(2)}, u32[]{:S(2)}) collective-permute-start(bf16[8,16,128]{2,1,0:T(8,128)(2,1)S(1)} %get-tuple-element.82), channel_id=1, source_target_pairs={{0,16},{16,32},{32,48},{48,64},{64,80},{80,96},{96,112},{112,128},... | collective-permute-start | bytes 98312 | tf_op jit(solution)/shard_map/ppermute | solution.py:27
  6.0 10.0 %collective-permute-start.1 = (bf16[8,16,128]{2,1,0:T(8,128)(2,1)S(1)}, bf16[8,16,128]{2,1,0:T(8,128)(2,1)S(1)}, u32[]{:S(2)}, u32[]{:S(2)}) collective-permute-start(bf16[8,16,128]{2,1,0:T(8,128)(2,1)S(1)} %get-tuple-element.87), channel_id=1, source_target_pairs={{0,496},{16,0},{32,16},{48,32},{64,48},{80,64},{96,80},{112,96},{1... | collective-permute-start | bytes 98312 | tf_op jit(solution)/shard_map/ppermute | solution.py:27
  17.5 8.6 %collective-permute-start.3 = (bf16[288,128]{1,0:T(8,128)(2,1)S(1)}, bf16[288,128]{1,0:T(8,128)(2,1)S(1)}, u32[]{:S(2)}, u32[]{:S(2)}) collective-permute-start(bf16[288,128]{1,0:T(8,128)(2,1)S(1)} %get-tuple-element.108.refs_0_), channel_id=1, source_target_pairs={{1,2},{3,4},{5,6},{7,8},{9,10},{11,12},{13,14},{15,0},{2,1},{4,3},... | collective-permute-start | bytes 221192 | tf_op jit(solution)/shard_map/ppermute | solution.py:33
  24.2 6.2 %collective-permute-start.2 = (bf16[288,128]{1,0:T(8,128)(2,1)S(1)}, bf16[288,128]{1,0:T(8,128)(2,1)S(1)}, u32[]{:S(2)}, u32[]{:S(2)}) collective-permute-start(bf16[288,128]{1,0:T(8,128)(2,1)S(1)} %get-tuple-element.95.refs_10_.refs_0_), channel_id=1, source_target_pairs={{0,1},{2,3},{4,5},{6,7},{8,9},{10,11},{12,13},{14,15},{1,0},{3,2},... | collective-permute-start | bytes 221192 | tf_op jit(solution)/shard_map/ppermute | solution.py:33

commit v16 on v15

--- a/solution.py
+++ b/solution.py
@@ -344,20 +344,20 @@
     out_ref[0:32, :] = out[n - 32 : n]
 
 
-def beside_far_border():
+def waits_in_even_swap():
     col, cols = lax.axis_index("gx"), lax.axis_size("gx")
     place = lax.rem(col, cols // 2)
-    return (place == 0) | (place == cols // 2 - 1)
+    return (place == 1) | (place == cols // 2 - 2)
 
 
 def middle_early_kernel(*refs):
-    @pl.when(jnp.logical_not(beside_far_border()))
+    @pl.when(waits_in_even_swap())
     def _():
         middle_kernel(*refs[0:9], *refs[11:])
 
 
 def middle_late_kernel(*refs):
-    @pl.when(beside_far_border())
+    @pl.when(jnp.logical_not(waits_in_even_swap()))
     def _():
         middle_kernel(*refs[0:9], *refs[16:])
 

time: 32.8 us -> 32.5 us (level)
  the two profiles are of different devices: /device:TPU:24 before, /device:TPU:2 now
where the time goes in v16:
time: 32.5 us; the launch traced here: 32.2 us
  starting transfers between devices  18.5 us (57%)
  Pallas kernels  10.1 us (31%)
  waiting for transfers between devices  2.51 us (8%)
  local copies, waits for them, and re-layouts  0.92 us (3%)
    pallas_call x9, Pallas kernels, call(): pl.pallas_call(kernel, out_shape=shapes, in_specs=vmem(len(operands)), ou...  10.1 us
    ppermute x2, starting transfers between devices, shift(): lax.ppermute(x, axis, [(i, (i + by) % length) for i in range(length)])  9.38 us
    ppermute x2, starting transfers between devices, swap(): return lax.ppermute(x, axis, there + [(b, a) for a, b in there])  9.15 us
    ppermute x2, waiting for transfers between devices, shift(): lax.ppermute(x, axis, [(i, (i + by) % length) for i in range(length)])  1.53 us
    ppermute x2, waiting for transfers between devices, swap(): return lax.ppermute(x, axis, there + [(b, a) for a, b in there])  0.98 us
    unnamed x16, local copies, waits for them, and re-layouts  0.92 us
  transfers between devices with their start and end apart: 4, of which 2 were waited for; matrix products, arithmetic and copies ran while one was open for 0% of the time, Pallas kernels for 19%

profile of v16, /device:TPU:2, one launch (start us, length us, event | category | flops | bytes accessed | tf_op | source)
XLA Modules:
  0.0 32.2 jit_solution(17238697544694020161)
XLA Ops:
  0.0 0.0 copy-start
  0.0 0.0 copy-start.2
  0.0 0.0 copy-start.1
  0.0 0.0 copy-start.3
  0.0 0.0 copy-start.5
  0.0 0.0 copy-start.6
  0.0 0.0 copy-start.7
  0.1 0.9 %copy-done = bf16[64,16,128]{2,1,0:T(8,128)(2,1)S(1)} copy-done((bf16[64,16,128]{2,1,0:T(8,128)(2,1)S(1)}, bf16[64,16,128]{2,1,0:T(8,128)(2,1)}, u32[]{:S(2)}) %copy-start) | copy-done | bytes 262168
  1.0 0.0 copy-done.2
  1.0 0.0 copy-done.1
  1.0 0.0 copy-done.3
  1.0 0.0 copy-start.4
  1.0 0.1 edge_rows.1
  1.1 1.9 %collective-permute-start = (bf16[8,16,128]{2,1,0:T(8,128)(2,1)S(1)}, bf16[8,16,128]{2,1,0:T(8,128)(2,1)S(1)}, u32[]{:S(2)}, u32[]{:S(2)}) collective-permute-start(bf16[8,16,128]{2,1,0:T(8,128)(2,1)S(1)} %get-tuple-element.82), channel_id=1, source_target_pairs={{0,16},{16,32},{32,48},{48,64},{64,80},{80,96},{96,112},{112,128},... | collective-permute-start | bytes 98312 | tf_op jit(solution)/shard_map/ppermute | solution.py:27
  3.0 0.0 copy-done.5
  3.0 0.0 copy-done.6
  3.0 0.0 copy-done.7
  3.0 0.0 copy-done.4
  3.1 2.9 %conditional.1 = (bf16[8,16,128]{2,1,0:T(8,128)(2,1)S(1)}, f32[512,128]{1,0:T(8,128)S(1)}, f32[256,128]{1,0:T(8,128)S(1)}, f32[256,128]{1,0:T(8,128)S(1)}, bf16[...) conditional(s32[]{:T(128)} %convert_element_type.3, ...), branch_computations={%region_0.0_spmd, %region_1.0_spmd} | conditional | flops 4000000000 | bytes 1114192 | solution.py:457
  3.1 2.9 %first.1 = (bf16[8,16,128]{2,1,0:T(8,128)(2,1)S(1)}, f32[512,128]{1,0:T(8,128)S(1)}, f32[256,128]{1,0:T(8,128)S(1)}, f32[256,128]{1,0:T(8,128)S(1)}, bf16[512,12...) custom-call(bf16[64,16,128]{2,1,0:T(8,128)(2,1)S(1)} %get-tuple-elem, ...), custom_call_target="tpu_custom_call", output_to_operand_aliasing={{0}: (8, {})} | custom-call | flops 4000000000 | bytes 1048576 | tf_op jit(solution)/shard_map/cond/branch_1_fun/first/pallas_call | solution.py:423
  6.0 7.5 %collective-permute-start.1 = (bf16[8,16,128]{2,1,0:T(8,128)(2,1)S(1)}, bf16[8,16,128]{2,1,0:T(8,128)(2,1)S(1)}, u32[]{:S(2)}, u32[]{:S(2)}) collective-permute-start(bf16[8,16,128]{2,1,0:T(8,128)(2,1)S(1)} %get-tuple-element.87), channel_id=1, source_target_pairs={{0,496},{16,0},{32,16},{48,32},{64,48},{80,64},{96,80},{112,96},{1... | collective-permute-start | bytes 98312 | tf_op jit(solution)/shard_map/ppermute | solution.py:27
  13.5 0.0 collective-permute-done.refs_17_.up_ref
  13.5 1.5 %collective-permute-done.1.down_ref = bf16[8,16,128]{2,1,0:T(8,128)(2,1)S(1)} collective-permute-done((bf16[8,16,128]{2,1,0:T(8,128)(2,1)S(1)}, bf16[8,16,128]{2,1,0:T(8,128)(2,1)S(1)}, u32[]{:S(2)}, u32[]{:S(2)}) %collective-permute-start.1) | collective-permute-done | bytes 32800 | tf_op jit(solution)/shard_map/ppermute | solution.py:27
  15.0 1.5 %halo.1 = (bf16[64,128]{1,0:T(8,128)(2,1)S(1)}, bf16[288,128]{1,0:T(8,128)(2,1)S(1)}, bf16[288,128]{1,0:T(8,128)(2,1)S(1)}) custom-call(bf16[8,16,128]{2,1,0:T(8,128)(2,1)S(1)} %collective-permute-done.refs_17_.up_ref, bf16[8,16,128]{2,1,0:T(8,128)(2,1)S(1)} %collective-permute-done.1.down_ref, bf16[256,128]{1,0:T(8,128)(2,1)S(1)} %get-tuple-element.88.own_right_ref, ...), custom_call_target="tpu_custom_call" | custom-call | flops 1000000000 | bytes 1048576 | tf_op jit(solution)/shard_map/halo/pallas_call | solution.py:423
  16.6 7.2 %collective-permute-start.3 = (bf16[288,128]{1,0:T(8,128)(2,1)S(1)}, bf16[288,128]{1,0:T(8,128)(2,1)S(1)}, u32[]{:S(2)}, u32[]{:S(2)}) collective-permute-start(bf16[288,128]{1,0:T(8,128)(2,1)S(1)} %get-tuple-element.108.refs_0_), channel_id=1, source_target_pairs={{1,2},{3,4},{5,6},{7,8},{9,10},{11,12},{13,14},{15,0},{2,1},{4,3},... | collective-permute-start | bytes 221192 | tf_op jit(solution)/shard_map/ppermute | solution.py:33
  23.8 1.9 %collective-permute-start.2 = (bf16[288,128]{1,0:T(8,128)(2,1)S(1)}, bf16[288,128]{1,0:T(8,128)(2,1)S(1)}, u32[]{:S(2)}, u32[]{:S(2)}) collective-permute-start(bf16[288,128]{1,0:T(8,128)(2,1)S(1)} %get-tuple-element.95.refs_10_.refs_0_), channel_id=1, source_target_pairs={{0,1},{2,3},{4,5},{6,7},{8,9},{10,11},{12,13},{14,15},{1,0},{3,2},... | collective-permute-start | bytes 221192 | tf_op jit(solution)/shard_map/ppermute | solution.py:33
  25.8 2.0 %middle_late.1 = (f32[512,128]{1,0:T(8,128)S(1)}, f32[64,512]{1,0:T(8,128)S(1)}, f32[64,512]{1,0:T(8,128)S(1)}, f32[64,512]{1,0:T(8,128)S(1)}, f32[64,512]{1,0:T...) custom-call(f32[512,128]{1,0:T(8,128)S(1)} %get-tuple-element.85.ref, ...), custom_call_target="tpu_custom_call", output_to_operand_aliasing={{0}: (9, {}), {1}: (10, {}), {2}: (11, {}), {3}: (12, {}), ... | custom-call | flops 2000000000 | bytes 1048576 | tf_op jit(solution)/shard_map/middle_late/pallas_call | solution.py:423
  27.7 0.0 collective-permute-done.3.refs_1_
  27.7 1.4 %odd_border.1.refs_11_ = f32[256,128]{1,0:T(8,128)S(1)} custom-call(f32[256,128]{1,0:T(8,128)S(1)} %get-tuple-element.83.fright_ref, f32[256,128]{1,0:T(8,128)S(1)} %get-tuple-element.84.fleft_ref, bf16[288,128]{1,0:T(8,128)(2,1)S(1)} %get-tuple-element.108.refs_0_, bf16[288,128]{1,0:T(8,128)(2,1)S(1)} %collective-permute-done.3.refs_1_, ...), custom_call_target="tpu_custom_call" | custom-call | flops 1000000000 | bytes 1048576 | tf_op jit(solution)/shard_map/odd_border/pallas_call | solution.py:423
  29.1 1.0 %collective-permute-done.2.refs_1_ = bf16[288,128]{1,0:T(8,128)(2,1)S(1)} collective-permute-done((bf16[288,128]{1,0:T(8,128)(2,1)S(1)}, bf16[288,128]{1,0:T(8,128)(2,1)S(1)}, u32[]{:S(2)}, u32[]{:S(2)}) %collective-permute-start.2) | collective-permute-done | bytes 73760 | tf_op jit(solution)/shard_map/ppermute | solution.py:33
  30.1 2.2 %even_border.1 = f32[64,16,128]{2,1,0:T(8,128)} custom-call(f32[256,128]{1,0:T(8,128)S(1)} %get-tuple-element.83.fright_ref, f32[256,128]{1,0:T(8,128)S(1)} %get-tuple-element.84.fleft_ref, bf16[288,128]{1,0:T(8,128)(2,1)S(1)} %get-tuple-element.95.refs_10_.refs_0_, bf16[288,128]{1,0:T(8,128)(2,1)S(1)} %collective-permute-done.2.refs_1_, ...), custom_call_target="tpu_custom_call" | custom-call | flops 1000000000 | bytes 1048576 | tf_op jit(solution)/shard_map/even_border/pallas_call | solution.py:423
  (4 shorter events, 0.1 us)
Async XLA Ops:
  0.0 0.9 %copy-start = (bf16[64,16,128]{2,1,0:T(8,128)(2,1)S(1)}, bf16[64,16,128]{2,1,0:T(8,128)(2,1)}, u32[]{:S(2)}) copy-start(bf16[64,16,128]{2,1,0:T(8,128)(2,1)} %refs_0_.2) | copy-start | bytes 786436
  0.0 1.0 %copy-start.2 = (f32[2,128]{1,0:T(2,128)S(1)}, f32[2,128]{1,0:T(2,128)}, u32[]{:S(2)}) copy-start(f32[2,128]{1,0:T(2,128)} %ag_ref.3) | copy-start | bytes 3076
  0.0 1.0 %copy-start.1 = (f32[2,4,225]{2,1,0:T(4,128)S(1)}, f32[2,4,225]{2,1,0:T(4,128)}, u32[]{:S(2)}) copy-start(f32[2,4,225]{2,1,0:T(4,128)} %refs_3_.5) | copy-start | bytes 21604
  0.0 0.9 %copy-start.3 = (f32[2,128]{1,0:T(2,128)S(1)}, f32[2,128]{1,0:T(2,128)}, u32[]{:S(2)}) copy-start(f32[2,128]{1,0:T(2,128)} %refs_9_.3) | copy-start | bytes 3076
  0.0 3.0 %copy-start.5 = (bf16[2,512,128]{2,1,0:T(8,128)(2,1)S(1)}, bf16[2,512,128]{2,1,0:T(8,128)(2,1)}, u32[]{:S(2)}) copy-start(bf16[2,512,128]{2,1,0:T(8,128)(2,1)} %refs_8_.7) | copy-start | bytes 786436
  0.0 3.0 %copy-start.6 = (bf16[2,128,384]{2,1,0:T(8,128)(2,1)S(1)}, bf16[2,128,384]{2,1,0:T(8,128)(2,1)}, u32[]{:S(2)}) copy-start(bf16[2,128,384]{2,1,0:T(8,128)(2,1)} %refs_4_.5) | copy-start | bytes 589828
  0.0 3.0 %copy-start.7 = (bf16[2,128,128]{2,1,0:T(8,128)(2,1)S(1)}, bf16[2,128,128]{2,1,0:T(8,128)(2,1)}, u32[]{:S(2)}) copy-start(bf16[2,128,128]{2,1,0:T(8,128)(2,1)} %refs_6_.9) | copy-start | bytes 196612
  1.0 2.1 %copy-start.4 = (bf16[2,128,512]{2,1,0:T(8,128)(2,1)S(1)}, bf16[2,128,512]{2,1,0:T(8,128)(2,1)}, u32[]{:S(2)}) copy-start(bf16[2,128,512]{2,1,0:T(8,128)(2,1)} %refs_7_.9) | copy-start | bytes 786436
  1.1 12.4 %collective-permute-start = (bf16[8,16,128]{2,1,0:T(8,128)(2,1)S(1)}, bf16[8,16,128]{2,1,0:T(8,128)(2,1)S(1)}, u32[]{:S(2)}, u32[]{:S(2)}) collective-permute-start(bf16[8,16,128]{2,1,0:T(8,128)(2,1)S(1)} %get-tuple-element.82), channel_id=1, source_target_pairs={{0,16},{16,32},{32,48},{48,64},{64,80},{80,96},{96,112},{112,128},... | collective-permute-start | bytes 98312 | tf_op jit(solution)/shard_map/ppermute | solution.py:27
  6.0 9.0 %collective-permute-start.1 = (bf16[8,16,128]{2,1,0:T(8,128)(2,1)S(1)}, bf16[8,16,128]{2,1,0:T(8,128)(2,1)S(1)}, u32[]{:S(2)}, u32[]{:S(2)}) collective-permute-start(bf16[8,16,128]{2,1,0:T(8,128)(2,1)S(1)} %get-tuple-element.87), channel_id=1, source_target_pairs={{0,496},{16,0},{32,16},{48,32},{64,48},{80,64},{96,80},{112,96},{1... | collective-permute-start | bytes 98312 | tf_op jit(solution)/shard_map/ppermute | solution.py:27
  16.6 11.2 %collective-permute-start.3 = (bf16[288,128]{1,0:T(8,128)(2,1)S(1)}, bf16[288,128]{1,0:T(8,128)(2,1)S(1)}, u32[]{:S(2)}, u32[]{:S(2)}) collective-permute-start(bf16[288,128]{1,0:T(8,128)(2,1)S(1)} %get-tuple-element.108.refs_0_), channel_id=1, source_target_pairs={{1,2},{3,4},{5,6},{7,8},{9,10},{11,12},{13,14},{15,0},{2,1},{4,3},... | collective-permute-start | bytes 221192 | tf_op jit(solution)/shard_map/ppermute | solution.py:33
  23.8 6.2 %collective-permute-start.2 = (bf16[288,128]{1,0:T(8,128)(2,1)S(1)}, bf16[288,128]{1,0:T(8,128)(2,1)S(1)}, u32[]{:S(2)}, u32[]{:S(2)}) collective-permute-start(bf16[288,128]{1,0:T(8,128)(2,1)S(1)} %get-tuple-element.95.refs_10_.refs_0_), channel_id=1, source_target_pairs={{0,1},{2,3},{4,5},{6,7},{8,9},{10,11},{12,13},{14,15},{1,0},{3,2},... | collective-permute-start | bytes 221192 | tf_op jit(solution)/shard_map/ppermute | solution.py:33
